TPU v7x, 512 devices: a whole 4x8x8 slice. The times are simulated.
512 devices in a mesh: rep: 2 (over core), dp: 32 (over y, x), tensor: 8 (over z).
Axes of the slice: x: 4, y: 8, z: 8, core: 2. Of those that a mesh axis runs over, the one named last changes fastest.
Arguments:
- queries: bfloat16 [2, 4096, 4096], P('rep', 'dp', 'tensor'), may hold values from -100 to 100
- passages: bfloat16 [2, 4096, 4096], P('rep', 'dp', 'tensor'), may hold values from -100 to 100
- positives: int32 [2, 4096], P('rep', 'dp'), may hold values from 0 to 4095, each once within a row
- hidden_rows: bfloat16 [2, 4096, 14336], P('rep', 'dp', 'tensor'), may hold values from -6 to 6
- sketch: float32 [4096, 32], P('tensor'), may hold values from -6 to 6
Outputs:
- grad_queries: bfloat16 [2, 4096, 4096], P('rep', 'dp', 'tensor')
- grad_passages: bfloat16 [2, 4096, 4096], P('rep', 'dp', 'tensor')
- p_factor: float32 [14336, 32], P('tensor')
- q_factor: float32 [4096, 32], P('tensor')
All inputs are finite; a program needn't handle non-finite values.
Results may differ from a plain program's by a relative error of at most 0.025.
Values may be sent and summed in bfloat16 or wider, within the bound.
No kernel may reach another device: no remote copies, remote signals or barrier semaphores. Data moves between devices by JAX's collectives and lax.ppermute only.
A program may use at most 128 MiB of HBM per device.

v0:
```python
import math

import jax
import jax.numpy as jnp
from jax import lax
from jax.sharding import PartitionSpec as P

LEVELS = 7


SOFTMAX_TEMP = 4.0


def carried_in(part, axis, combine, identity):
    place = lax.axis_index(axis)
    gathered = lax.all_gather(part, axis)
    state = jnp.zeros_like(part) + jnp.asarray(identity, part.dtype)

    def one(hop, state):
        return combine(state, lax.dynamic_index_in_dim(gathered, hop, 0, False))

    return lax.fori_loop(0, place, one, state)


def carried_in_2(shard, axis, join, neutral):
    count = lax.axis_size(axis)
    place = lax.axis_index(axis)
    ahead = count - 1 - place
    gathered = lax.all_gather(
        shard.astype(jnp.bfloat16 if shard.dtype == jnp.float32 else shard.dtype), axis
    )
    state = jnp.zeros_like(shard) + jnp.asarray(neutral, shard.dtype)

    def one(hop, state):
        source = count - 1 - hop
        return join(state, lax.dynamic_index_in_dim(gathered, source, 0, False).astype(shard.dtype))

    return lax.fori_loop(0, ahead, one, state)


def add_terms(earlier, later):
    return earlier + later


def level_gradient(raw_sum, nesting_width, targets):
    nesting_scale = SOFTMAX_TEMP / math.sqrt(nesting_width)
    logits = nesting_scale * raw_sum
    shifted = logits - jnp.max(logits, axis=1, keepdims=True)
    exponent = jnp.exp(shifted)
    softmax_rows = exponent / jnp.sum(exponent, axis=1, keepdims=True)
    return nesting_scale * (softmax_rows - targets)


def body(queries, passages, positives, hidden_rows, sketch):
    query_rows = queries[0]
    own_passages = passages[0]
    row_count, feature_width = query_rows.shape
    tensor_shard_count = lax.axis_size("tensor")
    tensor_pos = lax.axis_index("tensor")
    full_width = feature_width * tensor_shard_count
    widths = [full_width >> level for level in range(LEVELS)]
    large_levels = [level for level in range(LEVELS) if widths[level] >= feature_width]
    small_levels = [level for level in range(LEVELS) if widths[level] < feature_width]
    group_rows = row_count * lax.axis_size("dp")
    first_shard = (tensor_pos == 0).astype(jnp.float32)
    everyone = lax.all_gather(own_passages, "dp", axis=0, tiled=True)
    nested = []
    running = None
    edge = 0
    for score_level in reversed(small_levels):
        score_upper = widths[score_level]
        added = jnp.dot(
            query_rows[:, edge:score_upper],
            everyone[:, edge:score_upper].T,
            preferred_element_type=jnp.float32,
        )
        running = added if running is None else running + added
        nested.append(running)
        edge = score_upper
    rest = jnp.dot(query_rows[:, edge:], everyone[:, edge:].T, preferred_element_type=jnp.float32)
    whole_part = running + rest
    scores = jnp.stack(nested[::-1] + [whole_part])
    targets = (jnp.arange(group_rows, dtype=jnp.int32)[None, :] == positives[0][:, None]).astype(
        jnp.float32
    )
    whole = scores[-1]
    before = carried_in(whole, "tensor", add_terms, jnp.zeros_like(whole))
    inclusive = before + whole
    total_large = jnp.zeros_like(whole)
    for level in large_levels:
        end_shard = widths[level] // feature_width - 1
        owner = (tensor_pos == end_shard).astype(jnp.float32)
        total_large = total_large + level_gradient(inclusive, widths[level], targets) * owner
    later = carried_in_2(total_large, "tensor", add_terms, jnp.zeros_like(whole))
    base = later + total_large
    small_grads = [
        level_gradient(scores[slot], widths[level], targets) * first_shard
        for slot, level in enumerate(small_levels)
    ]
    edges = [feature_width] + [widths[level] for level in small_levels] + [0]
    regions = []
    running_coef = base
    for slot in range(len(small_levels) + 1):
        if slot > 0:
            running_coef = running_coef + small_grads[slot - 1]
        regions.append((edges[slot + 1], edges[slot], running_coef.astype(jnp.bfloat16)))
    regions = regions[::-1]
    grad_parts = [
        jnp.dot(coef, everyone[:, lower_edge:upper], preferred_element_type=jnp.float32)
        for lower_edge, upper, coef in regions
    ]
    grad_rows = jnp.concatenate(grad_parts, axis=1)
    grad_queries = grad_rows.astype(jnp.bfloat16)
    parts = []
    for lower_edge, upper, coef in regions:
        parts.append(
            jnp.einsum(
                "rg,rx->gx",
                coef,
                query_rows[:, lower_edge:upper],
                preferred_element_type=jnp.float32,
            )
        )
    grad_passages = lax.psum_scatter(
        jnp.concatenate(parts, axis=1).astype(jnp.bfloat16), "dp", scatter_dimension=0, tiled=True
    )
    batch_rows = row_count * lax.axis_size("dp") * lax.axis_size("rep")
    cotangent = grad_queries.astype(jnp.float32)
    hidden_local = hidden_rows[0].astype(jnp.float32)
    sketch_part = jnp.dot(cotangent, sketch, precision=lax.Precision.HIGHEST)
    sketched = lax.psum(sketch_part, "tensor") / batch_rows
    p_local = jnp.dot(hidden_local.T, sketched, precision=lax.Precision.HIGHEST)
    p_sum = lax.psum(p_local, ("rep", "dp"))
    partial_gram_block = jnp.dot(p_sum.T, p_sum, precision=lax.Precision.HIGHEST)
    gram = lax.psum(partial_gram_block, "tensor")
    lower = jnp.linalg.cholesky(gram)
    p_factor = lax.linalg.triangular_solve(
        lower, p_sum, left_side=False, lower=True, transpose_a=True
    )
    projected = lax.psum(jnp.dot(hidden_local, p_factor, precision=lax.Precision.HIGHEST), "tensor")
    q_local = jnp.dot(cotangent.T, projected, precision=lax.Precision.HIGHEST) / batch_rows
    q_factor = lax.psum(q_local, ("rep", "dp"))
    return (grad_queries[None], grad_passages[None], p_factor, q_factor)


def solution(mesh):
    placed = (
        P("rep", "dp", "tensor"),
        P("rep", "dp", "tensor"),
        P("rep", "dp"),
        P("rep", "dp", "tensor"),
        P("tensor", None),
    )
    return jax.shard_map(
        body,
        mesh=mesh,
        in_specs=placed,
        out_specs=(
            P("rep", "dp", "tensor"),
            P("rep", "dp", "tensor"),
            P("tensor", None),
            P("tensor", None),
        ),
        check_vma=False,
    )
```

profile of v0, /device:TPU:57, one launch (start us, length us, event | category | flops | bytes accessed | tf_op | source)
XLA Modules:
  0.0 1054.7 jit_solution(13099730933661097502)
XLA Ops:
  8.0 90.5 %all-gather.7.cloned.1.call-done = bf16[1,4096,512]{2,1,0:T(8,128)(2,1)} async-done(((bf16[1,128,512]{2,1,0:T(8,128)(2,1)}), bf16[1,4096,512]{2,1,0:T(8,128)(2,1)}) %all-gather.7.cloned.1.call-update) | async-done | bytes 4194320 | tf_op jit(solution)/shard_map/all_gather | solution.py:66
  98.5 1.8 multiply_reduce_fusion
  100.3 2.7 multiply_reduce_fusion.1
  105.7 2.1 convolution_add_fusion
  107.9 177.6 %all-gather.9.cloned.1.call-done = f32[1024,4096]{1,0:T(8,128)} async-done(((f32[128,4096]{1,0:T(8,128)}), f32[1024,4096]{1,0:T(8,128)}) %all-gather.9.cloned.1.call-update) | async-done | bytes 16777232 | tf_op jit(solution)/shard_map/all_gather | solution.py:16
  285.8 2.3 multiply_reduce_fusion.6
  289.6 4.0 fusion.60
  295.2 2.4 fusion.22
  297.7 105.1 %all-gather.11.cloned.1.call-done = bf16[1024,4096]{1,0:T(8,128)(2,1)} async-done(((bf16[128,4096]{1,0:T(8,128)(2,1)}), bf16[1024,4096]{1,0:T(8,128)(2,1)}) %all-gather.11.cloned.1.call-update) | async-done | bytes 8388624 | tf_op jit(solution)/shard_map/all_gather | solution.py:29
  403.0 12.2 %while.23 = (s32[]{:T(128)}, f32[128,4096]{1,0:T(8,128)S(1)}, s32[]{:T(128)}, bf16[8,128,4096]{2,1,0:T(8,128)(2,1)}, s32[]{:T(128)}, /*index=5*/s32[]{:T(128)}, s32[]{:T(128)}, s32[]{:T(128)}) while((s32[]{:T(128)}, f32[128,4096]{1,0:T(8,128)S(1)}, s32[]{:T(128)}, bf16[8,128,4096]{2,1,0:T(8,128)(2,1)}, s32[]{:T(128)}, ...), condition=%wide.region_11.12_spmd, body=%wide.region_10.11_spmd.sunk | while | flops 1048582 | bytes 5243015 | solution.py:38
  403.0 1.7 convert_add_fusion.2
  404.7 1.7 convert_add_fusion.2
  408.2 1.7 convert_add_fusion.2
  415.2 4.9 fusion.13
  427.2 20.8 %psum.35 = f32[128,32]{1,0:T(8,128)S(1)} all-reduce(f32[128,32]{1,0:T(8,128)S(1)} %fusion.54), channel_id=1, replica_groups=mesh['rep'=2,'dp'=32,'tensor'=8] {'tensor'}, use_global_device_ids=true, to_apply=%region_19.20 | all-reduce | flops 4096 | bytes 32768 | tf_op jit(solution)/shard_map/psum | solution.py:131
  449.2 3.3 pad_maximum_fusion
  452.5 6.5 copy.28
  459.4 176.1 %all-reduce.3.cloned.1.call-done = f32[1792,32]{0,1:T(8,128)} async-done(((f32[1792,32]{0,1:T(8,128)}), f32[1792,32]{0,1:T(8,128)}) %all-reduce.3.cloned.1.call-update) | async-done | bytes 229392 | tf_op jit(solution)/shard_map/psum | solution.py:133
  636.8 23.6 %psum.37 = f32[32,32]{0,1:T(8,128)S(1)} all-reduce(f32[32,32]{0,1:T(8,128)S(1)} %fusion.62), channel_id=1, replica_groups=mesh['rep'=2,'dp'=32,'tensor'=8] {'tensor'}, use_global_device_ids=true, to_apply=%region_21.22 | all-reduce | flops 1024 | bytes 8192 | tf_op jit(solution)/shard_map/psum | solution.py:135
  660.5 2.9 cholesky.16
  664.8 2.4 custom-call.6
  669.1 21.3 %psum.38 = f32[128,32]{0,1:T(8,128)S(1)} all-reduce(f32[128,32]{0,1:T(8,128)S(1)} %convolution_bitcast_fusion.1), channel_id=1, replica_groups=mesh['rep'=2,'dp'=32,'tensor'=8] {'tensor'}, use_global_device_ids=true, to_apply=%region_24.25 | all-reduce | flops 4096 | bytes 32768 | tf_op jit(solution)/shard_map/psum | solution.py:140
  692.1 168.4 %reduce-scatter.4.cloned.1.call-done = bf16[128,512]{1,0:T(8,128)(2,1)} async-done(((bf16[4096,512]{1,0:T(8,128)(2,1)}), bf16[128,512]{1,0:T(8,128)(2,1)}) %reduce-scatter.4.cloned.1.call-update) | async-done | bytes 131088
  862.2 184.2 %all-reduce.5.cloned.1.call-done = f32[512,32]{0,1:T(8,128)} async-done(((f32[512,32]{0,1:T(8,128)}), f32[512,32]{0,1:T(8,128)}) %all-reduce.5.cloned.1.call-update) | async-done | bytes 65552 | tf_op jit(solution)/shard_map/psum | solution.py:142
  (75 shorter events, 32.0 us)
Async XLA Ops:
  7.2 440.9 %copy-start = (bf16[1,128,1792]{2,1,0:T(8,128)(2,1)S(1)}, bf16[1,128,1792]{2,1,0:T(8,128)(2,1)}, u32[]{:S(2)}) copy-start(bf16[1,128,1792]{2,1,0:T(8,128)(2,1)} %param.12) | copy-start | bytes 1376260
  7.2 93.1 %copy-start.9 = (bf16[1,128,512]{2,1,0:T(8,128)(2,1)S(1)}, bf16[1,128,512]{2,1,0:T(8,128)(2,1)}, u32[]{:S(2)}) copy-start(bf16[1,128,512]{2,1,0:T(8,128)(2,1)} %param.9) | copy-start | bytes 393220
  7.2 91.3 %all-gather.7.cloned.1.call-start = ((), (), s32[]{:S(2)}) async-start(), calls=%async_computation.3 | async-start | bytes 4325376 | tf_op jit(solution)/shard_map/all_gather | solution.py:66
  7.9 277.6 %all-gather.9.cloned.1.call-start = ((), (), s32[]{:S(2)}) async-start(), calls=%async_computation.4 | async-start | bytes 18874368 | tf_op jit(solution)/shard_map/all_gather | solution.py:16
  100.3 2.7 copy-start.3
  100.3 3.3 copy-start.6
  103.0 1.3 copy-start.5
  104.3 1.4 copy-start.1
  107.9 294.9 %all-gather.11.cloned.1.call-start = ((), (), s32[]{:S(2)}) async-start(), calls=%async_computation.5 | async-start | bytes 9437184 | tf_op jit(solution)/shard_map/all_gather | solution.py:29
  288.1 1.5 copy-start.10
  289.6 4.1 copy-start.2
  293.6 341.9 %all-reduce.3.cloned.1.call-start = ((), (), s32[]{:S(2)}) async-start(), calls=%async_computation.1 | async-start | bytes 458752 | tf_op jit(solution)/shard_map/psum | solution.py:133
  293.6 1.6 copy-start.4
  415.2 4.9 copy-start.7
  424.8 2.1 copy-start.11
  449.1 411.3 %reduce-scatter.4.cloned.1.call-start = ((), (), s32[]{:S(2)}) async-start(), calls=%async_computation.6 | async-start | bytes 4325376
  458.9 587.5 %all-reduce.5.cloned.1.call-start = ((), (), s32[]{:S(2)}) async-start(), calls=%async_computation.2 | async-start | bytes 131072 | tf_op jit(solution)/shard_map/psum | solution.py:142
  668.6 379.3 %copy-start.8 = (f32[1792,32]{0,1:T(8,128)}, f32[1792,32]{0,1:T(8,128)S(1)}, u32[]{:S(2)}) copy-start(f32[1792,32]{0,1:T(8,128)S(1)} %fusion.51) | copy-start | bytes 688132
Sparse Core Ops, SparseCore 0:
  11.2 87.2 all-gather.6
  108.0 177.5 all-gather.8
  293.7 109.0 all-gather.10
  449.3 186.1 all-reduce.2
  640.4 219.9 reduce-scatter.3
  864.3 182.0 all-reduce.4
where the time goes:
time: 1060 us; the launch traced here: 1050 us
  waiting for transfers between devices  903 us (85%)
  blocking collectives  65.7 us (6%)
  other arithmetic  38.1 us (4%)
  matrix products  18.9 us (2%)
  between operations  14.5 us (1%)
  local copies, waits for them, and re-layouts  14.2 us (1%)
    psum x1, waiting for transfers between devices, body(): q_factor = lax.psum(q_local, ('rep', 'dp'))  184 us
    all_gather x1, waiting for transfers between devices, carried_in(): gathered = lax.all_gather(part, axis)  178 us
    psum x1, waiting for transfers between devices, body(): p_sum = lax.psum(p_local, ('rep', 'dp'))  176 us
    unnamed x7, waiting for transfers between devices  169 us
    all_gather x1, waiting for transfers between devices, carried_in_2(): lax.all_gather(shard.astype(jnp.bfloat16 if shard.dtype == jnp.float32 el...  105 us
    all_gather x1, waiting for transfers between devices, body(): everyone = lax.all_gather(own_passages, 'dp', axis=0, tiled=True)  90.5 us
    psum x1, blocking collectives, body(): gram = lax.psum(partial_gram_block, 'tensor')  23.6 us
    psum x1, blocking collectives, body(): lax.psum(jnp.dot(hidden_local, p_factor, precision=lax.Precision.HIGHEST)...  21.3 us
  transfers between devices with their start and end apart: 6, of which 6 were waited for; matrix products, arithmetic and copies ran while one was open for 3% of the time, Pallas kernels for 0%

commit v1 on v0

v1 whole, which is shorter than its diff:
```python
import functools
import math

import jax
import jax.numpy as jnp
from jax import lax
from jax.experimental import pallas as pl
from jax.experimental.pallas import tpu as pltpu
from jax.sharding import Mesh, PartitionSpec as P

LEVELS = 7
SOFTMAX_TEMP = 4.0
NY = 8
NX = 4
NZ = 8
LANES = 128
f32 = jnp.float32
bf16 = jnp.bfloat16
HIGHEST = lax.Precision.HIGHEST
VMEM = pl.BlockSpec(memory_space=pltpu.VMEM)
ALL_ROWS = ("rep", "y", "xh", "xl")
NT = (((1,), (1,)), ((), ()))
TN = (((0,), (0,)), ((), ()))


def scale_of(level, full):
    return SOFTMAX_TEMP / math.sqrt(full >> level)


def swap(blocks, axes):
    return lax.all_to_all(blocks, axes, 0, 0, tiled=True)


def share(block, axes, count):
    return swap(jnp.broadcast_to(block[None], (count,) + block.shape), axes)


def scores_kernel(q_ref, p_ref, e_ref, stats_ref):
    chunks, rows, width = q_ref.shape
    full = chunks * width
    cols = p_ref.shape[1]
    lane = lax.broadcasted_iota(jnp.int32, (rows, LANES), 1)
    table = jnp.where(lane == 8 + LEVELS, 1.0, 0.0).astype(f32)

    def dot(q, p):
        return lax.dot_general(q, p, NT, preferred_element_type=f32)

    def finish(level, raw, table):
        logits = scale_of(level, full) * raw
        top = jnp.max(logits, axis=1, keepdims=True)
        e = jnp.exp(logits - top)
        e_ref[level] = e
        total = jnp.sum(e, axis=1, keepdims=True)
        table = jnp.where(lane == level, top, table)
        return jnp.where(lane == 8 + level, total, table)

    raw = None
    for level in reversed(range(LEVELS)):
        upper = full >> level
        lower = full >> (level + 1) if level + 1 < LEVELS else 0
        if upper < LANES:
            q = q_ref[0, :, :LANES]
            q = jnp.where(lane < upper, q, jnp.zeros_like(q))
            part = dot(q, p_ref[0, :, :LANES])
            table = finish(level, part, table)
            continue
        if upper == LANES:
            raw = dot(q_ref[0, :, :LANES], p_ref[0, :, :LANES])
        elif upper <= width:
            raw = raw + dot(q_ref[0, :, lower:upper], p_ref[0, :, lower:upper])
        else:
            parts = [dot(q_ref[c], p_ref[c]) for c in range(lower // width, upper // width)]
            while len(parts) > 1:
                parts = [a + b for a, b in zip(parts[::2], parts[1::2])]
            raw = raw + parts[0]
        table = finish(level, raw, table)
    stats_ref[...] = table.T[:16]


def grads_kernel(q_ref, p_ref, e_ref, stats_ref, all_ref, pos_ref, s_ref, gq_ref, gp_ref, sk_ref):
    chunks, rows, width = q_ref.shape
    full = chunks * width
    cols = p_ref.shape[1]
    top = all_ref[0, :8]
    for src in range(1, all_ref.shape[0]):
        top = jnp.maximum(top, all_ref[src, :8])
    total = all_ref[0, 8:] * jnp.exp(all_ref[0, :8] - top)
    for src in range(1, all_ref.shape[0]):
        total = total + all_ref[src, 8:] * jnp.exp(all_ref[src, :8] - top)
    factor = jnp.exp(stats_ref[:8] - top) / total
    place = jnp.broadcast_to(pos_ref[...].astype(f32), (8, rows))
    table = jnp.concatenate([factor, place, jnp.zeros((LANES - 16, rows), f32)], axis=0).T
    column = lax.broadcasted_iota(jnp.int32, (rows, cols), 1).astype(f32)
    target = (column == table[:, 8:9]).astype(f32)
    coef = jnp.zeros((rows, cols), f32)
    sketched = jnp.zeros(sk_ref.shape, f32)
    lane = lax.broadcasted_iota(jnp.int32, (1, LANES), 1)

    def put(chunk, low, high, gq, gp, sketched):
        gq_ref[chunk, :, low:high] = gq.astype(bf16)
        gp_ref[chunk, :, low:high] = gp.astype(bf16)
        return sketched + lax.dot_general(
            s_ref[chunk, :, low:high], gq, NT, precision=HIGHEST, preferred_element_type=f32
        )

    def both(c, chunk, low, high):
        gq = jnp.dot(c, p_ref[chunk, :, low:high], preferred_element_type=f32)
        gp = lax.dot_general(c, q_ref[chunk, :, low:high], TN, preferred_element_type=f32)
        return gq, gp

    held = None
    for level in range(LEVELS):
        scale = scale_of(level, full)
        grad = scale * (e_ref[level] * table[:, level:level + 1] - target)
        coef = coef + grad
        c = coef.astype(bf16)
        upper = full >> level
        lower = full >> (level + 1) if level + 1 < LEVELS else 0
        if upper > width:
            for chunk in range(lower // width, upper // width):
                gq, gp = both(c, chunk, 0, width)
                sketched = put(chunk, 0, width, gq, gp, sketched)
        elif lower >= LANES:
            gq, gp = both(c, 0, lower, upper)
            sketched = put(0, lower, upper, gq, gp, sketched)
        else:
            gq, gp = both(c, 0, 0, LANES)
            if held is None:
                held = (gq, gp)
            else:
                gq = jnp.where(lane < upper, gq, held[0])
                gp = jnp.where(lane < upper, gp, held[1])
                sketched = put(0, 0, LANES, gq, gp, sketched)
    sk_ref[...] = sketched


def exact_dot(wide, narrow, dims):
    hi = wide.astype(bf16)
    rest = wide - hi.astype(f32)
    mid = rest.astype(bf16)
    lo = (rest - mid.astype(f32)).astype(bf16)
    terms = [lax.dot_general(t, narrow, dims, preferred_element_type=f32) for t in (lo, mid, hi)]
    return terms[0] + terms[1] + terms[2]


def sum_all(value):
    rows = value.shape[0]
    count = 2 * NY * NX
    landed = swap(value.reshape(count, rows // count, LANES), ALL_ROWS)
    return share(jnp.sum(landed, axis=0), ALL_ROWS, count).reshape(rows, LANES)


def body(queries, passages, positives, hidden_rows, sketch):
    q = queries[0]
    p = passages[0]
    rows, width = q.shape
    full = width * NZ
    rank = sketch.shape[1]
    xh = lax.axis_index("xh")
    xl = lax.axis_index("xl")
    zi = lax.axis_index("z")
    flip = [(0, 1), (1, 0)]

    q_other = lax.ppermute(q, "xl", flip)
    pos_other = lax.ppermute(positives, "xl", flip)
    q_pair = jnp.concatenate(
        [jnp.where(xl == 0, q, q_other), jnp.where(xl == 0, q_other, q)], axis=0
    )
    pos_pair = jnp.concatenate(
        [jnp.where(xl == 0, positives, pos_other), jnp.where(xl == 0, pos_other, positives)], axis=1
    )
    q_tile = lax.all_gather(q_pair, "z")

    turn = [(a * NZ + b, b * NZ + a) for a in range(NY) for b in range(NZ)]
    turn_far = [
        ((a * 2 + h) * NZ + b, (b * 2 + 1 - h) * NZ + a)
        for a in range(NY) for h in range(2) for b in range(NZ)
    ]
    p_near = lax.ppermute(p, ("y", "z"), turn)
    p_far = lax.ppermute(p, ("y", "xh", "z"), turn_far)
    p_pair = jnp.concatenate([p_near, p_far], axis=0)
    p_tile = share(p_pair, "y", NY)

    s_all = lax.all_gather(sketch.T, "z")

    tile = 2 * rows
    e, stats = pl.pallas_call(
        scores_kernel,
        out_shape=(
            jax.ShapeDtypeStruct((LEVELS, tile, tile), f32),
            jax.ShapeDtypeStruct((16, tile), f32),
        ),
        in_specs=[VMEM, VMEM],
        out_specs=(VMEM, VMEM),
        compiler_params=pltpu.CompilerParams(vmem_limit_bytes=40 << 20),
        name="scores",
    )(q_tile, p_tile)
    stats_all = share(stats, ("xl", "z"), 2 * NZ)

    own_y = pos_pair // (rows * NX)
    own_x = pos_pair // rows % NX
    inside = (own_y == zi) & (own_x % 2 == xl)
    local = jnp.where(inside, pos_pair % rows + jnp.where(own_x // 2 == xh, 0, rows), -1)

    gq_part, gp_part, sk_part = pl.pallas_call(
        grads_kernel,
        out_shape=(
            jax.ShapeDtypeStruct((NZ, tile, width), bf16),
            jax.ShapeDtypeStruct((NY, tile, width), bf16),
            jax.ShapeDtypeStruct((rank, tile), f32),
        ),
        in_specs=[VMEM] * 7,
        out_specs=(VMEM, VMEM, VMEM),
        compiler_params=pltpu.CompilerParams(vmem_limit_bytes=56 << 20),
        name="grads",
    )(q_tile, p_tile, e, stats, stats_all, local, s_all)

    sk_blocks = jnp.stack([sk_part[:, :rows], sk_part[:, rows:]])
    sk_blocks = jnp.broadcast_to(sk_blocks[:, None], (2, NZ, rank, rows))
    sk_landed = swap(sk_blocks.reshape(2 * NZ, rank, rows), ("xl", "z"))
    batch = rows * NX * NY * 2
    sketched = jnp.sum(sk_landed, axis=0) / batch

    gq_part, gp_part, sketched = lax.optimization_barrier((gq_part, gp_part, sketched))

    gp_sum = lax.psum_scatter(gp_part, "y", scatter_dimension=0)
    gp_far = lax.ppermute(gp_sum[rows:], "xh", flip)
    gp_own = (gp_sum[:rows].astype(f32) + gp_far.astype(f32)).astype(bf16)
    grad_passages = lax.ppermute(gp_own, ("y", "z"), turn)

    gq_sum = jnp.sum(swap(gq_part, "z").astype(f32), axis=0)
    mine = jnp.where(xl == 0, gq_sum[:rows], gq_sum[rows:])
    other = jnp.where(xl == 0, gq_sum[rows:], gq_sum[:rows])
    grad_queries = (mine + lax.ppermute(other, "xl", flip)).astype(bf16)

    hidden = hidden_rows[0]
    units = hidden.shape[1]
    tiles = units // LANES
    padded = -(-tiles // 2) * 2 + (2 if tiles % 4 else 0)
    p_local = exact_dot(sketched, hidden, (((1,), (0,)), ((), ())))
    flat = p_local.reshape(rank, tiles, LANES).transpose(1, 0, 2).reshape(tiles * rank, LANES)
    pad = padded * rank - tiles * rank
    flat = jnp.concatenate([flat, jnp.zeros((pad, LANES), f32)], axis=0)
    p_flat = sum_all(flat)[:tiles * rank]
    p_sum = p_flat.reshape(tiles, rank, LANES).transpose(1, 0, 2).reshape(rank, units)
    gram_part = lax.dot_general(p_sum, p_sum, NT, precision=HIGHEST)
    proj_part = exact_dot(p_sum, hidden, NT)
    joined = jnp.concatenate(
        [proj_part, jnp.pad(gram_part, ((0, 0), (0, LANES - rank)))], axis=0
    )
    joined = jnp.sum(share(joined, "z", NZ), axis=0)
    proj = joined[:rank]
    gram = joined[rank:, :rank]

    q_local = exact_dot(proj, grad_queries, (((1,), (0,)), ((), ())))
    q_flat = q_local.reshape(rank, width // LANES, LANES).transpose(1, 0, 2).reshape(-1, LANES)
    q_sum = sum_all(q_flat).reshape(width // LANES, rank, LANES).transpose(1, 0, 2)
    q_sum = q_sum.reshape(rank, width)

    lower = jnp.linalg.cholesky(gram)
    inverse = lax.linalg.triangular_solve(
        lower, jnp.eye(rank, dtype=f32), left_side=True, lower=True
    )
    p_factor = lax.dot_general(p_sum, inverse, (((0,), (1,)), ((), ())), precision=HIGHEST)
    q_factor = lax.dot_general(q_sum, inverse, (((0,), (1,)), ((), ())), precision=HIGHEST) / batch
    return (grad_queries[None], grad_passages[None], p_factor, q_factor)


def solution(mesh):
    grid = Mesh(mesh.devices.reshape(2, NY, 2, 2, NZ), ("rep", "y", "xh", "xl", "z"))
    dp = ("y", "xh", "xl")
    placed = (
        P("rep", dp, "z"),
        P("rep", dp, "z"),
        P("rep", dp),
        P("rep", dp, "z"),
        P("z", None),
    )
    return jax.shard_map(
        body,
        mesh=grid,
        in_specs=placed,
        out_specs=(P("rep", dp, "z"), P("rep", dp, "z"), P("z", None), P("z", None)),
        check_vma=False,
    )
```

time: 1060 us -> 342 us (0.32)
  waiting for transfers between devices: 903 us -> 121 us
  starting transfers between devices: 0.24 us -> 65.5 us
  blocking collectives: 65.7 us -> 103 us
  other arithmetic: 38.1 us -> 10.6 us
  matrix products: 18.9 us -> 4.17 us
  Pallas kernels: 0 us -> 12.5 us
    psum x2 -> x0, waiting for transfers between devices: 360 us -> none  [the longest x1 184 us: body(): q_factor = lax.psum(q_local, ('rep', 'dp'))]
    all_gather x3 -> x1, waiting for transfers between devices: 373 us -> 17.2 us  [body(): q_tile = lax.all_gather(q_pair, 'z')]
    unnamed x7 -> x2, waiting for transfers between devices: 169 us -> 0.71 us
    all_to_all x0 -> x4, blocking collectives: none -> 78.2 us  [swap(): return lax.all_to_all(blocks, axes, 0, 0, tiled=True)]
    all_to_all x0 -> x5, waiting for transfers between devices: none -> 71.9 us  [swap(): return lax.all_to_all(blocks, axes, 0, 0, tiled=True)]
    psum x3 -> x0, blocking collectives: 65.7 us -> none  [the longest x1 23.6 us: body(): gram = lax.psum(partial_gram_block, 'tensor')]
    all_to_all x0 -> x5, starting transfers between devices: none -> 36.7 us  [swap(): return lax.all_to_all(blocks, axes, 0, 0, tiled=True)]
    ppermute x0 -> x7, waiting for transfers between devices: none -> 31 us  [the longest x1 16 us: body(): p_far = lax.ppermute(p, ('y', 'xh', 'z'), turn_far)]
  transfers between devices with their start and end apart: 6 -> 14, of which waited for: 6 -> 9; matrix products, arithmetic and copies ran while one was open for 3% -> 5% of each run, Pallas kernels for 0% -> 0%
where the time goes in v1:
time: 342 us; the launch traced here: 341 us
  waiting for transfers between devices  121 us (35%)
  blocking collectives  103 us (30%)
  starting transfers between devices  65.5 us (19%)
  between operations  14.4 us (4%)
  Pallas kernels  12.5 us (4%)
  other arithmetic  10.6 us (3%)
  local copies, waits for them, and re-layouts  10.5 us (3%)
  matrix products  4.17 us (1%)
    all_to_all x4, blocking collectives, swap(): return lax.all_to_all(blocks, axes, 0, 0, tiled=True)  78.2 us
    all_to_all x5, waiting for transfers between devices, swap(): return lax.all_to_all(blocks, axes, 0, 0, tiled=True)  71.9 us
    all_to_all x5, starting transfers between devices, swap(): return lax.all_to_all(blocks, axes, 0, 0, tiled=True)  36.7 us
    all_gather x1, blocking collectives, body(): s_all = lax.all_gather(sketch.T, 'z')  24.4 us
    all_gather x1, waiting for transfers between devices, body(): q_tile = lax.all_gather(q_pair, 'z')  17.2 us
    ppermute x1, waiting for transfers between devices, body(): p_far = lax.ppermute(p, ('y', 'xh', 'z'), turn_far)  16 us
    ppermute x1, starting transfers between devices, body(): p_far = lax.ppermute(p, ('y', 'xh', 'z'), turn_far)  12 us
    ppermute x1, waiting for transfers between devices, body(): grad_passages = lax.ppermute(gp_own, ('y', 'z'), turn)  11.7 us
  transfers between devices with their start and end apart: 14, of which 9 were waited for; matrix products, arithmetic and copies ran while one was open for 5% of the time, Pallas kernels for 0%

profile of v1, /device:TPU:57, one launch (start us, length us, event | category | flops | bytes accessed | tf_op | source)
XLA Modules:
  0.0 341.0 jit_solution(7498640525177991887)
XLA Ops:
  7.2 3.3 collective-permute-start
  10.5 12.0 %collective-permute-start.2 = (bf16[128,512]{1,0:T(8,128)(2,1)}, bf16[128,512]{1,0:T(8,128)(2,1)S(1)}, u32[]{:S(2)}, u32[]{:S(2)}) collective-permute-start(bf16[128,512]{1,0:T(8,128)(2,1)} %bitcast.107), channel_id=1, source_target_pairs={{0,16},{1,48},{2,80},{3,112},{4,144},{5,176},{6,208},{7,240},{16,0... | collective-permute-start | bytes 393224 | tf_op jit(solution)/shard_map/ppermute | solution.py:180
  26.2 16.0 %collective-permute-done.2 = bf16[128,512]{1,0:T(8,128)(2,1)S(1)} collective-permute-done((bf16[128,512]{1,0:T(8,128)(2,1)}, bf16[128,512]{1,0:T(8,128)(2,1)S(1)}, u32[]{:S(2)}, u32[]{:S(2)}) %collective-permute-start.2) | collective-permute-done | bytes 131104 | tf_op jit(solution)/shard_map/ppermute | solution.py:180
  42.1 2.7 collective-permute-done.1
  46.3 4.1 %all-to-all-start = ((bf16[8,256,512]{2,1,0:T(8,128)(2,1)}), bf16[8,256,512]{2,1,0:T(8,128)(2,1)S(1)}, u32[]{:S(2)}, u32[]{:S(2)}) async-start(bf16[8,256,512]{2,1,0:T(8,128)(2,1)} %broadcast_in_dim.23), calls=%async_computation | async-start | bytes 4194304 | tf_op jit(solution)/shard_map/all_to_all | solution.py:31
  52.3 17.2 %all-gather.4.cloned.1.call-done = bf16[2048,512]{1,0:T(8,128)(2,1)} async-done(((bf16[256,512]{1,0:T(8,128)(2,1)}), bf16[2048,512]{1,0:T(8,128)(2,1)}) %all-gather.4.cloned.1.call-update) | async-done | bytes 2097168 | tf_op jit(solution)/shard_map/all_gather | solution.py:172
  69.5 23.2 %all-to-all-done.p_ref = bf16[8,256,512]{2,1,0:T(8,128)(2,1)S(1)} async-done(((bf16[8,256,512]{2,1,0:T(8,128)(2,1)}), bf16[8,256,512]{2,1,0:T(8,128)(2,1)S(1)}, u32[]{:S(2)}, u32[]{:S(2)}) %all-to-all-start) | async-done | bytes 2097184 | tf_op jit(solution)/shard_map/all_to_all | solution.py:31
  98.2 9.1 %all-to-all-start.1 = ((f32[16,16,256]{2,1,0:T(8,128)}), f32[16,16,256]{2,1,0:T(8,128)S(1)}, u32[]{:S(2)}, u32[]{:S(2)}) async-start(f32[16,16,256]{2,1,0:T(8,128)} %broadcast_in_dim.24), calls=%async_computation.1 | async-start | bytes 524288 | tf_op jit(solution)/shard_map/all_to_all | solution.py:31
  107.3 24.4 %all-gather.1 = f32[256,512]{1,0:T(8,128)} all-gather(f32[32,512]{1,0:T(8,128)S(1)} %bitcast.106), channel_id=3, replica_groups=mesh['rep'=2,'y'=8,'xh'=2,'xl'=2,'z'=8] {'z'}, dimensions={0}, use_global_device_ids=true | all-gather | bytes 589824 | tf_op jit(solution)/shard_map/all_gather | solution.py:184
  132.9 11.4 %grads.1 = (bf16[8,256,512]{2,1,0:T(8,128)(2,1)}, bf16[8,256,512]{2,1,0:T(8,128)(2,1)}, f32[32,256]{1,0:T(8,128)}) custom-call(bf16[8,256,512]{2,1,0:T(8,128)(2,1)} %bitcast.93, bf16[8,256,512]{2,1,0:T(8,128)(2,1)} %copy-done.1, f32[7,256,256]{2,1,0:T(8,128)} %copy-done.3, f32[16,256]{1,0:T(8,128)} %copy-done.4, f32[16,16,256]{2,1,0:T(8,128)} %copy-done.6, ...), custom_call_target="tpu_custom_call" | custom-call | tf_op jit(solution)/shard_map/grads/pallas_call | solution.py:205
  145.1 13.5 %all_to_all.45 = f32[16,32,128]{2,1,0:T(8,128)S(1)} all-to-all(f32[16,32,128]{2,1,0:T(8,128)S(1)} %bitcast.100), channel_id=1, replica_groups=mesh['rep'=2,'y'=8,'xh'=2,'xl'=2,'z'=8] {'xl','z'}, dimensions={0} | all-to-all | bytes 524288 | tf_op jit(solution)/shard_map/all_to_all | solution.py:31
  159.4 31.0 %all_to_all.46 = f32[64,8,128]{2,1,0:T(8,128)S(1)} all-to-all(f32[64,8,128]{2,1,0:T(8,128)S(1)} %pad_bitcast_fusion), channel_id=1, replica_groups=mesh['rep'=2,'y'=8,'xh'=2,'xl'=2,'z'=8] {'rep','y','xh','xl'}, dimensions={0} | all-to-all | bytes 524288 | tf_op jit(solution)/shard_map/all_to_all | solution.py:31
  190.5 17.7 %all_to_all.47 = f32[64,8,128]{2,1,0:T(8,128)S(1)} all-to-all(f32[64,8,128]{2,1,0:T(8,128)S(1)} %broadcast_in_dim.28), channel_id=1, replica_groups=mesh['rep'=2,'y'=8,'xh'=2,'xl'=2,'z'=8] {'rep','y','xh','xl'}, dimensions={0} | all-to-all | bytes 524288 | tf_op jit(solution)/shard_map/all_to_all | solution.py:31
  209.5 16.0 %all_to_all.48 = f32[8,64,128]{2,1,0:T(8,128)S(1)} all-to-all(f32[8,64,128]{2,1,0:T(8,128)S(1)} %broadcast_in_dim.29), channel_id=1, replica_groups=mesh['rep'=2,'y'=8,'xh'=2,'xl'=2,'z'=8] {'z'}, dimensions={0} | all-to-all | bytes 524288 | tf_op jit(solution)/shard_map/all_to_all | solution.py:31
  225.5 3.6 %all-to-all-start.3 = ((bf16[8,256,512]{2,1,0:T(8,128)(2,1)}), bf16[8,256,512]{2,1,0:T(8,128)(2,1)S(1)}, u32[]{:S(2)}, u32[]{:S(2)}) async-start(bf16[8,256,512]{2,1,0:T(8,128)(2,1)} %get-tuple-element.17), calls=%async_computation.3 | async-start | bytes 4194304 | tf_op jit(solution)/shard_map/all_to_all | solution.py:31
  230.0 2.9 cholesky.17
  233.6 43.5 %all-to-all-done.3 = bf16[8,256,512]{2,1,0:T(8,128)(2,1)S(1)} async-done(((bf16[8,256,512]{2,1,0:T(8,128)(2,1)}), bf16[8,256,512]{2,1,0:T(8,128)(2,1)S(1)}, u32[]{:S(2)}, u32[]{:S(2)}) %all-to-all-start.3) | async-done | bytes 2097184 | tf_op jit(solution)/shard_map/all_to_all | solution.py:31
  277.5 3.1 collective-permute-start.4
  281.2 2.4 custom-call.6
  285.7 12.0 %all-to-all-start.7 = ((f32[64,2,128]{2,1,0:T(2,128)}), f32[64,2,128]{2,1,0:T(2,128)S(1)}, u32[]{:S(2)}, u32[]{:S(2)}) async-start(f32[64,2,128]{2,1,0:T(2,128)} %bitcast.24), calls=%async_computation.8 | async-start | bytes 131072 | tf_op jit(solution)/shard_map/all_to_all | solution.py:31
  298.7 4.6 %collective-permute-start.5 = (bf16[128,512]{1,0:T(8,128)(2,1)S(1)}, bf16[128,512]{1,0:T(8,128)(2,1)S(1)}, u32[]{:S(2)}, u32[]{:S(2)}) collective-permute-start(bf16[128,512]{1,0:T(8,128)(2,1)S(1)} %slice_bitcast_fusion), channel_id=1, source_target_pairs={{0,16},{16,0},{1,17},{17,1},{2,18},{18,2},{3,19},{19,3},{4,20},{20... | collective-permute-start | bytes 393224 | tf_op jit(solution)/shard_map/ppermute | solution.py:227
  305.8 7.9 %all-to-all-start.8 = ((f32[64,2,128]{2,1,0:T(2,128)}), f32[64,2,128]{2,1,0:T(2,128)S(1)}, u32[]{:S(2)}, u32[]{:S(2)}) async-start(f32[64,2,128]{2,1,0:T(2,128)} %broadcast_in_dim.30), calls=%async_computation.9 | async-start | bytes 131072 | tf_op jit(solution)/shard_map/all_to_all | solution.py:31
  316.6 4.5 %all-to-all-done.8 = f32[64,2,128]{2,1,0:T(2,128)S(1)} async-done(((f32[64,2,128]{2,1,0:T(2,128)}), f32[64,2,128]{2,1,0:T(2,128)S(1)}, u32[]{:S(2)}, u32[]{:S(2)}) %all-to-all-start.8) | async-done | bytes 65568 | tf_op jit(solution)/shard_map/all_to_all | solution.py:31
  321.9 11.7 %collective-permute-done.6 = bf16[128,512]{1,0:T(8,128)(2,1)S(1)} collective-permute-done((bf16[128,512]{1,0:T(8,128)(2,1)S(1)}, bf16[128,512]{1,0:T(8,128)(2,1)S(1)}, u32[]{:S(2)}, u32[]{:S(2)}) %collective-permute-start.6) | collective-permute-done | bytes 131104 | tf_op jit(solution)/shard_map/ppermute | solution.py:229
  (83 shorter events, 29.1 us)
Async XLA Ops:
  7.2 151.5 %copy-start = (bf16[1,128,1792]{2,1,0:T(8,128)(2,1)S(1)}, bf16[1,128,1792]{2,1,0:T(8,128)(2,1)}, u32[]{:S(2)}) copy-start(bf16[1,128,1792]{2,1,0:T(8,128)(2,1)} %param.8) | copy-start | bytes 1376260
  7.2 62.3 %all-gather.4.cloned.1.call-start = ((), (), s32[]{:S(2)}) async-start(), calls=%async_computation.11 | async-start | bytes 2359296 | tf_op jit(solution)/shard_map/all_gather | solution.py:172
  7.2 17.2 %collective-permute-start = (bf16[128,512]{1,0:T(8,128)(2,1)}, bf16[128,512]{1,0:T(8,128)(2,1)S(1)}, u32[]{:S(2)}, u32[]{:S(2)}) collective-permute-start(bf16[128,512]{1,0:T(8,128)(2,1)} %bitcast.104), channel_id=1, source_target_pairs={{0,8},{8,0},{1,9},{9,1},{2,10},{10,2},{3,11},{11,3},{4,12},{12,4},... | collective-permute-start | bytes 393224 | tf_op jit(solution)/shard_map/ppermute | solution.py:164
  10.5 31.6 %collective-permute-start.2 = (bf16[128,512]{1,0:T(8,128)(2,1)}, bf16[128,512]{1,0:T(8,128)(2,1)S(1)}, u32[]{:S(2)}, u32[]{:S(2)}) collective-permute-start(bf16[128,512]{1,0:T(8,128)(2,1)} %bitcast.107), channel_id=1, source_target_pairs={{0,16},{1,48},{2,80},{3,112},{4,144},{5,176},{6,208},{7,240},{16,0... | collective-permute-start | bytes 393224 | tf_op jit(solution)/shard_map/ppermute | solution.py:180
  22.5 22.3 %collective-permute-start.1 = (bf16[128,512]{1,0:T(8,128)(2,1)}, bf16[128,512]{1,0:T(8,128)(2,1)S(1)}, u32[]{:S(2)}, u32[]{:S(2)}) collective-permute-start(bf16[128,512]{1,0:T(8,128)(2,1)} %bitcast.108), channel_id=1, source_target_pairs={{0,0},{1,32},{2,64},{3,96},{4,128},{5,160},{6,192},{7,224},{32,1},... | collective-permute-start | bytes 393224 | tf_op jit(solution)/shard_map/ppermute | solution.py:179
  46.3 4.1 %copy-start.8 = (s32[1,128]{1,0:T(1,128)S(1)}, s32[1,128]{1,0:T(1,128)}, u32[]{:S(2)}) copy-start(s32[1,128]{1,0:T(1,128)} %param.7) | copy-start | bytes 1540
  46.3 46.4 %all-to-all-start = ((bf16[8,256,512]{2,1,0:T(8,128)(2,1)}), bf16[8,256,512]{2,1,0:T(8,128)(2,1)S(1)}, u32[]{:S(2)}, u32[]{:S(2)}) async-start(bf16[8,256,512]{2,1,0:T(8,128)(2,1)} %broadcast_in_dim.23), calls=%async_computation | async-start | bytes 4194304 | tf_op jit(solution)/shard_map/all_to_all | solution.py:31
  50.4 81.2 %collective-permute-start.3 = (s32[1,128]{1,0:T(1,128)S(1)}, s32[1,128]{1,0:T(1,128)S(1)}, u32[]{:S(2)}, u32[]{:S(2)}) collective-permute-start(s32[1,128]{1,0:T(1,128)S(1)} %copy-done.8), channel_id=1, source_target_pairs={{0,8},{8,0},{1,9},{9,1},{2,10},{10,2},{3,11},{11,3},{4,12},{12,4},... | collective-permute-start | bytes 1544 | tf_op jit(solution)/shard_map/ppermute | solution.py:165
  92.7 3.4 %copy-start.1 = (bf16[8,256,512]{2,1,0:T(8,128)(2,1)}, bf16[8,256,512]{2,1,0:T(8,128)(2,1)S(1)}, u32[]{:S(2)}) copy-start(bf16[8,256,512]{2,1,0:T(8,128)(2,1)S(1)} %all-to-all-done.p_ref) | copy-start | bytes 6291460
  92.7 2.3 copy-start.2
  95.0 12.2 %copy-start.7 = (f32[512,32]{0,1:T(8,128)S(1)}, f32[512,32]{0,1:T(8,128)}, u32[]{:S(2)}) copy-start(f32[512,32]{0,1:T(8,128)} %param.9) | copy-start | bytes 196612
  96.1 1.3 copy-start.3
  97.4 34.8 %copy-start.4 = (f32[16,256]{1,0:T(8,128)}, f32[16,256]{1,0:T(8,128)S(1)}, u32[]{:S(2)}) copy-start(f32[16,256]{1,0:T(8,128)S(1)} %get-tuple-element.13.stats_ref) | copy-start | bytes 49156
  98.2 34.1 %all-to-all-start.1 = ((f32[16,16,256]{2,1,0:T(8,128)}), f32[16,16,256]{2,1,0:T(8,128)S(1)}, u32[]{:S(2)}, u32[]{:S(2)}) async-start(f32[16,16,256]{2,1,0:T(8,128)} %broadcast_in_dim.24), calls=%async_computation.1 | async-start | bytes 524288 | tf_op jit(solution)/shard_map/all_to_all | solution.py:31
  132.2 0.7 copy-start.6
  225.5 51.6 %all-to-all-start.3 = ((bf16[8,256,512]{2,1,0:T(8,128)(2,1)}), bf16[8,256,512]{2,1,0:T(8,128)(2,1)S(1)}, u32[]{:S(2)}, u32[]{:S(2)}) async-start(bf16[8,256,512]{2,1,0:T(8,128)(2,1)} %get-tuple-element.17), calls=%async_computation.3 | async-start | bytes 4194304 | tf_op jit(solution)/shard_map/all_to_all | solution.py:31
  229.1 68.6 %reduce-scatter.2.cloned.1.call-start = ((), (), s32[]{:S(2)}) async-start(), calls=%async_computation.10 | async-start | bytes 2359296 | tf_op jit(solution)/shard_map/reduce_scatter | solution.py:226
  277.5 7.1 %collective-permute-start.4 = (f32[128,512]{1,0:T(8,128)S(1)}, f32[128,512]{1,0:T(8,128)S(1)}, u32[]{:S(2)}, u32[]{:S(2)}) collective-permute-start(f32[128,512]{1,0:T(8,128)S(1)} %slice_select_fusion), channel_id=1, source_target_pairs={{0,8},{8,0},{1,9},{9,1},{2,10},{10,2},{3,11},{11,3},{4,12},{12,4},... | collective-permute-start | bytes 786440 | tf_op jit(solution)/shard_map/ppermute | solution.py:234
  284.6 49.6 %copy-start.5 = (bf16[128,512]{1,0:T(8,128)(2,1)}, bf16[128,512]{1,0:T(8,128)(2,1)S(1)}, u32[]{:S(2)}) copy-start(bf16[128,512]{1,0:T(8,128)(2,1)S(1)} %add_convert_fusion) | copy-start | bytes 393220
  285.7 19.4 %all-to-all-start.7 = ((f32[64,2,128]{2,1,0:T(2,128)}), f32[64,2,128]{2,1,0:T(2,128)S(1)}, u32[]{:S(2)}, u32[]{:S(2)}) async-start(f32[64,2,128]{2,1,0:T(2,128)} %bitcast.24), calls=%async_computation.8 | async-start | bytes 131072 | tf_op jit(solution)/shard_map/all_to_all | solution.py:31
  298.7 15.0 %collective-permute-start.5 = (bf16[128,512]{1,0:T(8,128)(2,1)S(1)}, bf16[128,512]{1,0:T(8,128)(2,1)S(1)}, u32[]{:S(2)}, u32[]{:S(2)}) collective-permute-start(bf16[128,512]{1,0:T(8,128)(2,1)S(1)} %slice_bitcast_fusion), channel_id=1, source_target_pairs={{0,16},{16,0},{1,17},{17,1},{2,18},{18,2},{3,19},{19,3},{4,20},{20... | collective-permute-start | bytes 393224 | tf_op jit(solution)/shard_map/ppermute | solution.py:227
  305.8 15.2 %all-to-all-start.8 = ((f32[64,2,128]{2,1,0:T(2,128)}), f32[64,2,128]{2,1,0:T(2,128)S(1)}, u32[]{:S(2)}, u32[]{:S(2)}) async-start(f32[64,2,128]{2,1,0:T(2,128)} %broadcast_in_dim.30), calls=%async_computation.9 | async-start | bytes 131072 | tf_op jit(solution)/shard_map/all_to_all | solution.py:31
  314.7 18.9 %collective-permute-start.6 = (bf16[128,512]{1,0:T(8,128)(2,1)S(1)}, bf16[128,512]{1,0:T(8,128)(2,1)S(1)}, u32[]{:S(2)}, u32[]{:S(2)}) collective-permute-start(bf16[128,512]{1,0:T(8,128)(2,1)S(1)} %fusion.10), channel_id=1, source_target_pairs={{0,0},{1,32},{2,64},{3,96},{4,128},{5,160},{6,192},{7,224},{32,1},... | collective-permute-start | bytes 393224 | tf_op jit(solution)/shard_map/ppermute | solution.py:229
Sparse Core Ops, SparseCore 0:
  26.3 43.1 all-gather.3
  232.8 36.0 reduce-scatter.1

commit v2 on v1

--- a/solution.py
+++ b/solution.py
@@ -1,4 +1,3 @@
-import functools
 import math
 
 import jax
@@ -35,12 +34,18 @@
     return swap(jnp.broadcast_to(block[None], (count,) + block.shape), axes)
 
 
-def scores_kernel(q_ref, p_ref, e_ref, stats_ref):
+def scores_kernel(q_ref, raw_p_ref, e_ref, stats_ref, p_ref):
     chunks, rows, width = q_ref.shape
     full = chunks * width
-    cols = p_ref.shape[1]
+    piece = raw_p_ref.shape[2]
     lane = lax.broadcasted_iota(jnp.int32, (rows, LANES), 1)
     table = jnp.where(lane == 8 + LEVELS, 1.0, 0.0).astype(f32)
+
+    for y in range(raw_p_ref.shape[0]):
+        for half in range(2):
+            place = (2 * y + half) * piece
+            for chunk in range(chunks):
+                p_ref[chunk, place:place + piece] = raw_p_ref[y, half * chunks + chunk]
 
     def dot(q, p):
         return lax.dot_general(q, p, NT, preferred_element_type=f32)
@@ -61,8 +66,7 @@
         if upper < LANES:
             q = q_ref[0, :, :LANES]
             q = jnp.where(lane < upper, q, jnp.zeros_like(q))
-            part = dot(q, p_ref[0, :, :LANES])
-            table = finish(level, part, table)
+            table = finish(level, dot(q, p_ref[0, :, :LANES]), table)
             continue
         if upper == LANES:
             raw = dot(q_ref[0, :, :LANES], p_ref[0, :, :LANES])
@@ -77,10 +81,21 @@
     stats_ref[...] = table.T[:16]
 
 
-def grads_kernel(q_ref, p_ref, e_ref, stats_ref, all_ref, pos_ref, s_ref, gq_ref, gp_ref, sk_ref):
+def three_terms(value):
+    hi = value.astype(bf16)
+    rest = value - hi.astype(f32)
+    mid = rest.astype(bf16)
+    return hi, mid, (rest - mid.astype(f32)).astype(bf16)
+
+
+def grads_kernel(
+    at_ref, q_ref, p_ref, e_ref, stats_ref, all_ref, pos_ref, s_ref, gq_ref, gp_ref, sk_ref
+):
     chunks, rows, width = q_ref.shape
     full = chunks * width
     cols = p_ref.shape[1]
+    rank = s_ref.shape[1]
+    piece = gp_ref.shape[2]
     top = all_ref[0, :8]
     for src in range(1, all_ref.shape[0]):
         top = jnp.maximum(top, all_ref[src, :8])
@@ -93,15 +108,27 @@
     column = lax.broadcasted_iota(jnp.int32, (rows, cols), 1).astype(f32)
     target = (column == table[:, 8:9]).astype(f32)
     coef = jnp.zeros((rows, cols), f32)
-    sketched = jnp.zeros(sk_ref.shape, f32)
     lane = lax.broadcasted_iota(jnp.int32, (1, LANES), 1)
-
-    def put(chunk, low, high, gq, gp, sketched):
-        gq_ref[chunk, :, low:high] = gq.astype(bf16)
-        gp_ref[chunk, :, low:high] = gp.astype(bf16)
-        return sketched + lax.dot_general(
-            s_ref[chunk, :, low:high], gq, NT, precision=HIGHEST, preferred_element_type=f32
+    sk_ref[...] = jnp.zeros(sk_ref.shape, f32)
+
+    def put(chunk, low, high, gq, gp):
+        gq_hi = gq.astype(bf16)
+        gq_ref[chunk, :, low:high] = gq_hi
+        gp = gp.astype(bf16)
+        for part in range(rows // piece):
+            gp_ref[part // 2, part % 2 * chunks + chunk, :, low:high] = gp[
+                part * piece:(part + 1) * piece
+            ]
+        gq_lo = (gq - gq_hi.astype(f32)).astype(bf16)
+        terms = three_terms(s_ref[(at_ref[0] + chunks - chunk) % chunks, :, low:high])
+        big = lax.dot_general(
+            jnp.concatenate(terms, axis=0), gq_hi, NT, preferred_element_type=f32
         )
+        low_part = lax.dot_general(
+            jnp.concatenate(terms[:2], axis=0), gq_lo, NT, preferred_element_type=f32
+        )
+        small = big[2 * rank:] + low_part[rank:]
+        sk_ref[...] += small + (big[rank:2 * rank] + low_part[:rank]) + big[:rank]
 
     def both(c, chunk, low, high):
         gq = jnp.dot(c, p_ref[chunk, :, low:high], preferred_element_type=f32)
@@ -118,11 +145,9 @@
         lower = full >> (level + 1) if level + 1 < LEVELS else 0
         if upper > width:
             for chunk in range(lower // width, upper // width):
-                gq, gp = both(c, chunk, 0, width)
-                sketched = put(chunk, 0, width, gq, gp, sketched)
+                put(chunk, 0, width, *both(c, chunk, 0, width))
         elif lower >= LANES:
-            gq, gp = both(c, 0, lower, upper)
-            sketched = put(0, lower, upper, gq, gp, sketched)
+            put(0, lower, upper, *both(c, 0, lower, upper))
         else:
             gq, gp = both(c, 0, 0, LANES)
             if held is None:
@@ -130,17 +155,14 @@
             else:
                 gq = jnp.where(lane < upper, gq, held[0])
                 gp = jnp.where(lane < upper, gp, held[1])
-                sketched = put(0, 0, LANES, gq, gp, sketched)
-    sk_ref[...] = sketched
+                put(0, 0, LANES, gq, gp)
 
 
 def exact_dot(wide, narrow, dims):
-    hi = wide.astype(bf16)
-    rest = wide - hi.astype(f32)
-    mid = rest.astype(bf16)
-    lo = (rest - mid.astype(f32)).astype(bf16)
-    terms = [lax.dot_general(t, narrow, dims, preferred_element_type=f32) for t in (lo, mid, hi)]
-    return terms[0] + terms[1] + terms[2]
+    hi, mid, lo = [
+        lax.dot_general(t, narrow, dims, preferred_element_type=f32) for t in three_terms(wide)
+    ]
+    return (lo + mid) + hi
 
 
 def sum_all(value):
@@ -156,10 +178,14 @@
     rows, width = q.shape
     full = width * NZ
     rank = sketch.shape[1]
-    xh = lax.axis_index("xh")
     xl = lax.axis_index("xl")
     zi = lax.axis_index("z")
     flip = [(0, 1), (1, 0)]
+
+    piece = rows // NZ
+    p_cut = jnp.broadcast_to(p.reshape(1, NZ, piece, width), (2, NZ, piece, width))
+    p_cut = swap(p_cut.reshape(2 * NZ, piece, width), ("xh", "z"))
+    p_raw = lax.all_gather(p_cut, "y")
 
     q_other = lax.ppermute(q, "xl", flip)
     pos_other = lax.ppermute(positives, "xl", flip)
@@ -169,69 +195,67 @@
     pos_pair = jnp.concatenate(
         [jnp.where(xl == 0, positives, pos_other), jnp.where(xl == 0, pos_other, positives)], axis=1
     )
-    q_tile = lax.all_gather(q_pair, "z")
-
-    turn = [(a * NZ + b, b * NZ + a) for a in range(NY) for b in range(NZ)]
-    turn_far = [
-        ((a * 2 + h) * NZ + b, (b * 2 + 1 - h) * NZ + a)
-        for a in range(NY) for h in range(2) for b in range(NZ)
-    ]
-    p_near = lax.ppermute(p, ("y", "z"), turn)
-    p_far = lax.ppermute(p, ("y", "xh", "z"), turn_far)
-    p_pair = jnp.concatenate([p_near, p_far], axis=0)
-    p_tile = share(p_pair, "y", NY)
-
-    s_all = lax.all_gather(sketch.T, "z")
+    q_tile = share(q_pair, "z", NZ)
+
+    s_own, p_cut = lax.optimization_barrier((sketch.T, p_cut))
+    s_all = jnp.stack(
+        [s_own]
+        + [
+            lax.ppermute(s_own, "z", [(i, (i + k) % NZ) for i in range(NZ)])
+            for k in range(1, NZ)
+        ]
+    )
+    q_tile, p_raw, s_all = lax.optimization_barrier((q_tile, p_raw, s_all))
 
     tile = 2 * rows
-    e, stats = pl.pallas_call(
+    e, stats, p_tile = pl.pallas_call(
         scores_kernel,
         out_shape=(
             jax.ShapeDtypeStruct((LEVELS, tile, tile), f32),
             jax.ShapeDtypeStruct((16, tile), f32),
+            jax.ShapeDtypeStruct((NZ, tile, width), bf16),
         ),
         in_specs=[VMEM, VMEM],
-        out_specs=(VMEM, VMEM),
+        out_specs=(VMEM, VMEM, VMEM),
         compiler_params=pltpu.CompilerParams(vmem_limit_bytes=40 << 20),
         name="scores",
-    )(q_tile, p_tile)
+    )(q_tile, p_raw)
     stats_all = share(stats, ("xl", "z"), 2 * NZ)
 
     own_y = pos_pair // (rows * NX)
     own_x = pos_pair // rows % NX
-    inside = (own_y == zi) & (own_x % 2 == xl)
-    local = jnp.where(inside, pos_pair % rows + jnp.where(own_x // 2 == xh, 0, rows), -1)
+    inside = (own_x % 2 == xl) & (pos_pair % rows // piece == zi)
+    local = (own_y * 2 + own_x // 2) * piece + pos_pair % piece
+    local = jnp.where(inside, local, -1)
 
     gq_part, gp_part, sk_part = pl.pallas_call(
         grads_kernel,
         out_shape=(
             jax.ShapeDtypeStruct((NZ, tile, width), bf16),
-            jax.ShapeDtypeStruct((NY, tile, width), bf16),
+            jax.ShapeDtypeStruct((NY, 2 * NZ, piece, width), bf16),
             jax.ShapeDtypeStruct((rank, tile), f32),
         ),
-        in_specs=[VMEM] * 7,
+        in_specs=[pl.BlockSpec(memory_space=pltpu.SMEM)] + [VMEM] * 7,
         out_specs=(VMEM, VMEM, VMEM),
         compiler_params=pltpu.CompilerParams(vmem_limit_bytes=56 << 20),
         name="grads",
-    )(q_tile, p_tile, e, stats, stats_all, local, s_all)
+    )(zi.astype(jnp.int32).reshape(1), q_tile, p_tile, e, stats, stats_all, local, s_all)
+
+    gq_sum = lax.psum_scatter(gq_part, "z", scatter_dimension=0)
+    mine = jnp.where(xl == 0, gq_sum[:rows], gq_sum[rows:])
+    other = jnp.where(xl == 0, gq_sum[rows:], gq_sum[:rows])
+    other = lax.ppermute(other, "xl", flip)
+    grad_queries = (mine.astype(f32) + other.astype(f32)).astype(bf16)
+
+    gp_sum = lax.psum_scatter(gp_part, "y", scatter_dimension=0)
+    gp_home = swap(gp_sum, ("xh", "z")).reshape(2, rows, width).astype(f32)
+    grad_passages = (gp_home[0] + gp_home[1]).astype(bf16)
 
     sk_blocks = jnp.stack([sk_part[:, :rows], sk_part[:, rows:]])
     sk_blocks = jnp.broadcast_to(sk_blocks[:, None], (2, NZ, rank, rows))
     sk_landed = swap(sk_blocks.reshape(2 * NZ, rank, rows), ("xl", "z"))
     batch = rows * NX * NY * 2
     sketched = jnp.sum(sk_landed, axis=0) / batch
-
-    gq_part, gp_part, sketched = lax.optimization_barrier((gq_part, gp_part, sketched))
-
-    gp_sum = lax.psum_scatter(gp_part, "y", scatter_dimension=0)
-    gp_far = lax.ppermute(gp_sum[rows:], "xh", flip)
-    gp_own = (gp_sum[:rows].astype(f32) + gp_far.astype(f32)).astype(bf16)
-    grad_passages = lax.ppermute(gp_own, ("y", "z"), turn)
-
-    gq_sum = jnp.sum(swap(gq_part, "z").astype(f32), axis=0)
-    mine = jnp.where(xl == 0, gq_sum[:rows], gq_sum[rows:])
-    other = jnp.where(xl == 0, gq_sum[rows:], gq_sum[:rows])
-    grad_queries = (mine + lax.ppermute(other, "xl", flip)).astype(bf16)
 
     hidden = hidden_rows[0]
     units = hidden.shape[1]

time: 342 us -> 278 us (0.81)
  blocking collectives: 103 us -> 46.4 us
  waiting for transfers between devices: 121 us -> 74.9 us
  starting transfers between devices: 65.5 us -> 101 us
  Pallas kernels: 12.5 us -> 8.97 us
    all_to_all x5 -> x7, waiting for transfers between devices: 71.9 us -> 34.2 us  [swap(): return lax.all_to_all(blocks, axes, 0, 0, tiled=True)]
    all_to_all x4 -> x3, blocking collectives: 78.2 us -> 46.4 us  [swap(): return lax.all_to_all(blocks, axes, 0, 0, tiled=True)]
    all_gather x1 -> x0, blocking collectives: 24.4 us -> none  [body(): s_all = lax.all_gather(sketch.T, 'z')]
    all_to_all x5 -> x7, starting transfers between devices: 36.7 us -> 56.5 us  [swap(): return lax.all_to_all(blocks, axes, 0, 0, tiled=True)]
    all_gather x1, waiting for transfers between devices: 17.2 us -> 0.02 us  [body(): p_raw = lax.all_gather(p_cut, 'y')]
    ppermute x5 -> x8, starting transfers between devices: 23.6 us -> 38.6 us  [the longest x7 36 us: body(): lax.ppermute(s_own, 'z', [(i, (i + k) % NZ) for i in range(NZ)])]
    ppermute x1, waiting for transfers between devices: 0.01 us -> 5.86 us  [body(): q_other = lax.ppermute(q, 'xl', flip)]
    pallas_call x1, Pallas kernels: 11.4 us -> 7.81 us  [body(): pl.pallas_call(grads_kernel, out_shape=(jax.ShapeDtypeStruct((NZ, tile, w...]
  transfers between devices with their start and end apart: 14 -> 20, of which waited for: 9 -> 12; matrix products, arithmetic and copies ran while one was open for 5% -> 6% of each run, Pallas kernels for 0% -> 0%
where the time goes in v2:
time: 278 us; the launch traced here: 274 us
  starting transfers between devices  101 us (36%)
  waiting for transfers between devices  74.9 us (27%)
  blocking collectives  46.4 us (17%)
  between operations  14.2 us (5%)
  local copies, waits for them, and re-layouts  13 us (5%)
  other arithmetic  11.3 us (4%)
  Pallas kernels  8.97 us (3%)
  matrix products  4.16 us (1%)
    all_to_all x7, starting transfers between devices, swap(): return lax.all_to_all(blocks, axes, 0, 0, tiled=True)  56.5 us
    all_to_all x3, blocking collectives, swap(): return lax.all_to_all(blocks, axes, 0, 0, tiled=True)  46.4 us
    ppermute x7, starting transfers between devices, body(): lax.ppermute(s_own, 'z', [(i, (i + k) % NZ) for i in range(NZ)])  36 us
    all_to_all x7, waiting for transfers between devices, swap(): return lax.all_to_all(blocks, axes, 0, 0, tiled=True)  34.2 us
    ppermute x7, waiting for transfers between devices, body(): lax.ppermute(s_own, 'z', [(i, (i + k) % NZ) for i in range(NZ)])  31.4 us
    pallas_call x1, Pallas kernels, body(): pl.pallas_call(grads_kernel, out_shape=(jax.ShapeDtypeStruct((NZ, tile, w...  7.81 us
    unnamed x34, local copies, waits for them, and re-layouts  6.78 us
    ppermute x1, waiting for transfers between devices, body(): q_other = lax.ppermute(q, 'xl', flip)  5.86 us
  transfers between devices with their start and end apart: 20, of which 12 were waited for; matrix products, arithmetic and copies ran while one was open for 6% of the time, Pallas kernels for 0%

profile of v2, /device:TPU:57, one launch (start us, length us, event | category | flops | bytes accessed | tf_op | source)
XLA Modules:
  0.0 273.7 jit_solution(498903969688339155)
XLA Ops:
  8.9 12.6 %all-to-all-start.1 = ((bf16[16,16,512]{2,1,0:T(8,128)(2,1)}), bf16[16,16,512]{2,1,0:T(8,128)(2,1)S(1)}, u32[]{:S(2)}, u32[]{:S(2)}) async-start(bf16[16,16,512]{2,1,0:T(8,128)(2,1)} %bitcast.3), calls=%async_computation.1 | async-start | bytes 524288 | tf_op jit(solution)/shard_map/all_to_all | solution.py:30
  23.7 5.9 %collective-permute-done = bf16[128,512]{1,0:T(8,128)(2,1)S(1)} collective-permute-done((bf16[128,512]{1,0:T(8,128)(2,1)}, bf16[128,512]{1,0:T(8,128)(2,1)S(1)}, u32[]{:S(2)}, u32[]{:S(2)}) %collective-permute-start) | collective-permute-done | bytes 131104 | tf_op jit(solution)/shard_map/ppermute | solution.py:190
  33.2 4.8 %all-to-all-start = ((bf16[8,256,512]{2,1,0:T(8,128)(2,1)}), bf16[8,256,512]{2,1,0:T(8,128)(2,1)S(1)}, u32[]{:S(2)}, u32[]{:S(2)}) async-start(bf16[8,256,512]{2,1,0:T(8,128)(2,1)} %broadcast_in_dim.21), calls=%async_computation | async-start | bytes 4194304 | tf_op jit(solution)/shard_map/all_to_all | solution.py:30
  38.8 4.6 %collective-permute-start.7 = (f32[32,512]{1,0:T(8,128)S(1)}, f32[32,512]{1,0:T(8,128)S(1)}, u32[]{:S(2)}, u32[]{:S(2)}) collective-permute-start(f32[32,512]{1,0:T(8,128)S(1)} %bitcast.122), channel_id=1, source_target_pairs={{0,7},{1,0},{2,1},{3,2},{4,3},{5,4},{6,5},{7,6},{8,15},{9,8},{10,9... | collective-permute-start | bytes 196616 | tf_op jit(solution)/shard_map/ppermute | solution.py:204
  43.4 4.0 %collective-permute-start.6 = (f32[32,512]{1,0:T(8,128)S(1)}, f32[32,512]{1,0:T(8,128)S(1)}, u32[]{:S(2)}, u32[]{:S(2)}) collective-permute-start(f32[32,512]{1,0:T(8,128)S(1)} %bitcast.123), channel_id=1, source_target_pairs={{0,6},{1,7},{2,0},{3,1},{4,2},{5,3},{6,4},{7,5},{8,14},{9,15},{10,... | collective-permute-start | bytes 196616 | tf_op jit(solution)/shard_map/ppermute | solution.py:204
  50.5 5.2 %collective-permute-start.4 = (f32[32,512]{1,0:T(8,128)S(1)}, f32[32,512]{1,0:T(8,128)S(1)}, u32[]{:S(2)}, u32[]{:S(2)}) collective-permute-start(f32[32,512]{1,0:T(8,128)S(1)} %bitcast.125), channel_id=1, source_target_pairs={{0,4},{1,5},{2,6},{3,7},{4,0},{5,1},{6,2},{7,3},{8,12},{9,13},{10,... | collective-permute-start | bytes 196616 | tf_op jit(solution)/shard_map/ppermute | solution.py:204
  57.9 23.7 %collective-permute-done.1 = f32[32,512]{1,0:T(8,128)S(1)} collective-permute-done((f32[32,512]{1,0:T(8,128)S(1)}, f32[32,512]{1,0:T(8,128)S(1)}, u32[]{:S(2)}, u32[]{:S(2)}) %collective-permute-start.1) | collective-permute-done | bytes 65568 | tf_op jit(solution)/shard_map/ppermute | solution.py:204
  81.6 10.2 %collective-permute-start.2 = (f32[32,512]{1,0:T(8,128)S(1)}, f32[32,512]{1,0:T(8,128)S(1)}, u32[]{:S(2)}, u32[]{:S(2)}) collective-permute-start(f32[32,512]{1,0:T(8,128)S(1)} %bitcast.128), channel_id=1, source_target_pairs={{0,2},{1,3},{2,4},{3,5},{4,6},{5,7},{6,0},{7,1},{8,10},{9,11},{10,... | collective-permute-start | bytes 196616 | tf_op jit(solution)/shard_map/ppermute | solution.py:204
  93.8 6.8 %collective-permute-start.3 = (f32[32,512]{1,0:T(8,128)S(1)}, f32[32,512]{1,0:T(8,128)S(1)}, u32[]{:S(2)}, u32[]{:S(2)}) collective-permute-start(f32[32,512]{1,0:T(8,128)S(1)} %bitcast.129), channel_id=1, source_target_pairs={{0,3},{1,4},{2,5},{3,6},{4,7},{5,0},{6,1},{7,2},{8,11},{9,12},{10,... | collective-permute-start | bytes 196616 | tf_op jit(solution)/shard_map/ppermute | solution.py:204
  100.6 5.7 %collective-permute-done.3 = f32[32,512]{1,0:T(8,128)S(1)} collective-permute-done((f32[32,512]{1,0:T(8,128)S(1)}, f32[32,512]{1,0:T(8,128)S(1)}, u32[]{:S(2)}, u32[]{:S(2)}) %collective-permute-start.3) | collective-permute-done | bytes 65568 | tf_op jit(solution)/shard_map/ppermute | solution.py:204
  113.6 7.0 %all-to-all-start.2 = ((f32[16,16,256]{2,1,0:T(8,128)}), f32[16,16,256]{2,1,0:T(8,128)S(1)}, u32[]{:S(2)}, u32[]{:S(2)}) async-start(f32[16,16,256]{2,1,0:T(8,128)} %broadcast_in_dim.24), calls=%async_computation.2 | async-start | bytes 524288 | tf_op jit(solution)/shard_map/all_to_all | solution.py:30
  120.7 3.3 %collective-permute-start.8 = (s32[1,128]{1,0:T(1,128)S(1)}, s32[1,128]{1,0:T(1,128)S(1)}, u32[]{:S(2)}, u32[]{:S(2)}) collective-permute-start(s32[1,128]{1,0:T(1,128)S(1)} %copy-done.12), channel_id=1, source_target_pairs={{0,8},{8,0},{1,9},{9,1},{2,10},{10,2},{3,11},{11,3},{4,12},{12,4},... | collective-permute-start | bytes 1544 | tf_op jit(solution)/shard_map/ppermute | solution.py:191
  129.1 7.8 %grads.1 = (bf16[8,256,512]{2,1,0:T(8,128)(2,1)}, bf16[8,16,16,512]{3,2,1,0:T(8,128)(2,1)}, f32[32,256]{1,0:T(8,128)}) custom-call(s32[1]{0:T(128)} %bitcast.at_ref, bf16[8,256,512]{2,1,0:T(8,128)(2,1)} %copy-done.1, bf16[8,256,512]{2,1,0:T(8,128)(2,1)} %copy-done.3, f32[7,256,256]{2,1,0:T(8,128)} %copy-done.4, f32[16,256]{1,0:T(8,128)} %copy-done.5, ...), custom_call_target="tpu_custom_call" | custom-call | tf_op jit(solution)/shard_map/grads/pallas_call | solution.py:231
  137.7 13.0 %all_to_all.50 = f32[16,32,128]{2,1,0:T(8,128)S(1)} all-to-all(f32[16,32,128]{2,1,0:T(8,128)S(1)} %bitcast.114), channel_id=1, replica_groups=mesh['rep'=2,'y'=8,'xh'=2,'xl'=2,'z'=8] {'xl','z'}, dimensions={0} | all-to-all | bytes 524288 | tf_op jit(solution)/shard_map/all_to_all | solution.py:30
  152.2 14.4 %all-to-all-start.5 = ((f32[64,8,128]{2,1,0:T(8,128)}), f32[64,8,128]{2,1,0:T(8,128)S(1)}, u32[]{:S(2)}, u32[]{:S(2)}) async-start(f32[64,8,128]{2,1,0:T(8,128)} %pad_bitcast_fusion), calls=%async_computation.7 | async-start | bytes 524288 | tf_op jit(solution)/shard_map/all_to_all | solution.py:30
  167.3 10.2 %all-to-all-done.5 = f32[64,8,128]{2,1,0:T(8,128)S(1)} async-done(((f32[64,8,128]{2,1,0:T(8,128)}), f32[64,8,128]{2,1,0:T(8,128)S(1)}, u32[]{:S(2)}, u32[]{:S(2)}) %all-to-all-start.5) | async-done | bytes 262176 | tf_op jit(solution)/shard_map/all_to_all | solution.py:30
  177.6 17.7 %all_to_all.51 = f32[64,8,128]{2,1,0:T(8,128)S(1)} all-to-all(f32[64,8,128]{2,1,0:T(8,128)S(1)} %broadcast_in_dim.27), channel_id=1, replica_groups=mesh['rep'=2,'y'=8,'xh'=2,'xl'=2,'z'=8] {'rep','y','xh','xl'}, dimensions={0} | all-to-all | bytes 524288 | tf_op jit(solution)/shard_map/all_to_all | solution.py:30
  196.5 15.8 %all_to_all.52 = f32[8,64,128]{2,1,0:T(8,128)S(1)} all-to-all(f32[8,64,128]{2,1,0:T(8,128)S(1)} %broadcast_in_dim.28), channel_id=1, replica_groups=mesh['rep'=2,'y'=8,'xh'=2,'xl'=2,'z'=8] {'z'}, dimensions={0} | all-to-all | bytes 524288 | tf_op jit(solution)/shard_map/all_to_all | solution.py:30
  222.1 7.5 %all-to-all-start.8 = ((f32[64,2,128]{2,1,0:T(2,128)}), f32[64,2,128]{2,1,0:T(2,128)S(1)}, u32[]{:S(2)}, u32[]{:S(2)}) async-start(f32[64,2,128]{2,1,0:T(2,128)} %bitcast.34), calls=%async_computation.10 | async-start | bytes 131072 | tf_op jit(solution)/shard_map/all_to_all | solution.py:30
  230.3 6.7 %all-to-all-done.8 = f32[64,2,128]{2,1,0:T(2,128)S(1)} async-done(((f32[64,2,128]{2,1,0:T(2,128)}), f32[64,2,128]{2,1,0:T(2,128)S(1)}, u32[]{:S(2)}, u32[]{:S(2)}) %all-to-all-start.8) | async-done | bytes 65568 | tf_op jit(solution)/shard_map/all_to_all | solution.py:30
  237.7 6.7 %all-to-all-start.9 = ((f32[64,2,128]{2,1,0:T(2,128)}), f32[64,2,128]{2,1,0:T(2,128)S(1)}, u32[]{:S(2)}, u32[]{:S(2)}) async-start(f32[64,2,128]{2,1,0:T(2,128)} %broadcast_in_dim.29), calls=%async_computation.11 | async-start | bytes 131072 | tf_op jit(solution)/shard_map/all_to_all | solution.py:30
  247.5 4.3 %all-to-all-done.9 = f32[64,2,128]{2,1,0:T(2,128)S(1)} async-done(((f32[64,2,128]{2,1,0:T(2,128)}), f32[64,2,128]{2,1,0:T(2,128)S(1)}, u32[]{:S(2)}, u32[]{:S(2)}) %all-to-all-start.9) | async-done | bytes 65568 | tf_op jit(solution)/shard_map/all_to_all | solution.py:30
  251.7 3.5 %all-to-all-start.3 = ((bf16[16,16,512]{2,1,0:T(8,128)(2,1)}), bf16[16,16,512]{2,1,0:T(8,128)(2,1)S(1)}, u32[]{:S(2)}, u32[]{:S(2)}) async-start(bf16[16,16,512]{2,1,0:T(8,128)(2,1)} %bitcast.117), calls=%async_computation.5 | async-start | bytes 524288 | tf_op jit(solution)/shard_map/all_to_all | solution.py:30
  257.3 9.1 %all-to-all-done.3 = bf16[16,16,512]{2,1,0:T(8,128)(2,1)S(1)} async-done(((bf16[16,16,512]{2,1,0:T(8,128)(2,1)}), bf16[16,16,512]{2,1,0:T(8,128)(2,1)S(1)}, u32[]{:S(2)}, u32[]{:S(2)}) %all-to-all-start.3) | async-done | bytes 262176 | tf_op jit(solution)/shard_map/all_to_all | solution.py:30
  (107 shorter events, 49.3 us)
Async XLA Ops:
  7.2 143.5 %copy-start = (bf16[1,128,1792]{2,1,0:T(8,128)(2,1)S(1)}, bf16[1,128,1792]{2,1,0:T(8,128)(2,1)}, u32[]{:S(2)}) copy-start(bf16[1,128,1792]{2,1,0:T(8,128)(2,1)} %param.8) | copy-start | bytes 1376260
  8.9 22.8 %all-to-all-start.1 = ((bf16[16,16,512]{2,1,0:T(8,128)(2,1)}), bf16[16,16,512]{2,1,0:T(8,128)(2,1)S(1)}, u32[]{:S(2)}, u32[]{:S(2)}) async-start(bf16[16,16,512]{2,1,0:T(8,128)(2,1)} %bitcast.3), calls=%async_computation.1 | async-start | bytes 524288 | tf_op jit(solution)/shard_map/all_to_all | solution.py:30
  21.5 8.1 %collective-permute-start = (bf16[128,512]{1,0:T(8,128)(2,1)}, bf16[128,512]{1,0:T(8,128)(2,1)S(1)}, u32[]{:S(2)}, u32[]{:S(2)}) collective-permute-start(bf16[128,512]{1,0:T(8,128)(2,1)} %bitcast.120), channel_id=1, source_target_pairs={{0,8},{8,0},{1,9},{9,1},{2,10},{10,2},{3,11},{11,3},{4,12},{12,4},... | collective-permute-start | bytes 393224 | tf_op jit(solution)/shard_map/ppermute | solution.py:190
  33.2 73.2 %all-to-all-start = ((bf16[8,256,512]{2,1,0:T(8,128)(2,1)}), bf16[8,256,512]{2,1,0:T(8,128)(2,1)S(1)}, u32[]{:S(2)}, u32[]{:S(2)}) async-start(bf16[8,256,512]{2,1,0:T(8,128)(2,1)} %broadcast_in_dim.21), calls=%async_computation | async-start | bytes 4194304 | tf_op jit(solution)/shard_map/all_to_all | solution.py:30
  38.1 68.4 %all-gather.3.cloned.1.call-start = ((), (), s32[]{:S(2)}) async-start(), calls=%async_computation.14 | async-start | bytes 2359296 | tf_op jit(solution)/shard_map/all_gather | solution.py:188
  38.8 67.6 %collective-permute-start.7 = (f32[32,512]{1,0:T(8,128)S(1)}, f32[32,512]{1,0:T(8,128)S(1)}, u32[]{:S(2)}, u32[]{:S(2)}) collective-permute-start(f32[32,512]{1,0:T(8,128)S(1)} %bitcast.122), channel_id=1, source_target_pairs={{0,7},{1,0},{2,1},{3,2},{4,3},{5,4},{6,5},{7,6},{8,15},{9,8},{10,9... | collective-permute-start | bytes 196616 | tf_op jit(solution)/shard_map/ppermute | solution.py:204
  43.4 63.0 %collective-permute-start.6 = (f32[32,512]{1,0:T(8,128)S(1)}, f32[32,512]{1,0:T(8,128)S(1)}, u32[]{:S(2)}, u32[]{:S(2)}) collective-permute-start(f32[32,512]{1,0:T(8,128)S(1)} %bitcast.123), channel_id=1, source_target_pairs={{0,6},{1,7},{2,0},{3,1},{4,2},{5,3},{6,4},{7,5},{8,14},{9,15},{10,... | collective-permute-start | bytes 196616 | tf_op jit(solution)/shard_map/ppermute | solution.py:204
  47.4 59.0 %collective-permute-start.5 = (f32[32,512]{1,0:T(8,128)S(1)}, f32[32,512]{1,0:T(8,128)S(1)}, u32[]{:S(2)}, u32[]{:S(2)}) collective-permute-start(f32[32,512]{1,0:T(8,128)S(1)} %bitcast.124), channel_id=1, source_target_pairs={{0,5},{1,6},{2,7},{3,0},{4,1},{5,2},{6,3},{7,4},{8,13},{9,14},{10,... | collective-permute-start | bytes 196616 | tf_op jit(solution)/shard_map/ppermute | solution.py:204
  50.5 55.8 %collective-permute-start.4 = (f32[32,512]{1,0:T(8,128)S(1)}, f32[32,512]{1,0:T(8,128)S(1)}, u32[]{:S(2)}, u32[]{:S(2)}) collective-permute-start(f32[32,512]{1,0:T(8,128)S(1)} %bitcast.125), channel_id=1, source_target_pairs={{0,4},{1,5},{2,6},{3,7},{4,0},{5,1},{6,2},{7,3},{8,12},{9,13},{10,... | collective-permute-start | bytes 196616 | tf_op jit(solution)/shard_map/ppermute | solution.py:204
  55.7 25.9 %collective-permute-start.1 = (f32[32,512]{1,0:T(8,128)S(1)}, f32[32,512]{1,0:T(8,128)S(1)}, u32[]{:S(2)}, u32[]{:S(2)}) collective-permute-start(f32[32,512]{1,0:T(8,128)S(1)} %bitcast.126), channel_id=1, source_target_pairs={{0,1},{1,2},{2,3},{3,4},{4,5},{5,6},{6,7},{7,0},{8,9},{9,10},{10,1... | collective-permute-start | bytes 196616 | tf_op jit(solution)/shard_map/ppermute | solution.py:204
  81.6 12.2 %collective-permute-start.2 = (f32[32,512]{1,0:T(8,128)S(1)}, f32[32,512]{1,0:T(8,128)S(1)}, u32[]{:S(2)}, u32[]{:S(2)}) collective-permute-start(f32[32,512]{1,0:T(8,128)S(1)} %bitcast.128), channel_id=1, source_target_pairs={{0,2},{1,3},{2,4},{3,5},{4,6},{5,7},{6,0},{7,1},{8,10},{9,11},{10,... | collective-permute-start | bytes 196616 | tf_op jit(solution)/shard_map/ppermute | solution.py:204
  93.8 12.5 %collective-permute-start.3 = (f32[32,512]{1,0:T(8,128)S(1)}, f32[32,512]{1,0:T(8,128)S(1)}, u32[]{:S(2)}, u32[]{:S(2)}) collective-permute-start(f32[32,512]{1,0:T(8,128)S(1)} %bitcast.129), channel_id=1, source_target_pairs={{0,3},{1,4},{2,5},{3,6},{4,7},{5,0},{6,1},{7,2},{8,11},{9,12},{10,... | collective-permute-start | bytes 196616 | tf_op jit(solution)/shard_map/ppermute | solution.py:204
  109.0 11.7 %copy-start.12 = (s32[1,128]{1,0:T(1,128)S(1)}, s32[1,128]{1,0:T(1,128)}, u32[]{:S(2)}) copy-start(s32[1,128]{1,0:T(1,128)} %param.7) | copy-start | bytes 1540
  112.8 15.6 %copy-start.5 = (f32[16,256]{1,0:T(8,128)}, f32[16,256]{1,0:T(8,128)S(1)}, u32[]{:S(2)}) copy-start(f32[16,256]{1,0:T(8,128)S(1)} %get-tuple-element.19.stats_ref) | copy-start | bytes 49156
  113.6 14.8 %all-to-all-start.2 = ((f32[16,16,256]{2,1,0:T(8,128)}), f32[16,16,256]{2,1,0:T(8,128)S(1)}, u32[]{:S(2)}, u32[]{:S(2)}) async-start(f32[16,16,256]{2,1,0:T(8,128)} %broadcast_in_dim.24), calls=%async_computation.2 | async-start | bytes 524288 | tf_op jit(solution)/shard_map/all_to_all | solution.py:30
  120.6 91.8 %reduce-scatter.3.cloned.1.call-start = ((), (), s32[]{:S(2)}) async-start(), calls=%async_computation.12 | async-start | bytes 2359296 | tf_op jit(solution)/shard_map/reduce_scatter | solution.py:244
  120.7 4.3 %collective-permute-start.8 = (s32[1,128]{1,0:T(1,128)S(1)}, s32[1,128]{1,0:T(1,128)S(1)}, u32[]{:S(2)}, u32[]{:S(2)}) collective-permute-start(s32[1,128]{1,0:T(1,128)S(1)} %copy-done.12), channel_id=1, source_target_pairs={{0,8},{8,0},{1,9},{9,1},{2,10},{10,2},{3,11},{11,3},{4,12},{12,4},... | collective-permute-start | bytes 1544 | tf_op jit(solution)/shard_map/ppermute | solution.py:191
  152.2 25.3 %all-to-all-start.5 = ((f32[64,8,128]{2,1,0:T(8,128)}), f32[64,8,128]{2,1,0:T(8,128)S(1)}, u32[]{:S(2)}, u32[]{:S(2)}) async-start(f32[64,8,128]{2,1,0:T(8,128)} %pad_bitcast_fusion), calls=%async_computation.7 | async-start | bytes 524288 | tf_op jit(solution)/shard_map/all_to_all | solution.py:30
  166.6 80.9 %reduce-scatter.5.cloned.1.call-start = ((), (), s32[]{:S(2)}) async-start(), calls=%async_computation.13 | async-start | bytes 2359296 | tf_op jit(solution)/shard_map/reduce_scatter | solution.py:250
  213.4 6.6 %collective-permute-start.9 = (bf16[128,512]{1,0:T(8,128)(2,1)S(1)}, bf16[128,512]{1,0:T(8,128)(2,1)S(1)}, u32[]{:S(2)}, u32[]{:S(2)}) collective-permute-start(bf16[128,512]{1,0:T(8,128)(2,1)S(1)} %select_bitcast_fusion), channel_id=1, source_target_pairs={{0,8},{8,0},{1,9},{9,1},{2,10},{10,2},{3,11},{11,3},{4,12},{12,4},... | collective-permute-start | bytes 393224 | tf_op jit(solution)/shard_map/ppermute | solution.py:247
  221.0 46.1 %copy-start.6 = (bf16[128,512]{1,0:T(8,128)(2,1)}, bf16[128,512]{1,0:T(8,128)(2,1)S(1)}, u32[]{:S(2)}) copy-start(bf16[128,512]{1,0:T(8,128)(2,1)S(1)} %fusion.11) | copy-start | bytes 393220
  222.1 14.8 %all-to-all-start.8 = ((f32[64,2,128]{2,1,0:T(2,128)}), f32[64,2,128]{2,1,0:T(2,128)S(1)}, u32[]{:S(2)}, u32[]{:S(2)}) async-start(f32[64,2,128]{2,1,0:T(2,128)} %bitcast.34), calls=%async_computation.10 | async-start | bytes 131072 | tf_op jit(solution)/shard_map/all_to_all | solution.py:30
  237.7 14.0 %all-to-all-start.9 = ((f32[64,2,128]{2,1,0:T(2,128)}), f32[64,2,128]{2,1,0:T(2,128)S(1)}, u32[]{:S(2)}, u32[]{:S(2)}) async-start(f32[64,2,128]{2,1,0:T(2,128)} %broadcast_in_dim.29), calls=%async_computation.11 | async-start | bytes 131072 | tf_op jit(solution)/shard_map/all_to_all | solution.py:30
  251.7 14.7 %all-to-all-start.3 = ((bf16[16,16,512]{2,1,0:T(8,128)(2,1)}), bf16[16,16,512]{2,1,0:T(8,128)(2,1)S(1)}, u32[]{:S(2)}, u32[]{:S(2)}) async-start(bf16[16,16,512]{2,1,0:T(8,128)(2,1)} %bitcast.117), calls=%async_computation.5 | async-start | bytes 524288 | tf_op jit(solution)/shard_map/all_to_all | solution.py:30
  (9 other events, 21.2 us)
Sparse Core Ops, SparseCore 0:
  41.0 41.1 all-gather.2
  137.1 42.6 reduce-scatter.2
  182.6 41.3 reduce-scatter.4

commit v3 on v2

v3 whole, which is shorter than its diff:
```python
import math

import jax
import jax.numpy as jnp
from jax import lax
from jax.experimental import pallas as pl
from jax.experimental.pallas import tpu as pltpu
from jax.sharding import Mesh, PartitionSpec as P

LEVELS = 7
SOFTMAX_TEMP = 4.0
NY = 8
NX = 4
NZ = 8
LANES = 128
f32 = jnp.float32
bf16 = jnp.bfloat16
HIGHEST = lax.Precision.HIGHEST
VMEM = pl.BlockSpec(memory_space=pltpu.VMEM)
ANY = pl.BlockSpec(memory_space=pl.ANY)
ALL_ROWS = ("rep", "y", "xh", "xl")
NT = (((1,), (1,)), ((), ()))
TN = (((0,), (0,)), ((), ()))


def scale_of(level, full):
    return SOFTMAX_TEMP / math.sqrt(full >> level)


def swap(blocks, axes):
    return lax.all_to_all(blocks, axes, 0, 0, tiled=True)


def share(block, axes, count):
    return swap(jnp.broadcast_to(block[None], (count,) + block.shape), axes)


def query_rows(q_ref, chunk, low, high):
    return jnp.concatenate([q_ref[half, chunk, :, low:high] for half in range(2)], axis=0)


def level_scores(q_ref, raw_p_ref, p_ref, sems, finish):
    _, chunks, half_rows, width = q_ref.shape
    full = chunks * width
    piece = raw_p_ref.shape[2]
    lane = lax.broadcasted_iota(jnp.int32, (2 * half_rows, LANES), 1)
    moves = []
    for y in range(raw_p_ref.shape[0]):
        for half in range(2):
            moves.append(
                pltpu.make_async_copy(
                    raw_p_ref.at[y, pl.ds(half * chunks, chunks)],
                    p_ref.at[:, pl.ds((2 * y + half) * piece, piece)],
                    sems.at[2 * y + half],
                )
            )
    for move in moves:
        move.start()
    for move in moves:
        move.wait()

    def dot(chunk, low, high):
        return lax.dot_general(
            query_rows(q_ref, chunk, low, high), p_ref[chunk, :, low:high], NT,
            preferred_element_type=f32,
        )

    raw = None
    for level in reversed(range(LEVELS)):
        upper = full >> level
        lower = full >> (level + 1) if level + 1 < LEVELS else 0
        if upper < LANES:
            q = query_rows(q_ref, 0, 0, LANES)
            q = jnp.where(lane < upper, q, jnp.zeros_like(q))
            finish(
                level,
                lax.dot_general(q, p_ref[0, :, :LANES], NT, preferred_element_type=f32),
            )
            continue
        if upper == LANES:
            raw = dot(0, 0, LANES)
        elif upper <= width:
            raw = raw + dot(0, lower, upper)
        else:
            parts = [dot(c, 0, width) for c in range(lower // width, upper // width)]
            while len(parts) > 1:
                parts = [a + b for a, b in zip(parts[::2], parts[1::2])]
            raw = raw + parts[0]
        finish(level, raw)


def scores_kernel(q_ref, raw_p_ref, stats_ref, p_ref, table_ref, sems):
    full = q_ref.shape[1] * q_ref.shape[3]
    lane = lax.broadcasted_iota(jnp.int32, table_ref.shape, 1)
    table_ref[...] = jnp.zeros(table_ref.shape, f32)

    def finish(level, raw):
        logits = scale_of(level, full) * raw
        top = jnp.max(logits, axis=1, keepdims=True)
        total = jnp.sum(jnp.exp(logits - top), axis=1, keepdims=True)
        table_ref[...] = jnp.where(lane == level, top + jnp.log(total), table_ref[...])

    level_scores(q_ref, raw_p_ref, p_ref, sems, finish)
    stats_ref[...] = table_ref[...].T[:8]


def three_terms(value):
    hi = value.astype(bf16)
    rest = value - hi.astype(f32)
    mid = rest.astype(bf16)
    return hi, mid, (rest - mid.astype(f32)).astype(bf16)


def grads_kernel(
    at_ref, q_ref, raw_p_ref, all_ref, pos_ref, s_ref, gq_ref, gp_ref, sk_ref, p_ref, grad_ref, sems
):
    _, chunks, half_rows, width = q_ref.shape
    rows = 2 * half_rows
    full = chunks * width
    cols = p_ref.shape[1]
    rank = s_ref.shape[1]
    piece = gp_ref.shape[2]
    peak = all_ref[0]
    for src in range(1, all_ref.shape[0]):
        peak = jnp.maximum(peak, all_ref[src])
    total = jnp.exp(all_ref[0] - peak)
    for src in range(1, all_ref.shape[0]):
        total = total + jnp.exp(all_ref[src] - peak)
    joint = peak + jnp.log(total)
    place = jnp.broadcast_to(pos_ref[...].astype(f32), (8, rows))
    table = jnp.concatenate([joint, place, jnp.zeros((LANES - 16, rows), f32)], axis=0).T
    column = lax.broadcasted_iota(jnp.int32, (rows, cols), 1).astype(f32)

    def finish(level, raw):
        scale = scale_of(level, full)
        soft = jnp.exp(scale * raw - table[:, level:level + 1])
        grad_ref[level] = scale * jnp.where(column == table[:, 8:9], soft - 1.0, soft)

    level_scores(q_ref, raw_p_ref, p_ref, sems, finish)
    coef = jnp.zeros((rows, cols), f32)
    lane = lax.broadcasted_iota(jnp.int32, (1, LANES), 1)
    sk_ref[...] = jnp.zeros(sk_ref.shape, f32)

    def put(chunk, low, high, gq, gp):
        gq_hi = gq.astype(bf16)
        gq_ref[chunk, :, low:high] = gq_hi
        gp = gp.astype(bf16)
        for part in range(rows // piece):
            gp_ref[part // 2, part % 2 * chunks + chunk, :, low:high] = gp[
                part * piece:(part + 1) * piece
            ]
        gq_lo = (gq - gq_hi.astype(f32)).astype(bf16)
        terms = three_terms(s_ref[(at_ref[0] + chunks - chunk) % chunks, :, low:high])
        big = lax.dot_general(
            jnp.concatenate(terms, axis=0), gq_hi, NT, preferred_element_type=f32
        )
        low_part = lax.dot_general(
            jnp.concatenate(terms[:2], axis=0), gq_lo, NT, preferred_element_type=f32
        )
        small = big[2 * rank:] + low_part[rank:]
        sk_ref[...] += small + (big[rank:2 * rank] + low_part[:rank]) + big[:rank]

    def both(c, chunk, low, high):
        gq = jnp.dot(c, p_ref[chunk, :, low:high], preferred_element_type=f32)
        gp = lax.dot_general(
            c, query_rows(q_ref, chunk, low, high), TN, preferred_element_type=f32
        )
        return gq, gp

    held = None
    for level in range(LEVELS):
        coef = coef + grad_ref[level]
        c = coef.astype(bf16)
        upper = full >> level
        lower = full >> (level + 1) if level + 1 < LEVELS else 0
        if upper > width:
            for chunk in range(lower // width, upper // width):
                put(chunk, 0, width, *both(c, chunk, 0, width))
        elif lower >= LANES:
            put(0, lower, upper, *both(c, 0, lower, upper))
        else:
            gq, gp = both(c, 0, 0, LANES)
            if held is None:
                held = (gq, gp)
            else:
                gq = jnp.where(lane < upper, gq, held[0])
                gp = jnp.where(lane < upper, gp, held[1])
                put(0, 0, LANES, gq, gp)


def exact_dot(wide, narrow, dims):
    hi, mid, lo = [
        lax.dot_general(t, narrow, dims, preferred_element_type=f32) for t in three_terms(wide)
    ]
    return (lo + mid) + hi


def sum_scattered(value):
    count = 2 * NY * NX
    return jnp.sum(swap(value.reshape(count, -1, LANES), ALL_ROWS), axis=0)


def gathered(piece):
    return share(piece, ALL_ROWS, 2 * NY * NX).reshape(-1, LANES)


def body(queries, passages, positives, hidden_rows, sketch):
    q = queries[0]
    p = passages[0]
    rows, width = q.shape
    full = width * NZ
    rank = sketch.shape[1]
    xl = lax.axis_index("xl")
    zi = lax.axis_index("z")
    flip = [(0, 1), (1, 0)]

    piece = rows // NZ
    p_cut = jnp.broadcast_to(p.reshape(1, NZ, piece, width), (2, NZ, piece, width))
    p_cut = swap(p_cut.reshape(2 * NZ, piece, width), ("xh", "z"))
    q_blocks = jnp.broadcast_to(q[None], (2 * NZ, rows, width))
    pos_other = lax.ppermute(positives, "xl", flip)
    p_cut, q_blocks, s_own, pos_other = lax.optimization_barrier(
        (p_cut, q_blocks, sketch.T, pos_other)
    )
    p_raw = lax.all_gather(p_cut, "y")

    q_tile = swap(q_blocks, ("xl", "z")).reshape(2, NZ, rows, width)
    pos_pair = jnp.concatenate(
        [jnp.where(xl == 0, positives, pos_other), jnp.where(xl == 0, pos_other, positives)], axis=1
    )

    fetched = []
    for odd in range(2):
        pairs = []
        for r in range(2):
            for h in range(2):
                far = 2 * (2 * h + r) + odd
                at = (2 * r + h) * NZ
                pairs += [(at + i, at + (i + far) % NZ) for i in range(NZ)]
        fetched.append(lax.ppermute(s_own, ("rep", "xl", "z"), pairs))
    q_tile, p_raw, fetched = lax.optimization_barrier((q_tile, p_raw, fetched))
    tile = 2 * rows
    stats = pl.pallas_call(
        scores_kernel,
        out_shape=jax.ShapeDtypeStruct((8, tile), f32),
        in_specs=[VMEM, ANY],
        out_specs=VMEM,
        scratch_shapes=[
            pltpu.VMEM((NZ, tile, width), bf16),
            pltpu.VMEM((tile, LANES), f32),
            pltpu.SemaphoreType.DMA((2 * NY,)),
        ],
        compiler_params=pltpu.CompilerParams(vmem_limit_bytes=20 << 20),
        name="scores",
    )(q_tile, p_raw)
    stats, fetched = lax.optimization_barrier((stats, fetched))
    stats_all = share(stats, ("xl", "z"), 2 * NZ)
    s_all = jnp.stack(fetched)
    for axis in ("rep", "xl"):
        s_far = lax.ppermute(s_all, axis, flip)
        low = lax.axis_index(axis) == 0
        s_all = jnp.concatenate([jnp.where(low, s_all, s_far), jnp.where(low, s_far, s_all)])

    own_y = pos_pair // (rows * NX)
    own_x = pos_pair // rows % NX
    inside = (own_x % 2 == xl) & (pos_pair % rows // piece == zi)
    local = (own_y * 2 + own_x // 2) * piece + pos_pair % piece
    local = jnp.where(inside, local, -1)

    gq_part, gp_part, sk_part = pl.pallas_call(
        grads_kernel,
        out_shape=(
            jax.ShapeDtypeStruct((NZ, tile, width), bf16),
            jax.ShapeDtypeStruct((NY, 2 * NZ, piece, width), bf16),
            jax.ShapeDtypeStruct((rank, tile), f32),
        ),
        in_specs=[pl.BlockSpec(memory_space=pltpu.SMEM), VMEM, ANY] + [VMEM] * 3,
        out_specs=(VMEM, VMEM, VMEM),
        scratch_shapes=[
            pltpu.VMEM((NZ, tile, width), bf16),
            pltpu.VMEM((LEVELS, tile, tile), f32),
            pltpu.SemaphoreType.DMA((2 * NY,)),
        ],
        compiler_params=pltpu.CompilerParams(vmem_limit_bytes=28 << 20),
        name="grads",
    )(zi.astype(jnp.int32).reshape(1), q_tile, p_raw, stats_all, local, s_all)

    gq_sum = lax.psum_scatter(gq_part, "z", scatter_dimension=0)

    gp_sum = lax.psum_scatter(gp_part, "y", scatter_dimension=0)

    sk_blocks = jnp.stack([sk_part[:, :rows], sk_part[:, rows:]])
    sk_blocks = jnp.broadcast_to(sk_blocks[:, None], (2, NZ, rank, rows))
    sk_landed = swap(sk_blocks.reshape(2 * NZ, rank, rows), ("xl", "z"))
    batch = rows * NX * NY * 2
    sketched = jnp.sum(sk_landed, axis=0) / batch

    hidden = hidden_rows[0]
    units = hidden.shape[1]
    tiles = units // LANES
    padded = -(-tiles // 2) * 2 + (2 if tiles % 4 else 0)
    p_local = exact_dot(sketched, hidden, (((1,), (0,)), ((), ())))
    flat = p_local.reshape(rank, tiles, LANES).transpose(1, 0, 2).reshape(tiles * rank, LANES)
    pad = padded * rank - tiles * rank
    flat = jnp.concatenate([flat, jnp.zeros((pad, LANES), f32)], axis=0)
    p_flat = gathered(sum_scattered(flat))[:tiles * rank]
    p_sum = p_flat.reshape(tiles, rank, LANES).transpose(1, 0, 2).reshape(rank, units)
    gram_part = lax.dot_general(p_sum, p_sum, NT, precision=HIGHEST)
    proj_part = exact_dot(p_sum, hidden, NT)
    joined = jnp.concatenate(
        [proj_part, jnp.pad(gram_part, ((0, 0), (0, LANES - rank)))], axis=0
    )
    joined, gq_sum = lax.optimization_barrier((joined, gq_sum))
    mine = jnp.where(xl == 0, gq_sum[:rows], gq_sum[rows:])
    other = jnp.where(xl == 0, gq_sum[rows:], gq_sum[:rows])
    other = lax.ppermute(other, "xl", flip)
    grad_queries = (mine.astype(f32) + other.astype(f32)).astype(bf16)
    joined = jnp.sum(share(joined, "z", NZ), axis=0)
    proj = joined[:rank]
    gram = joined[rank:, :rank]

    q_local = exact_dot(proj, grad_queries, (((1,), (0,)), ((), ())))
    q_flat = q_local.reshape(rank, width // LANES, LANES).transpose(1, 0, 2).reshape(-1, LANES)
    q_part = sum_scattered(q_flat)
    q_part, gp_sum = lax.optimization_barrier((q_part, gp_sum))
    q_sum = gathered(q_part).reshape(width // LANES, rank, LANES).transpose(1, 0, 2)
    q_sum = q_sum.reshape(rank, width)
    keep = lax.axis_index("xh") == 0
    gp_far = lax.ppermute(jnp.where(keep, gp_sum[NZ:], gp_sum[:NZ]), "xh", flip)
    gp_near = jnp.where(keep, gp_sum[:NZ], gp_sum[NZ:])
    gp_pair = (gp_near.astype(f32) + gp_far.astype(f32)).astype(bf16)
    grad_passages = swap(gp_pair, "z").reshape(rows, width)

    lower = jnp.linalg.cholesky(gram)
    inverse = lax.linalg.triangular_solve(
        lower, jnp.eye(rank, dtype=f32), left_side=True, lower=True
    )
    p_factor = lax.dot_general(p_sum, inverse, (((0,), (1,)), ((), ())), precision=HIGHEST)
    q_factor = lax.dot_general(q_sum, inverse, (((0,), (1,)), ((), ())), precision=HIGHEST) / batch
    return (grad_queries[None], grad_passages[None], p_factor, q_factor)


def solution(mesh):
    grid = Mesh(mesh.devices.reshape(2, NY, 2, 2, NZ), ("rep", "y", "xh", "xl", "z"))
    dp = ("y", "xh", "xl")
    placed = (
        P("rep", dp, "z"),
        P("rep", dp, "z"),
        P("rep", dp),
        P("rep", dp, "z"),
        P("z", None),
    )
    return jax.shard_map(
        body,
        mesh=grid,
        in_specs=placed,
        out_specs=(P("rep", dp, "z"), P("rep", dp, "z"), P("z", None), P("z", None)),
        check_vma=False,
    )
```

time: 278 us -> 262 us (0.942)
  starting transfers between devices: 101 us -> 73.8 us
  waiting for transfers between devices: 74.9 us -> 92 us
  blocking collectives: 46.4 us -> 41.1 us
    ppermute x8 -> x5, starting transfers between devices: 38.3 us -> 16.9 us  [the longest x2 9.37 us: body(): fetched.append(lax.ppermute(s_own, ('rep', 'xl', 'z'), pairs))]
    ppermute x8 -> x5, waiting for transfers between devices: 37.2 us -> 44.5 us  [the longest x2 43.2 us: body(): fetched.append(lax.ppermute(s_own, ('rep', 'xl', 'z'), pairs))]
    all_to_all x7 -> x8, waiting for transfers between devices: 34.2 us -> 39.7 us  [swap(): return lax.all_to_all(blocks, axes, 0, 0, tiled=True)]
    all_to_all x3 -> x2, blocking collectives: 46.4 us -> 41.1 us  [swap(): return lax.all_to_all(blocks, axes, 0, 0, tiled=True)]
    all_to_all x7 -> x8, starting transfers between devices: 56.5 us -> 52 us  [swap(): return lax.all_to_all(blocks, axes, 0, 0, tiled=True)]
    ppermute x1, waiting for transfers between devices: 1.06 us -> 4.19 us  [body(): other = lax.ppermute(other, 'xl', flip)]
    unnamed x34 -> x18, local copies, waits for them, and re-layouts: 6.78 us -> 5.23 us
  transfers between devices with their start and end apart: 20 -> 18, of which waited for: 12 -> 12; matrix products, arithmetic and copies ran while one was open for 6% -> 7% of each run, Pallas kernels for 0% -> 0%
where the time goes in v3:
time: 262 us; the launch traced here: 258 us
  waiting for transfers between devices  92 us (35%)
  starting transfers between devices  73.8 us (28%)
  blocking collectives  41.1 us (16%)
  between operations  14.1 us (5%)
  local copies, waits for them, and re-layouts  13 us (5%)
  other arithmetic  11.8 us (5%)
  Pallas kernels  7.54 us (3%)
  matrix products  4.15 us (2%)
    all_to_all x8, starting transfers between devices, swap(): return lax.all_to_all(blocks, axes, 0, 0, tiled=True)  52 us
    ppermute x2, waiting for transfers between devices, body(): fetched.append(lax.ppermute(s_own, ('rep', 'xl', 'z'), pairs))  43.2 us
    all_to_all x2, blocking collectives, swap(): return lax.all_to_all(blocks, axes, 0, 0, tiled=True)  41.1 us
    all_to_all x8, waiting for transfers between devices, swap(): return lax.all_to_all(blocks, axes, 0, 0, tiled=True)  39.7 us
    ppermute x2, starting transfers between devices, body(): fetched.append(lax.ppermute(s_own, ('rep', 'xl', 'z'), pairs))  9.37 us
    pallas_call x1, Pallas kernels, body(): pl.pallas_call(grads_kernel, out_shape=(jax.ShapeDtypeStruct((NZ, tile, w...  5.93 us
  transfers between devices with their start and end apart: 18, of which 12 were waited for; matrix products, arithmetic and copies ran while one was open for 7% of the time, Pallas kernels for 0%

profile of v3, /device:TPU:57, one launch (start us, length us, event | category | flops | bytes accessed | tf_op | source)
XLA Modules:
  0.0 257.6 jit_solution(8370363465171117762)
XLA Ops:
  8.9 12.6 %all-to-all-start = ((bf16[16,16,512]{2,1,0:T(8,128)(2,1)}), bf16[16,16,512]{2,1,0:T(8,128)(2,1)S(1)}, u32[]{:S(2)}, u32[]{:S(2)}) async-start(bf16[16,16,512]{2,1,0:T(8,128)(2,1)} %bitcast.2), calls=%async_computation | async-start | bytes 524288 | tf_op jit(solution)/shard_map/all_to_all | solution.py:31
  25.9 5.8 %all-to-all-done = bf16[16,16,512]{2,1,0:T(8,128)(2,1)S(1)} async-done(((bf16[16,16,512]{2,1,0:T(8,128)(2,1)}), bf16[16,16,512]{2,1,0:T(8,128)(2,1)S(1)}, u32[]{:S(2)}, u32[]{:S(2)}) %all-to-all-start) | async-done | bytes 262176 | tf_op jit(solution)/shard_map/all_to_all | solution.py:31
  34.2 4.6 %all-to-all-start.1 = ((bf16[16,128,512]{2,1,0:T(8,128)(2,1)}), bf16[16,128,512]{2,1,0:T(8,128)(2,1)S(1)}, u32[]{:S(2)}, u32[]{:S(2)}) async-start(bf16[16,128,512]{2,1,0:T(8,128)(2,1)} %broadcast_in_dim.26), calls=%async_computation.1 | async-start | bytes 4194304 | tf_op jit(solution)/shard_map/all_to_all | solution.py:31
  39.6 5.1 %collective-permute-start.2 = (f32[32,512]{1,0:T(8,128)S(1)}, f32[32,512]{1,0:T(8,128)S(1)}, u32[]{:S(2)}, u32[]{:S(2)}) collective-permute-start(f32[32,512]{1,0:T(8,128)S(1)} %bitcast.112), channel_id=1, source_target_pairs={{0,1},{1,2},{2,3},{3,4},{4,5},{5,6},{6,7},{7,0},{8,13},{9,14},{10,... | collective-permute-start | bytes 196616 | tf_op jit(solution)/shard_map/ppermute | solution.py:240
  44.7 4.3 %collective-permute-start.1 = (f32[32,512]{1,0:T(8,128)S(1)}, f32[32,512]{1,0:T(8,128)S(1)}, u32[]{:S(2)}, u32[]{:S(2)}) collective-permute-start(f32[32,512]{1,0:T(8,128)S(1)} %bitcast.113), channel_id=1, source_target_pairs={{0,0},{1,1},{2,2},{3,3},{4,4},{5,5},{6,6},{7,7},{8,12},{9,13},{10,... | collective-permute-start | bytes 196616 | tf_op jit(solution)/shard_map/ppermute | solution.py:240
  49.0 39.8 %collective-permute-done.2 = f32[32,512]{1,0:T(8,128)S(1)} collective-permute-done((f32[32,512]{1,0:T(8,128)S(1)}, f32[32,512]{1,0:T(8,128)S(1)}, u32[]{:S(2)}, u32[]{:S(2)}) %collective-permute-start.2) | collective-permute-done | bytes 65568 | tf_op jit(solution)/shard_map/ppermute | solution.py:240
  88.8 3.3 %collective-permute-done.1 = f32[32,512]{1,0:T(8,128)S(1)} collective-permute-done((f32[32,512]{1,0:T(8,128)S(1)}, f32[32,512]{1,0:T(8,128)S(1)}, u32[]{:S(2)}, u32[]{:S(2)}) %collective-permute-start.1) | collective-permute-done | bytes 65568 | tf_op jit(solution)/shard_map/ppermute | solution.py:240
  102.1 6.2 %all-to-all-start.2 = ((f32[16,8,256]{2,1,0:T(8,128)}), f32[16,8,256]{2,1,0:T(8,128)S(1)}, u32[]{:S(2)}, u32[]{:S(2)}) async-start(f32[16,8,256]{2,1,0:T(8,128)} %broadcast_in_dim.27), calls=%async_computation.2 | async-start | bytes 262144 | tf_op jit(solution)/shard_map/all_to_all | solution.py:31
  108.4 7.3 %all-to-all-done.2.all_ref = f32[16,8,256]{2,1,0:T(8,128)S(1)} async-done(((f32[16,8,256]{2,1,0:T(8,128)}), f32[16,8,256]{2,1,0:T(8,128)S(1)}, u32[]{:S(2)}, u32[]{:S(2)}) %all-to-all-start.2) | async-done | bytes 131104 | tf_op jit(solution)/shard_map/all_to_all | solution.py:31
  117.3 5.9 %grads.1 = (bf16[8,256,512]{2,1,0:T(8,128)(2,1)S(1)}, bf16[8,16,16,512]{3,2,1,0:T(8,128)(2,1)}, f32[32,256]{1,0:T(8,128)S(1)}) custom-call(s32[1]{0:T(128)} %bitcast.at_ref, bf16[2,8,128,512]{3,2,1,0:T(8,128)(2,1)S(1)} %bitcast.91, bf16[8,16,16,512]{3,2,1,0:T(8,128)(2,1)S(1)} %bitcast.93, f32[16,8,256]{2,1,0:T(8,128)S(1)} %all-to-all-done.2.all_ref, ...), custom_call_target="tpu_custom_call" | custom-call | tf_op jit(solution)/shard_map/grads/pallas_call | solution.py:270
  125.3 3.5 %all-to-all-start.3 = ((f32[16,32,128]{2,1,0:T(8,128)}), f32[16,32,128]{2,1,0:T(8,128)S(1)}, u32[]{:S(2)}, u32[]{:S(2)}) async-start(f32[16,32,128]{2,1,0:T(8,128)} %bitcast.11), calls=%async_computation.3 | async-start | bytes 524288 | tf_op jit(solution)/shard_map/all_to_all | solution.py:31
  129.6 7.0 %all-to-all-done.3 = f32[16,32,128]{2,1,0:T(8,128)S(1)} async-done(((f32[16,32,128]{2,1,0:T(8,128)}), f32[16,32,128]{2,1,0:T(8,128)S(1)}, u32[]{:S(2)}, u32[]{:S(2)}) %all-to-all-start.3) | async-done | bytes 262176 | tf_op jit(solution)/shard_map/all_to_all | solution.py:31
  137.4 23.4 %all_to_all.50 = f32[64,8,128]{2,1,0:T(8,128)S(1)} all-to-all(f32[64,8,128]{2,1,0:T(8,128)S(1)} %pad_bitcast_fusion), channel_id=1, replica_groups=mesh['rep'=2,'y'=8,'xh'=2,'xl'=2,'z'=8] {'rep','y','xh','xl'}, dimensions={0} | all-to-all | bytes 524288 | tf_op jit(solution)/shard_map/all_to_all | solution.py:31
  160.9 17.7 %all_to_all.51 = f32[64,8,128]{2,1,0:T(8,128)S(1)} all-to-all(f32[64,8,128]{2,1,0:T(8,128)S(1)} %broadcast_in_dim.29), channel_id=1, replica_groups=mesh['rep'=2,'y'=8,'xh'=2,'xl'=2,'z'=8] {'rep','y','xh','xl'}, dimensions={0} | all-to-all | bytes 524288 | tf_op jit(solution)/shard_map/all_to_all | solution.py:31
  180.6 3.7 %all-to-all-start.6 = ((f32[8,64,128]{2,1,0:T(8,128)}), f32[8,64,128]{2,1,0:T(8,128)S(1)}, u32[]{:S(2)}, u32[]{:S(2)}) async-start(f32[8,64,128]{2,1,0:T(8,128)} %broadcast_in_dim.60), calls=%async_computation.7 | async-start | bytes 524288 | tf_op jit(solution)/shard_map/all_to_all | solution.py:31
  187.9 4.2 %collective-permute-done.5 = bf16[128,512]{1,0:T(8,128)(2,1)S(1)} collective-permute-done((bf16[128,512]{1,0:T(8,128)(2,1)S(1)}, bf16[128,512]{1,0:T(8,128)(2,1)S(1)}, u32[]{:S(2)}, u32[]{:S(2)}) %collective-permute-start.5) | collective-permute-done | bytes 131104 | tf_op jit(solution)/shard_map/ppermute | solution.py:316
  193.2 3.5 %all-to-all-done.6 = f32[8,64,128]{2,1,0:T(8,128)S(1)} async-done(((f32[8,64,128]{2,1,0:T(8,128)}), f32[8,64,128]{2,1,0:T(8,128)S(1)}, u32[]{:S(2)}, u32[]{:S(2)}) %all-to-all-start.6) | async-done | bytes 262176 | tf_op jit(solution)/shard_map/all_to_all | solution.py:31
  196.8 2.9 %cholesky.17 = f32[32,32]{1,0:T(8,128)S(1)} custom-call(f32[32,32]{1,0:T(8,128)S(1)} %fusion.27), custom_call_target="Cholesky" | custom-call | tf_op jit(solution)/shard_map/jit(cholesky)/cholesky | solution.py:334
  200.8 6.9 %all-to-all-start.7 = ((f32[64,2,128]{2,1,0:T(2,128)}), f32[64,2,128]{2,1,0:T(2,128)S(1)}, u32[]{:S(2)}, u32[]{:S(2)}) async-start(f32[64,2,128]{2,1,0:T(2,128)} %bitcast.23), calls=%async_computation.8 | async-start | bytes 131072 | tf_op jit(solution)/shard_map/all_to_all | solution.py:31
  211.4 3.9 %all-to-all-done.7 = f32[64,2,128]{2,1,0:T(2,128)S(1)} async-done(((f32[64,2,128]{2,1,0:T(2,128)}), f32[64,2,128]{2,1,0:T(2,128)S(1)}, u32[]{:S(2)}, u32[]{:S(2)}) %all-to-all-start.7) | async-done | bytes 65568 | tf_op jit(solution)/shard_map/all_to_all | solution.py:31
  220.1 7.8 %all-to-all-start.9 = ((f32[64,2,128]{2,1,0:T(2,128)}), f32[64,2,128]{2,1,0:T(2,128)S(1)}, u32[]{:S(2)}, u32[]{:S(2)}) async-start(f32[64,2,128]{2,1,0:T(2,128)} %broadcast_in_dim.61), calls=%async_computation.11 | async-start | bytes 131072 | tf_op jit(solution)/shard_map/all_to_all | solution.py:31
  229.6 5.7 %all-to-all-done.9 = f32[64,2,128]{2,1,0:T(2,128)S(1)} async-done(((f32[64,2,128]{2,1,0:T(2,128)}), f32[64,2,128]{2,1,0:T(2,128)S(1)}, u32[]{:S(2)}, u32[]{:S(2)}) %all-to-all-start.9) | async-done | bytes 65568 | tf_op jit(solution)/shard_map/all_to_all | solution.py:31
  235.3 6.7 %all-to-all-start.8 = ((bf16[8,16,512]{2,1,0:T(8,128)(2,1)}), bf16[8,16,512]{2,1,0:T(8,128)(2,1)S(1)}, u32[]{:S(2)}, u32[]{:S(2)}) async-start(bf16[8,16,512]{2,1,0:T(8,128)(2,1)} %add_convert_fusion), calls=%async_computation.10 | async-start | bytes 262144 | tf_op jit(solution)/shard_map/all_to_all | solution.py:31
  243.8 6.5 %all-to-all-done.8 = bf16[8,16,512]{2,1,0:T(8,128)(2,1)S(1)} async-done(((bf16[8,16,512]{2,1,0:T(8,128)(2,1)}), bf16[8,16,512]{2,1,0:T(8,128)(2,1)S(1)}, u32[]{:S(2)}, u32[]{:S(2)}) %all-to-all-start.8) | async-done | bytes 131104 | tf_op jit(solution)/shard_map/all_to_all | solution.py:31
  (88 shorter events, 45.1 us)
Async XLA Ops:
  7.2 129.5 %copy-start = (bf16[1,128,1792]{2,1,0:T(8,128)(2,1)S(1)}, bf16[1,128,1792]{2,1,0:T(8,128)(2,1)}, u32[]{:S(2)}) copy-start(bf16[1,128,1792]{2,1,0:T(8,128)(2,1)} %param.8) | copy-start | bytes 1376260
  8.9 22.8 %all-to-all-start = ((bf16[16,16,512]{2,1,0:T(8,128)(2,1)}), bf16[16,16,512]{2,1,0:T(8,128)(2,1)S(1)}, u32[]{:S(2)}, u32[]{:S(2)}) async-start(bf16[16,16,512]{2,1,0:T(8,128)(2,1)} %bitcast.2), calls=%async_computation | async-start | bytes 524288 | tf_op jit(solution)/shard_map/all_to_all | solution.py:31
  21.5 4.4 %collective-permute-start = (s32[1,128]{1,0:T(1,128)}, s32[1,128]{1,0:T(1,128)S(1)}, u32[]{:S(2)}, u32[]{:S(2)}) collective-permute-start(s32[1,128]{1,0:T(1,128)} %param.7), channel_id=1, source_target_pairs={{0,8},{8,0},{1,9},{9,1},{2,10},{10,2},{3,11},{11,3},{4,12},{12,4},... | collective-permute-start | bytes 1544 | tf_op jit(solution)/shard_map/ppermute | solution.py:221
  31.7 2.5 copy-start.5
  34.2 5.4 %copy-start.7 = (f32[512,32]{0,1:T(8,128)S(1)}, f32[512,32]{0,1:T(8,128)}, u32[]{:S(2)}) copy-start(f32[512,32]{0,1:T(8,128)} %param.9) | copy-start | bytes 196612
  34.2 57.9 %all-to-all-start.1 = ((bf16[16,128,512]{2,1,0:T(8,128)(2,1)}), bf16[16,128,512]{2,1,0:T(8,128)(2,1)S(1)}, u32[]{:S(2)}, u32[]{:S(2)}) async-start(bf16[16,128,512]{2,1,0:T(8,128)(2,1)} %broadcast_in_dim.26), calls=%async_computation.1 | async-start | bytes 4194304 | tf_op jit(solution)/shard_map/all_to_all | solution.py:31
  38.8 53.3 %all-gather.3.cloned.1.call-start = ((), (), s32[]{:S(2)}) async-start(), calls=%async_computation.14 | async-start | bytes 2359296 | tf_op jit(solution)/shard_map/all_gather | solution.py:225
  39.6 49.2 %collective-permute-start.2 = (f32[32,512]{1,0:T(8,128)S(1)}, f32[32,512]{1,0:T(8,128)S(1)}, u32[]{:S(2)}, u32[]{:S(2)}) collective-permute-start(f32[32,512]{1,0:T(8,128)S(1)} %bitcast.112), channel_id=1, source_target_pairs={{0,1},{1,2},{2,3},{3,4},{4,5},{5,6},{6,7},{7,0},{8,13},{9,14},{10,... | collective-permute-start | bytes 196616 | tf_op jit(solution)/shard_map/ppermute | solution.py:240
  44.7 47.5 %collective-permute-start.1 = (f32[32,512]{1,0:T(8,128)S(1)}, f32[32,512]{1,0:T(8,128)S(1)}, u32[]{:S(2)}, u32[]{:S(2)}) collective-permute-start(f32[32,512]{1,0:T(8,128)S(1)} %bitcast.113), channel_id=1, source_target_pairs={{0,0},{1,1},{2,2},{3,3},{4,4},{5,5},{6,6},{7,7},{8,12},{9,13},{10,... | collective-permute-start | bytes 196616 | tf_op jit(solution)/shard_map/ppermute | solution.py:240
  92.1 1.6 copy-start.1
  93.7 7.6 %copy-start.6 = (s32[1,128]{1,0:T(1,128)S(1)}, s32[1,128]{1,0:T(1,128)}, u32[]{:S(2)}) copy-start(s32[1,128]{1,0:T(1,128)} %param.7) | copy-start | bytes 1540
  95.4 3.2 %collective-permute-start.3 = (f32[2,32,512]{2,1,0:T(8,128)S(1)}, f32[2,32,512]{2,1,0:T(8,128)S(1)}, u32[]{:S(2)}, u32[]{:S(2)}) collective-permute-start(f32[2,32,512]{2,1,0:T(8,128)S(1)} %pad_maximum_fusion.2), channel_id=1, source_target_pairs={{0,256},{256,0},{1,257},{257,1},{2,258},{258,2},{3,259},{259,3},{4... | collective-permute-start | bytes 393224 | tf_op jit(solution)/shard_map/ppermute | solution.py:260
  98.7 9.7 %collective-permute-start.4 = (f32[4,32,512]{2,1,0:T(8,128)S(1)}, f32[4,32,512]{2,1,0:T(8,128)S(1)}, u32[]{:S(2)}, u32[]{:S(2)}) collective-permute-start(f32[4,32,512]{2,1,0:T(8,128)S(1)} %pad_maximum_fusion.1), channel_id=1, source_target_pairs={{0,8},{8,0},{1,9},{9,1},{2,10},{10,2},{3,11},{11,3},{4,12},{12,4},... | collective-permute-start | bytes 786440 | tf_op jit(solution)/shard_map/ppermute | solution.py:260
  102.1 13.6 %all-to-all-start.2 = ((f32[16,8,256]{2,1,0:T(8,128)}), f32[16,8,256]{2,1,0:T(8,128)S(1)}, u32[]{:S(2)}, u32[]{:S(2)}) async-start(f32[16,8,256]{2,1,0:T(8,128)} %broadcast_in_dim.27), calls=%async_computation.2 | async-start | bytes 262144 | tf_op jit(solution)/shard_map/all_to_all | solution.py:31
  108.3 71.6 %reduce-scatter.3.cloned.1.call-start = ((), (), s32[]{:S(2)}) async-start(), calls=%async_computation.12 | async-start | bytes 2359296 | tf_op jit(solution)/shard_map/reduce_scatter | solution.py:288
  125.3 11.3 %all-to-all-start.3 = ((f32[16,32,128]{2,1,0:T(8,128)}), f32[16,32,128]{2,1,0:T(8,128)S(1)}, u32[]{:S(2)}, u32[]{:S(2)}) async-start(f32[16,32,128]{2,1,0:T(8,128)} %bitcast.11), calls=%async_computation.3 | async-start | bytes 524288 | tf_op jit(solution)/shard_map/all_to_all | solution.py:31
  128.9 86.5 %reduce-scatter.5.cloned.1.call-start = ((), (), s32[]{:S(2)}) async-start(), calls=%async_computation.13 | async-start | bytes 2359296 | tf_op jit(solution)/shard_map/reduce_scatter | solution.py:290
  180.6 16.1 %all-to-all-start.6 = ((f32[8,64,128]{2,1,0:T(8,128)}), f32[8,64,128]{2,1,0:T(8,128)S(1)}, u32[]{:S(2)}, u32[]{:S(2)}) async-start(f32[8,64,128]{2,1,0:T(8,128)} %broadcast_in_dim.60), calls=%async_computation.7 | async-start | bytes 524288 | tf_op jit(solution)/shard_map/all_to_all | solution.py:31
  185.3 6.8 %collective-permute-start.5 = (bf16[128,512]{1,0:T(8,128)(2,1)S(1)}, bf16[128,512]{1,0:T(8,128)(2,1)S(1)}, u32[]{:S(2)}, u32[]{:S(2)}) collective-permute-start(bf16[128,512]{1,0:T(8,128)(2,1)S(1)} %broadcast_select_fusion.3), channel_id=1, source_target_pairs={{0,8},{8,0},{1,9},{9,1},{2,10},{10,2},{3,11},{11,3},{4,12},{12,4},... | collective-permute-start | bytes 393224 | tf_op jit(solution)/shard_map/ppermute | solution.py:316
  193.2 57.9 %copy-start.4 = (bf16[128,512]{1,0:T(8,128)(2,1)}, bf16[128,512]{1,0:T(8,128)(2,1)S(1)}, u32[]{:S(2)}) copy-start(bf16[128,512]{1,0:T(8,128)(2,1)S(1)} %add_convert_fusion.1) | copy-start | bytes 393220
  200.8 14.5 %all-to-all-start.7 = ((f32[64,2,128]{2,1,0:T(2,128)}), f32[64,2,128]{2,1,0:T(2,128)S(1)}, u32[]{:S(2)}, u32[]{:S(2)}) async-start(f32[64,2,128]{2,1,0:T(2,128)} %bitcast.23), calls=%async_computation.8 | async-start | bytes 131072 | tf_op jit(solution)/shard_map/all_to_all | solution.py:31
  216.4 11.5 %collective-permute-start.6 = (bf16[8,16,512]{2,1,0:T(8,128)(2,1)S(1)}, bf16[8,16,512]{2,1,0:T(8,128)(2,1)S(1)}, u32[]{:S(2)}, u32[]{:S(2)}) collective-permute-start(bf16[8,16,512]{2,1,0:T(8,128)(2,1)S(1)} %broadcast_select_fusion), channel_id=1, source_target_pairs={{0,16},{16,0},{1,17},{17,1},{2,18},{18,2},{3,19},{19,3},{4,20},{20... | collective-permute-start | bytes 393224 | tf_op jit(solution)/shard_map/ppermute | solution.py:329
  220.1 15.2 %all-to-all-start.9 = ((f32[64,2,128]{2,1,0:T(2,128)}), f32[64,2,128]{2,1,0:T(2,128)S(1)}, u32[]{:S(2)}, u32[]{:S(2)}) async-start(f32[64,2,128]{2,1,0:T(2,128)} %broadcast_in_dim.61), calls=%async_computation.11 | async-start | bytes 131072 | tf_op jit(solution)/shard_map/all_to_all | solution.py:31
  235.3 15.1 %all-to-all-start.8 = ((bf16[8,16,512]{2,1,0:T(8,128)(2,1)}), bf16[8,16,512]{2,1,0:T(8,128)(2,1)S(1)}, u32[]{:S(2)}, u32[]{:S(2)}) async-start(bf16[8,16,512]{2,1,0:T(8,128)(2,1)} %add_convert_fusion), calls=%async_computation.10 | async-start | bytes 262144 | tf_op jit(solution)/shard_map/all_to_all | solution.py:31
  (2 other events, 2.9 us)
Sparse Core Ops, SparseCore 0:
  41.7 39.6 all-gather.2
  124.7 38.8 reduce-scatter.2
  166.5 41.6 reduce-scatter.4

commit v4 on v3

--- a/solution.py
+++ b/solution.py
@@ -17,7 +17,7 @@
 bf16 = jnp.bfloat16
 HIGHEST = lax.Precision.HIGHEST
 VMEM = pl.BlockSpec(memory_space=pltpu.VMEM)
-ANY = pl.BlockSpec(memory_space=pl.ANY)
+HBM = pl.BlockSpec(memory_space=pltpu.HBM)
 ALL_ROWS = ("rep", "y", "xh", "xl")
 NT = (((1,), (1,)), ((), ()))
 TN = (((0,), (0,)), ((), ()))
@@ -33,6 +33,28 @@
 
 def share(block, axes, count):
     return swap(jnp.broadcast_to(block[None], (count,) + block.shape), axes)
+
+
+def three_terms(value):
+    hi = value.astype(bf16)
+    rest = value - hi.astype(f32)
+    mid = rest.astype(bf16)
+    return hi, mid, (rest - mid.astype(f32)).astype(bf16)
+
+
+def pieces_kernel(p_ref, s_ref, out_ref):
+    _, chunks, piece, _ = out_ref.shape
+    width = p_ref.shape[1]
+    terms = [jnp.dot(p_ref[...], t, preferred_element_type=f32) for t in three_terms(s_ref[...])]
+    products = terms[2] + terms[1] + terms[0]
+    hi = products.astype(bf16)
+    lo = (products - hi.astype(f32)).astype(bf16)
+    for half in range(2):
+        for chunk in range(chunks):
+            rows = slice(chunk * piece, (chunk + 1) * piece)
+            out_ref[half, chunk, :, :width] = p_ref[rows]
+            out_ref[half, chunk, :, width:width + LANES] = hi[rows]
+            out_ref[half, chunk, :, width + LANES:] = lo[rows]
 
 
 def query_rows(q_ref, chunk, low, high):
@@ -49,7 +71,7 @@
         for half in range(2):
             moves.append(
                 pltpu.make_async_copy(
-                    raw_p_ref.at[y, pl.ds(half * chunks, chunks)],
+                    raw_p_ref.at[y, pl.ds(half * chunks, chunks), :, pl.ds(0, p_ref.shape[2])],
                     p_ref.at[:, pl.ds((2 * y + half) * piece, piece)],
                     sems.at[2 * y + half],
                 )
@@ -104,21 +126,14 @@
     stats_ref[...] = table_ref[...].T[:8]
 
 
-def three_terms(value):
-    hi = value.astype(bf16)
-    rest = value - hi.astype(f32)
-    mid = rest.astype(bf16)
-    return hi, mid, (rest - mid.astype(f32)).astype(bf16)
-
-
 def grads_kernel(
-    at_ref, q_ref, raw_p_ref, all_ref, pos_ref, s_ref, gq_ref, gp_ref, sk_ref, p_ref, grad_ref, sems
+    q_ref, raw_p_ref, all_ref, pos_ref, gq_ref, gp_ref, sk_ref, p_ref, grad_ref, sems
 ):
     _, chunks, half_rows, width = q_ref.shape
     rows = 2 * half_rows
     full = chunks * width
     cols = p_ref.shape[1]
-    rank = s_ref.shape[1]
+    rank = sk_ref.shape[0]
     piece = gp_ref.shape[2]
     peak = all_ref[0]
     for src in range(1, all_ref.shape[0]):
@@ -139,26 +154,20 @@
     level_scores(q_ref, raw_p_ref, p_ref, sems, finish)
     coef = jnp.zeros((rows, cols), f32)
     lane = lax.broadcasted_iota(jnp.int32, (1, LANES), 1)
-    sk_ref[...] = jnp.zeros(sk_ref.shape, f32)
+    sub_lane = lax.broadcasted_iota(jnp.int32, (cols, LANES), 1) // rank
+    sketched = jnp.zeros((rows, LANES), f32)
+
+    def products(chunk):
+        hi = p_ref[chunk, :, width:width + LANES].astype(f32)
+        return hi + p_ref[chunk, :, width + LANES:].astype(f32)
 
     def put(chunk, low, high, gq, gp):
-        gq_hi = gq.astype(bf16)
-        gq_ref[chunk, :, low:high] = gq_hi
+        gq_ref[chunk, :, low:high] = gq.astype(bf16)
         gp = gp.astype(bf16)
         for part in range(rows // piece):
             gp_ref[part // 2, part % 2 * chunks + chunk, :, low:high] = gp[
                 part * piece:(part + 1) * piece
             ]
-        gq_lo = (gq - gq_hi.astype(f32)).astype(bf16)
-        terms = three_terms(s_ref[(at_ref[0] + chunks - chunk) % chunks, :, low:high])
-        big = lax.dot_general(
-            jnp.concatenate(terms, axis=0), gq_hi, NT, preferred_element_type=f32
-        )
-        low_part = lax.dot_general(
-            jnp.concatenate(terms[:2], axis=0), gq_lo, NT, preferred_element_type=f32
-        )
-        small = big[2 * rank:] + low_part[rank:]
-        sk_ref[...] += small + (big[rank:2 * rank] + low_part[:rank]) + big[:rank]
 
     def both(c, chunk, low, high):
         gq = jnp.dot(c, p_ref[chunk, :, low:high], preferred_element_type=f32)
@@ -173,6 +182,14 @@
         c = coef.astype(bf16)
         upper = full >> level
         lower = full >> (level + 1) if level + 1 < LEVELS else 0
+        if upper > width:
+            own = products(lower // width)
+            for chunk in range(lower // width + 1, upper // width):
+                own = own + products(chunk)
+        else:
+            own = jnp.where(sub_lane == LEVELS - 1 - level, products(0), 0.0)
+        for term in three_terms(own)[::-1]:
+            sketched = sketched + jnp.dot(c, term, preferred_element_type=f32)
         if upper > width:
             for chunk in range(lower // width, upper // width):
                 put(chunk, 0, width, *both(c, chunk, 0, width))
@@ -186,6 +203,11 @@
                 gq = jnp.where(lane < upper, gq, held[0])
                 gp = jnp.where(lane < upper, gp, held[1])
                 put(0, 0, LANES, gq, gp)
+    turned = sketched.T
+    total = turned[:rank]
+    for sub in range(1, LANES // rank):
+        total = total + turned[sub * rank:(sub + 1) * rank]
+    sk_ref[...] = total
 
 
 def exact_dot(wide, narrow, dims):
@@ -215,13 +237,24 @@
     flip = [(0, 1), (1, 0)]
 
     piece = rows // NZ
-    p_cut = jnp.broadcast_to(p.reshape(1, NZ, piece, width), (2, NZ, piece, width))
-    p_cut = swap(p_cut.reshape(2 * NZ, piece, width), ("xh", "z"))
+    row = lax.broadcasted_iota(jnp.int32, (width, LANES), 0)
+    sub = lax.broadcasted_iota(jnp.int32, (width, LANES), 1) // rank
+    upper = (full >> (LEVELS - 1)) << sub
+    lower = jnp.where(sub == 0, 0, upper // 2)
+    s_subs = jnp.where((row >= lower) & (row < upper), jnp.tile(sketch, (1, LANES // rank)), 0.0)
+    wide = width + 2 * LANES
+    p_cut = pl.pallas_call(
+        pieces_kernel,
+        out_shape=jax.ShapeDtypeStruct((2, NZ, piece, wide), bf16),
+        in_specs=[VMEM, VMEM],
+        out_specs=VMEM,
+        compiler_params=pltpu.CompilerParams(vmem_limit_bytes=8 << 20),
+        name="pieces",
+    )(p, s_subs)
+    p_cut = swap(p_cut.reshape(2 * NZ, piece, wide), ("xh", "z"))
     q_blocks = jnp.broadcast_to(q[None], (2 * NZ, rows, width))
     pos_other = lax.ppermute(positives, "xl", flip)
-    p_cut, q_blocks, s_own, pos_other = lax.optimization_barrier(
-        (p_cut, q_blocks, sketch.T, pos_other)
-    )
+    p_cut, q_blocks, pos_other = lax.optimization_barrier((p_cut, q_blocks, pos_other))
     p_raw = lax.all_gather(p_cut, "y")
 
     q_tile = swap(q_blocks, ("xl", "z")).reshape(2, NZ, rows, width)
@@ -229,21 +262,11 @@
         [jnp.where(xl == 0, positives, pos_other), jnp.where(xl == 0, pos_other, positives)], axis=1
     )
 
-    fetched = []
-    for odd in range(2):
-        pairs = []
-        for r in range(2):
-            for h in range(2):
-                far = 2 * (2 * h + r) + odd
-                at = (2 * r + h) * NZ
-                pairs += [(at + i, at + (i + far) % NZ) for i in range(NZ)]
-        fetched.append(lax.ppermute(s_own, ("rep", "xl", "z"), pairs))
-    q_tile, p_raw, fetched = lax.optimization_barrier((q_tile, p_raw, fetched))
     tile = 2 * rows
     stats = pl.pallas_call(
         scores_kernel,
         out_shape=jax.ShapeDtypeStruct((8, tile), f32),
-        in_specs=[VMEM, ANY],
+        in_specs=[VMEM, HBM],
         out_specs=VMEM,
         scratch_shapes=[
             pltpu.VMEM((NZ, tile, width), bf16),
@@ -253,14 +276,7 @@
         compiler_params=pltpu.CompilerParams(vmem_limit_bytes=20 << 20),
         name="scores",
     )(q_tile, p_raw)
-    stats, fetched = lax.optimization_barrier((stats, fetched))
     stats_all = share(stats, ("xl", "z"), 2 * NZ)
-    s_all = jnp.stack(fetched)
-    for axis in ("rep", "xl"):
-        s_far = lax.ppermute(s_all, axis, flip)
-        low = lax.axis_index(axis) == 0
-        s_all = jnp.concatenate([jnp.where(low, s_all, s_far), jnp.where(low, s_far, s_all)])
-
     own_y = pos_pair // (rows * NX)
     own_x = pos_pair // rows % NX
     inside = (own_x % 2 == xl) & (pos_pair % rows // piece == zi)
@@ -274,16 +290,16 @@
             jax.ShapeDtypeStruct((NY, 2 * NZ, piece, width), bf16),
             jax.ShapeDtypeStruct((rank, tile), f32),
         ),
-        in_specs=[pl.BlockSpec(memory_space=pltpu.SMEM), VMEM, ANY] + [VMEM] * 3,
+        in_specs=[VMEM, HBM, VMEM, VMEM],
         out_specs=(VMEM, VMEM, VMEM),
         scratch_shapes=[
-            pltpu.VMEM((NZ, tile, width), bf16),
+            pltpu.VMEM((NZ, tile, wide), bf16),
             pltpu.VMEM((LEVELS, tile, tile), f32),
             pltpu.SemaphoreType.DMA((2 * NY,)),
         ],
         compiler_params=pltpu.CompilerParams(vmem_limit_bytes=28 << 20),
         name="grads",
-    )(zi.astype(jnp.int32).reshape(1), q_tile, p_raw, stats_all, local, s_all)
+    )(q_tile, p_raw, stats_all, local)
 
     gq_sum = lax.psum_scatter(gq_part, "z", scatter_dimension=0)
 

time: 262 us -> 254 us (0.969)
  starting transfers between devices: 73.8 us -> 60.3 us
  waiting for transfers between devices: 92 us -> 96 us
    all_to_all x8, waiting for transfers between devices: 39.7 us -> 88.9 us  [swap(): return lax.all_to_all(blocks, axes, 0, 0, tiled=True)]
    ppermute x4 -> x0, waiting for transfers between devices: 44.5 us -> none  [the longest x2 43.2 us: body(): fetched.append(lax.ppermute(s_own, ('rep', 'xl', 'z'), pairs))]
    ppermute x4 -> x0, starting transfers between devices: 14 us -> none  [the longest x2 9.37 us: body(): fetched.append(lax.ppermute(s_own, ('rep', 'xl', 'z'), pairs))]
    unnamed x18 -> x20, local copies, waits for them, and re-layouts: 5.23 us -> 6.75 us
  transfers between devices with their start and end apart: 18 -> 14, of which waited for: 12 -> 10; matrix products, arithmetic and copies ran while one was open for 7% -> 7% of each run, Pallas kernels for 0% -> 0%
where the time goes in v4:
time: 254 us; the launch traced here: 250 us
  waiting for transfers between devices  96 us (38%)
  starting transfers between devices  60.3 us (24%)
  blocking collectives  42.8 us (17%)
  between operations  14.1 us (6%)
  local copies, waits for them, and re-layouts  13 us (5%)
  other arithmetic  11.8 us (5%)
  Pallas kernels  7.8 us (3%)
  matrix products  4.16 us (2%)
    all_to_all x8, waiting for transfers between devices, swap(): return lax.all_to_all(blocks, axes, 0, 0, tiled=True)  88.9 us
    all_to_all x8, starting transfers between devices, swap(): return lax.all_to_all(blocks, axes, 0, 0, tiled=True)  52.4 us
    all_to_all x2, blocking collectives, swap(): return lax.all_to_all(blocks, axes, 0, 0, tiled=True)  42.8 us
    unnamed x20, local copies, waits for them, and re-layouts  6.75 us
    pallas_call x1, Pallas kernels, body(): pl.pallas_call(grads_kernel, out_shape=(jax.ShapeDtypeStruct((NZ, tile, w...  5.35 us
  transfers between devices with their start and end apart: 14, of which 10 were waited for; matrix products, arithmetic and copies ran while one was open for 7% of the time, Pallas kernels for 0%

profile of v4, /device:TPU:57, one launch (start us, length us, event | category | flops | bytes accessed | tf_op | source)
XLA Modules:
  0.0 249.8 jit_solution(10672781909090179082)
XLA Ops:
  10.3 12.6 %all-to-all-start = ((bf16[16,16,768]{2,1,0:T(8,128)(2,1)}), bf16[16,16,768]{2,1,0:T(8,128)(2,1)S(1)}, u32[]{:S(2)}, u32[]{:S(2)}) async-start(bf16[16,16,768]{2,1,0:T(8,128)(2,1)} %bitcast.2), calls=%async_computation | async-start | bytes 786432 | tf_op jit(solution)/shard_map/all_to_all | solution.py:31
  27.2 7.9 %all-to-all-done = bf16[16,16,768]{2,1,0:T(8,128)(2,1)S(1)} async-done(((bf16[16,16,768]{2,1,0:T(8,128)(2,1)}), bf16[16,16,768]{2,1,0:T(8,128)(2,1)S(1)}, u32[]{:S(2)}, u32[]{:S(2)}) %all-to-all-start) | async-done | bytes 393248 | tf_op jit(solution)/shard_map/all_to_all | solution.py:31
  36.7 5.0 %all-to-all-start.1 = ((bf16[16,128,512]{2,1,0:T(8,128)(2,1)}), bf16[16,128,512]{2,1,0:T(8,128)(2,1)S(1)}, u32[]{:S(2)}, u32[]{:S(2)}) async-start(bf16[16,128,512]{2,1,0:T(8,128)(2,1)} %broadcast_in_dim.27), calls=%async_computation.1 | async-start | bytes 4194304 | tf_op jit(solution)/shard_map/all_to_all | solution.py:31
  41.7 47.2 %all-to-all-done.1 = bf16[16,128,512]{2,1,0:T(8,128)(2,1)S(1)} async-done(((bf16[16,128,512]{2,1,0:T(8,128)(2,1)}), bf16[16,128,512]{2,1,0:T(8,128)(2,1)S(1)}, u32[]{:S(2)}, u32[]{:S(2)}) %all-to-all-start.1) | async-done | bytes 2097184 | tf_op jit(solution)/shard_map/all_to_all | solution.py:31
  92.9 5.8 %all-to-all-start.2 = ((f32[16,8,256]{2,1,0:T(8,128)}), f32[16,8,256]{2,1,0:T(8,128)S(1)}, u32[]{:S(2)}, u32[]{:S(2)}) async-start(f32[16,8,256]{2,1,0:T(8,128)} %broadcast_in_dim.28), calls=%async_computation.2 | async-start | bytes 262144 | tf_op jit(solution)/shard_map/all_to_all | solution.py:31
  98.8 7.4 %all-to-all-done.2.all_ref = f32[16,8,256]{2,1,0:T(8,128)S(1)} async-done(((f32[16,8,256]{2,1,0:T(8,128)}), f32[16,8,256]{2,1,0:T(8,128)S(1)}, u32[]{:S(2)}, u32[]{:S(2)}) %all-to-all-start.2) | async-done | bytes 131104 | tf_op jit(solution)/shard_map/all_to_all | solution.py:31
  108.2 5.3 %grads.1 = (bf16[8,256,512]{2,1,0:T(8,128)(2,1)S(1)}, bf16[8,16,16,512]{3,2,1,0:T(8,128)(2,1)}, f32[32,256]{1,0:T(8,128)S(1)}) custom-call(bf16[2,8,128,512]{3,2,1,0:T(8,128)(2,1)S(1)} %bitcast.88, bf16[8,16,16,768]{3,2,1,0:T(8,128)(2,1)S(1)} %bitcast.90, f32[16,8,256]{2,1,0:T(8,128)S(1)} %all-to-all-done.2.all_ref, s32[1,256]{1,0:T(1,128)S(1)} %and_select_fusion.3.pos_ref), custom_call_target="tpu_custom_call" | custom-call | tf_op jit(solution)/shard_map/grads/pallas_call | solution.py:286
  115.6 3.5 %all-to-all-start.3 = ((f32[16,32,128]{2,1,0:T(8,128)}), f32[16,32,128]{2,1,0:T(8,128)S(1)}, u32[]{:S(2)}, u32[]{:S(2)}) async-start(f32[16,32,128]{2,1,0:T(8,128)} %bitcast.8), calls=%async_computation.3 | async-start | bytes 524288 | tf_op jit(solution)/shard_map/all_to_all | solution.py:31
  119.9 7.0 %all-to-all-done.3 = f32[16,32,128]{2,1,0:T(8,128)S(1)} async-done(((f32[16,32,128]{2,1,0:T(8,128)}), f32[16,32,128]{2,1,0:T(8,128)S(1)}, u32[]{:S(2)}, u32[]{:S(2)}) %all-to-all-start.3) | async-done | bytes 262176 | tf_op jit(solution)/shard_map/all_to_all | solution.py:31
  127.7 25.1 %all_to_all.50 = f32[64,8,128]{2,1,0:T(8,128)S(1)} all-to-all(f32[64,8,128]{2,1,0:T(8,128)S(1)} %pad_bitcast_fusion), channel_id=1, replica_groups=mesh['rep'=2,'y'=8,'xh'=2,'xl'=2,'z'=8] {'rep','y','xh','xl'}, dimensions={0} | all-to-all | bytes 524288 | tf_op jit(solution)/shard_map/all_to_all | solution.py:31
  152.9 17.7 %all_to_all.51 = f32[64,8,128]{2,1,0:T(8,128)S(1)} all-to-all(f32[64,8,128]{2,1,0:T(8,128)S(1)} %broadcast_in_dim.30), channel_id=1, replica_groups=mesh['rep'=2,'y'=8,'xh'=2,'xl'=2,'z'=8] {'rep','y','xh','xl'}, dimensions={0} | all-to-all | bytes 524288 | tf_op jit(solution)/shard_map/all_to_all | solution.py:31
  172.6 3.7 %all-to-all-start.6 = ((f32[8,64,128]{2,1,0:T(8,128)}), f32[8,64,128]{2,1,0:T(8,128)S(1)}, u32[]{:S(2)}, u32[]{:S(2)}) async-start(f32[8,64,128]{2,1,0:T(8,128)} %broadcast_in_dim.58), calls=%async_computation.7 | async-start | bytes 524288 | tf_op jit(solution)/shard_map/all_to_all | solution.py:31
  177.3 2.6 %collective-permute-start.1 = (bf16[128,512]{1,0:T(8,128)(2,1)S(1)}, bf16[128,512]{1,0:T(8,128)(2,1)S(1)}, u32[]{:S(2)}, u32[]{:S(2)}) collective-permute-start(bf16[128,512]{1,0:T(8,128)(2,1)S(1)} %broadcast_select_fusion.1), channel_id=1, source_target_pairs={{0,8},{8,0},{1,9},{9,1},{2,10},{10,2},{3,11},{11,3},{4,12},{12,4},... | collective-permute-start | bytes 393224 | tf_op jit(solution)/shard_map/ppermute | solution.py:332
  179.9 4.2 %collective-permute-done.1 = bf16[128,512]{1,0:T(8,128)(2,1)S(1)} collective-permute-done((bf16[128,512]{1,0:T(8,128)(2,1)S(1)}, bf16[128,512]{1,0:T(8,128)(2,1)S(1)}, u32[]{:S(2)}, u32[]{:S(2)}) %collective-permute-start.1) | collective-permute-done | bytes 131104 | tf_op jit(solution)/shard_map/ppermute | solution.py:332
  185.2 3.5 %all-to-all-done.6 = f32[8,64,128]{2,1,0:T(8,128)S(1)} async-done(((f32[8,64,128]{2,1,0:T(8,128)}), f32[8,64,128]{2,1,0:T(8,128)S(1)}, u32[]{:S(2)}, u32[]{:S(2)}) %all-to-all-start.6) | async-done | bytes 262176 | tf_op jit(solution)/shard_map/all_to_all | solution.py:31
  188.8 2.9 %cholesky.17 = f32[32,32]{1,0:T(8,128)S(1)} custom-call(f32[32,32]{1,0:T(8,128)S(1)} %fusion.37), custom_call_target="Cholesky" | custom-call | tf_op jit(solution)/shard_map/jit(cholesky)/cholesky | solution.py:350
  192.8 6.8 %all-to-all-start.7 = ((f32[64,2,128]{2,1,0:T(2,128)}), f32[64,2,128]{2,1,0:T(2,128)S(1)}, u32[]{:S(2)}, u32[]{:S(2)}) async-start(f32[64,2,128]{2,1,0:T(2,128)} %bitcast.20), calls=%async_computation.8 | async-start | bytes 131072 | tf_op jit(solution)/shard_map/all_to_all | solution.py:31
  201.0 2.4 custom-call.6
  203.4 3.8 %all-to-all-done.7 = f32[64,2,128]{2,1,0:T(2,128)S(1)} async-done(((f32[64,2,128]{2,1,0:T(2,128)}), f32[64,2,128]{2,1,0:T(2,128)S(1)}, u32[]{:S(2)}, u32[]{:S(2)}) %all-to-all-start.7) | async-done | bytes 65568 | tf_op jit(solution)/shard_map/all_to_all | solution.py:31
  208.3 2.9 %collective-permute-start.2 = (bf16[8,16,512]{2,1,0:T(8,128)(2,1)S(1)}, bf16[8,16,512]{2,1,0:T(8,128)(2,1)S(1)}, u32[]{:S(2)}, u32[]{:S(2)}) collective-permute-start(bf16[8,16,512]{2,1,0:T(8,128)(2,1)S(1)} %broadcast_select_fusion), channel_id=1, source_target_pairs={{0,16},{16,0},{1,17},{17,1},{2,18},{18,2},{3,19},{19,3},{4,20},{20... | collective-permute-start | bytes 393224 | tf_op jit(solution)/shard_map/ppermute | solution.py:345
  212.1 7.8 %all-to-all-start.9 = ((f32[64,2,128]{2,1,0:T(2,128)}), f32[64,2,128]{2,1,0:T(2,128)S(1)}, u32[]{:S(2)}, u32[]{:S(2)}) async-start(f32[64,2,128]{2,1,0:T(2,128)} %broadcast_in_dim.59), calls=%async_computation.11 | async-start | bytes 131072 | tf_op jit(solution)/shard_map/all_to_all | solution.py:31
  221.5 5.7 %all-to-all-done.9 = f32[64,2,128]{2,1,0:T(2,128)S(1)} async-done(((f32[64,2,128]{2,1,0:T(2,128)}), f32[64,2,128]{2,1,0:T(2,128)S(1)}, u32[]{:S(2)}, u32[]{:S(2)}) %all-to-all-start.9) | async-done | bytes 65568 | tf_op jit(solution)/shard_map/all_to_all | solution.py:31
  227.2 7.1 %all-to-all-start.8 = ((bf16[8,16,512]{2,1,0:T(8,128)(2,1)}), bf16[8,16,512]{2,1,0:T(8,128)(2,1)S(1)}, u32[]{:S(2)}, u32[]{:S(2)}) async-start(bf16[8,16,512]{2,1,0:T(8,128)(2,1)} %add_convert_fusion), calls=%async_computation.10 | async-start | bytes 262144 | tf_op jit(solution)/shard_map/all_to_all | solution.py:31
  236.1 6.5 %all-to-all-done.8 = bf16[8,16,512]{2,1,0:T(8,128)(2,1)S(1)} async-done(((bf16[8,16,512]{2,1,0:T(8,128)(2,1)}), bf16[8,16,512]{2,1,0:T(8,128)(2,1)S(1)}, u32[]{:S(2)}, u32[]{:S(2)}) %all-to-all-start.8) | async-done | bytes 131104 | tf_op jit(solution)/shard_map/all_to_all | solution.py:31
  (82 shorter events, 31.1 us)
Async XLA Ops:
  7.2 119.7 %copy-start = (bf16[1,128,1792]{2,1,0:T(8,128)(2,1)S(1)}, bf16[1,128,1792]{2,1,0:T(8,128)(2,1)}, u32[]{:S(2)}) copy-start(bf16[1,128,1792]{2,1,0:T(8,128)(2,1)} %param.8) | copy-start | bytes 1376260
  7.2 15.7 %copy-start.8 = (s32[1,128]{1,0:T(1,128)S(1)}, s32[1,128]{1,0:T(1,128)}, u32[]{:S(2)}) copy-start(s32[1,128]{1,0:T(1,128)} %param.7) | copy-start | bytes 1540
  7.2 27.9 %copy-start.7 = (bf16[1,128,512]{2,1,0:T(8,128)(2,1)S(1)}, bf16[1,128,512]{2,1,0:T(8,128)(2,1)}, u32[]{:S(2)}) copy-start(bf16[1,128,512]{2,1,0:T(8,128)(2,1)} %param.5) | copy-start | bytes 393220
  8.3 0.9 copy-start.4
  10.3 24.8 %all-to-all-start = ((bf16[16,16,768]{2,1,0:T(8,128)(2,1)}), bf16[16,16,768]{2,1,0:T(8,128)(2,1)S(1)}, u32[]{:S(2)}, u32[]{:S(2)}) async-start(bf16[16,16,768]{2,1,0:T(8,128)(2,1)} %bitcast.2), calls=%async_computation | async-start | bytes 786432 | tf_op jit(solution)/shard_map/all_to_all | solution.py:31
  22.9 66.1 %all-gather.3.cloned.1.call-start = ((), (), s32[]{:S(2)}) async-start(), calls=%async_computation.14 | async-start | bytes 3538944 | tf_op jit(solution)/shard_map/all_gather | solution.py:258
  22.9 4.3 %collective-permute-start = (s32[1,128]{1,0:T(1,128)S(1)}, s32[1,128]{1,0:T(1,128)S(1)}, u32[]{:S(2)}, u32[]{:S(2)}) collective-permute-start(s32[1,128]{1,0:T(1,128)S(1)} %copy-done.8), channel_id=1, source_target_pairs={{0,8},{8,0},{1,9},{9,1},{2,10},{10,2},{3,11},{11,3},{4,12},{12,4},... | collective-permute-start | bytes 1544 | tf_op jit(solution)/shard_map/ppermute | solution.py:256
  35.1 1.6 copy-start.6
  36.7 52.2 %all-to-all-start.1 = ((bf16[16,128,512]{2,1,0:T(8,128)(2,1)}), bf16[16,128,512]{2,1,0:T(8,128)(2,1)S(1)}, u32[]{:S(2)}, u32[]{:S(2)}) async-start(bf16[16,128,512]{2,1,0:T(8,128)(2,1)} %broadcast_in_dim.27), calls=%async_computation.1 | async-start | bytes 4194304 | tf_op jit(solution)/shard_map/all_to_all | solution.py:31
  88.9 1.9 copy-start.1
  92.9 13.3 %all-to-all-start.2 = ((f32[16,8,256]{2,1,0:T(8,128)}), f32[16,8,256]{2,1,0:T(8,128)S(1)}, u32[]{:S(2)}, u32[]{:S(2)}) async-start(f32[16,8,256]{2,1,0:T(8,128)} %broadcast_in_dim.28), calls=%async_computation.2 | async-start | bytes 262144 | tf_op jit(solution)/shard_map/all_to_all | solution.py:31
  98.7 73.1 %reduce-scatter.3.cloned.1.call-start = ((), (), s32[]{:S(2)}) async-start(), calls=%async_computation.12 | async-start | bytes 2359296 | tf_op jit(solution)/shard_map/reduce_scatter | solution.py:304
  106.3 1.9 copy-start.2
  113.5 1.3 copy-start.3
  115.6 11.3 %all-to-all-start.3 = ((f32[16,32,128]{2,1,0:T(8,128)}), f32[16,32,128]{2,1,0:T(8,128)S(1)}, u32[]{:S(2)}, u32[]{:S(2)}) async-start(f32[16,32,128]{2,1,0:T(8,128)} %bitcast.8), calls=%async_computation.3 | async-start | bytes 524288 | tf_op jit(solution)/shard_map/all_to_all | solution.py:31
  119.2 88.1 %reduce-scatter.5.cloned.1.call-start = ((), (), s32[]{:S(2)}) async-start(), calls=%async_computation.13 | async-start | bytes 2359296 | tf_op jit(solution)/shard_map/reduce_scatter | solution.py:306
  172.6 16.1 %all-to-all-start.6 = ((f32[8,64,128]{2,1,0:T(8,128)}), f32[8,64,128]{2,1,0:T(8,128)S(1)}, u32[]{:S(2)}, u32[]{:S(2)}) async-start(f32[8,64,128]{2,1,0:T(8,128)} %broadcast_in_dim.58), calls=%async_computation.7 | async-start | bytes 524288 | tf_op jit(solution)/shard_map/all_to_all | solution.py:31
  177.3 6.9 %collective-permute-start.1 = (bf16[128,512]{1,0:T(8,128)(2,1)S(1)}, bf16[128,512]{1,0:T(8,128)(2,1)S(1)}, u32[]{:S(2)}, u32[]{:S(2)}) collective-permute-start(bf16[128,512]{1,0:T(8,128)(2,1)S(1)} %broadcast_select_fusion.1), channel_id=1, source_target_pairs={{0,8},{8,0},{1,9},{9,1},{2,10},{10,2},{3,11},{11,3},{4,12},{12,4},... | collective-permute-start | bytes 393224 | tf_op jit(solution)/shard_map/ppermute | solution.py:332
  185.2 58.1 %copy-start.5 = (bf16[128,512]{1,0:T(8,128)(2,1)}, bf16[128,512]{1,0:T(8,128)(2,1)S(1)}, u32[]{:S(2)}) copy-start(bf16[128,512]{1,0:T(8,128)(2,1)S(1)} %add_convert_fusion.1) | copy-start | bytes 393220
  192.8 14.4 %all-to-all-start.7 = ((f32[64,2,128]{2,1,0:T(2,128)}), f32[64,2,128]{2,1,0:T(2,128)S(1)}, u32[]{:S(2)}, u32[]{:S(2)}) async-start(f32[64,2,128]{2,1,0:T(2,128)} %bitcast.20), calls=%async_computation.8 | async-start | bytes 131072 | tf_op jit(solution)/shard_map/all_to_all | solution.py:31
  208.3 11.6 %collective-permute-start.2 = (bf16[8,16,512]{2,1,0:T(8,128)(2,1)S(1)}, bf16[8,16,512]{2,1,0:T(8,128)(2,1)S(1)}, u32[]{:S(2)}, u32[]{:S(2)}) collective-permute-start(bf16[8,16,512]{2,1,0:T(8,128)(2,1)S(1)} %broadcast_select_fusion), channel_id=1, source_target_pairs={{0,16},{16,0},{1,17},{17,1},{2,18},{18,2},{3,19},{19,3},{4,20},{20... | collective-permute-start | bytes 393224 | tf_op jit(solution)/shard_map/ppermute | solution.py:345
  212.1 15.1 %all-to-all-start.9 = ((f32[64,2,128]{2,1,0:T(2,128)}), f32[64,2,128]{2,1,0:T(2,128)S(1)}, u32[]{:S(2)}, u32[]{:S(2)}) async-start(f32[64,2,128]{2,1,0:T(2,128)} %broadcast_in_dim.59), calls=%async_computation.11 | async-start | bytes 131072 | tf_op jit(solution)/shard_map/all_to_all | solution.py:31
  227.2 15.4 %all-to-all-start.8 = ((bf16[8,16,512]{2,1,0:T(8,128)(2,1)}), bf16[8,16,512]{2,1,0:T(8,128)(2,1)S(1)}, u32[]{:S(2)}, u32[]{:S(2)}) async-start(bf16[8,16,512]{2,1,0:T(8,128)(2,1)} %add_convert_fusion), calls=%async_computation.10 | async-start | bytes 262144 | tf_op jit(solution)/shard_map/all_to_all | solution.py:31
Sparse Core Ops, SparseCore 0:
  36.8 43.7 all-gather.2
  115.0 40.6 reduce-scatter.2
  158.5 41.8 reduce-scatter.4

commit v5 on v4

--- a/solution.py
+++ b/solution.py
@@ -337,15 +337,13 @@
 
     q_local = exact_dot(proj, grad_queries, (((1,), (0,)), ((), ())))
     q_flat = q_local.reshape(rank, width // LANES, LANES).transpose(1, 0, 2).reshape(-1, LANES)
+    q_flat, gram = lax.optimization_barrier((q_flat, gram))
     q_part = sum_scattered(q_flat)
-    q_part, gp_sum = lax.optimization_barrier((q_part, gp_sum))
-    q_sum = gathered(q_part).reshape(width // LANES, rank, LANES).transpose(1, 0, 2)
-    q_sum = q_sum.reshape(rank, width)
-    keep = lax.axis_index("xh") == 0
-    gp_far = lax.ppermute(jnp.where(keep, gp_sum[NZ:], gp_sum[:NZ]), "xh", flip)
-    gp_near = jnp.where(keep, gp_sum[:NZ], gp_sum[NZ:])
-    gp_pair = (gp_near.astype(f32) + gp_far.astype(f32)).astype(bf16)
-    grad_passages = swap(gp_pair, "z").reshape(rows, width)
+    q_sum = gathered(q_part)
+    q_sum, gp_sum = lax.optimization_barrier((q_sum, gp_sum))
+    q_sum = q_sum.reshape(width // LANES, rank, LANES).transpose(1, 0, 2).reshape(rank, width)
+    gp_home = swap(gp_sum, ("xh", "z")).reshape(2, rows, width).astype(f32)
+    grad_passages = (gp_home[0] + gp_home[1]).astype(bf16)
 
     lower = jnp.linalg.cholesky(gram)
     inverse = lax.linalg.triangular_solve(

time: 254 us -> 246 us (0.969)
  starting transfers between devices: 60.3 us -> 54.5 us
    ppermute x1 -> x0, starting transfers between devices: 2.95 us -> none  [body(): gp_far = lax.ppermute(jnp.where(keep, gp_sum[NZ:], gp_sum[:NZ]), 'xh', flip)]
    all_to_all x8, starting transfers between devices: 52.4 us -> 49.5 us  [swap(): return lax.all_to_all(blocks, axes, 0, 0, tiled=True)]
    unnamed x20 -> x18, local copies, waits for them, and re-layouts: 6.75 us -> 6.03 us
  transfers between devices with their start and end apart: 14 -> 13, of which waited for: 10 -> 10; matrix products, arithmetic and copies ran while one was open for 7% -> 7% of each run, Pallas kernels for 0% -> 0%
where the time goes in v5:
time: 246 us; the launch traced here: 242 us
  waiting for transfers between devices  96.3 us (39%)
  starting transfers between devices  54.5 us (22%)
  blocking collectives  42.7 us (17%)
  between operations  14.1 us (6%)
  local copies, waits for them, and re-layouts  12.4 us (5%)
  other arithmetic  9.86 us (4%)
  Pallas kernels  7.84 us (3%)
  matrix products  4.16 us (2%)
    all_to_all x8, waiting for transfers between devices, swap(): return lax.all_to_all(blocks, axes, 0, 0, tiled=True)  89.3 us
    all_to_all x8, starting transfers between devices, swap(): return lax.all_to_all(blocks, axes, 0, 0, tiled=True)  49.5 us
    all_to_all x2, blocking collectives, swap(): return lax.all_to_all(blocks, axes, 0, 0, tiled=True)  42.7 us
    unnamed x18, local copies, waits for them, and re-layouts  6.03 us
    pallas_call x1, Pallas kernels, body(): pl.pallas_call(grads_kernel, out_shape=(jax.ShapeDtypeStruct((NZ, tile, w...  5.39 us
  transfers between devices with their start and end apart: 13, of which 10 were waited for; matrix products, arithmetic and copies ran while one was open for 7% of the time, Pallas kernels for 0%

profile of v5, /device:TPU:57, one launch (start us, length us, event | category | flops | bytes accessed | tf_op | source)
XLA Modules:
  0.0 241.8 jit_solution(17168843951414528815)
XLA Ops:
  10.3 12.6 %all-to-all-start = ((bf16[16,16,768]{2,1,0:T(8,128)(2,1)}), bf16[16,16,768]{2,1,0:T(8,128)(2,1)S(1)}, u32[]{:S(2)}, u32[]{:S(2)}) async-start(bf16[16,16,768]{2,1,0:T(8,128)(2,1)} %bitcast.2), calls=%async_computation | async-start | bytes 786432 | tf_op jit(solution)/shard_map/all_to_all | solution.py:31
  22.9 2.2 collective-permute-start
  27.2 7.9 %all-to-all-done = bf16[16,16,768]{2,1,0:T(8,128)(2,1)S(1)} async-done(((bf16[16,16,768]{2,1,0:T(8,128)(2,1)}), bf16[16,16,768]{2,1,0:T(8,128)(2,1)S(1)}, u32[]{:S(2)}, u32[]{:S(2)}) %all-to-all-start) | async-done | bytes 393248 | tf_op jit(solution)/shard_map/all_to_all | solution.py:31
  36.7 5.0 %all-to-all-start.1 = ((bf16[16,128,512]{2,1,0:T(8,128)(2,1)}), bf16[16,128,512]{2,1,0:T(8,128)(2,1)S(1)}, u32[]{:S(2)}, u32[]{:S(2)}) async-start(bf16[16,128,512]{2,1,0:T(8,128)(2,1)} %broadcast_in_dim.27), calls=%async_computation.1 | async-start | bytes 4194304 | tf_op jit(solution)/shard_map/all_to_all | solution.py:31
  41.7 47.2 %all-to-all-done.1 = bf16[16,128,512]{2,1,0:T(8,128)(2,1)S(1)} async-done(((bf16[16,128,512]{2,1,0:T(8,128)(2,1)}), bf16[16,128,512]{2,1,0:T(8,128)(2,1)S(1)}, u32[]{:S(2)}, u32[]{:S(2)}) %all-to-all-start.1) | async-done | bytes 2097184 | tf_op jit(solution)/shard_map/all_to_all | solution.py:31
  92.9 5.8 %all-to-all-start.2 = ((f32[16,8,256]{2,1,0:T(8,128)}), f32[16,8,256]{2,1,0:T(8,128)S(1)}, u32[]{:S(2)}, u32[]{:S(2)}) async-start(f32[16,8,256]{2,1,0:T(8,128)} %broadcast_in_dim.28), calls=%async_computation.2 | async-start | bytes 262144 | tf_op jit(solution)/shard_map/all_to_all | solution.py:31
  98.8 7.4 %all-to-all-done.2.all_ref = f32[16,8,256]{2,1,0:T(8,128)S(1)} async-done(((f32[16,8,256]{2,1,0:T(8,128)}), f32[16,8,256]{2,1,0:T(8,128)S(1)}, u32[]{:S(2)}, u32[]{:S(2)}) %all-to-all-start.2) | async-done | bytes 131104 | tf_op jit(solution)/shard_map/all_to_all | solution.py:31
  108.1 5.4 %grads.1 = (bf16[8,256,512]{2,1,0:T(8,128)(2,1)S(1)}, bf16[8,16,16,512]{3,2,1,0:T(8,128)(2,1)}, f32[32,256]{1,0:T(8,128)S(1)}) custom-call(bf16[2,8,128,512]{3,2,1,0:T(8,128)(2,1)S(1)} %bitcast.90, bf16[8,16,16,768]{3,2,1,0:T(8,128)(2,1)S(1)} %bitcast.92, f32[16,8,256]{2,1,0:T(8,128)S(1)} %all-to-all-done.2.all_ref, s32[1,256]{1,0:T(1,128)S(1)} %and_select_fusion.3.pos_ref), custom_call_target="tpu_custom_call" | custom-call | tf_op jit(solution)/shard_map/grads/pallas_call | solution.py:286
  115.6 3.5 %all-to-all-start.3 = ((f32[16,32,128]{2,1,0:T(8,128)}), f32[16,32,128]{2,1,0:T(8,128)S(1)}, u32[]{:S(2)}, u32[]{:S(2)}) async-start(f32[16,32,128]{2,1,0:T(8,128)} %bitcast.8), calls=%async_computation.3 | async-start | bytes 524288 | tf_op jit(solution)/shard_map/all_to_all | solution.py:31
  119.9 7.0 %all-to-all-done.3 = f32[16,32,128]{2,1,0:T(8,128)S(1)} async-done(((f32[16,32,128]{2,1,0:T(8,128)}), f32[16,32,128]{2,1,0:T(8,128)S(1)}, u32[]{:S(2)}, u32[]{:S(2)}) %all-to-all-start.3) | async-done | bytes 262176 | tf_op jit(solution)/shard_map/all_to_all | solution.py:31
  127.7 25.0 %all_to_all.50 = f32[64,8,128]{2,1,0:T(8,128)S(1)} all-to-all(f32[64,8,128]{2,1,0:T(8,128)S(1)} %pad_bitcast_fusion), channel_id=1, replica_groups=mesh['rep'=2,'y'=8,'xh'=2,'xl'=2,'z'=8] {'rep','y','xh','xl'}, dimensions={0} | all-to-all | bytes 524288 | tf_op jit(solution)/shard_map/all_to_all | solution.py:31
  152.8 17.7 %all_to_all.51 = f32[64,8,128]{2,1,0:T(8,128)S(1)} all-to-all(f32[64,8,128]{2,1,0:T(8,128)S(1)} %broadcast_in_dim.30), channel_id=1, replica_groups=mesh['rep'=2,'y'=8,'xh'=2,'xl'=2,'z'=8] {'rep','y','xh','xl'}, dimensions={0} | all-to-all | bytes 524288 | tf_op jit(solution)/shard_map/all_to_all | solution.py:31
  172.5 3.7 %all-to-all-start.6 = ((f32[8,64,128]{2,1,0:T(8,128)}), f32[8,64,128]{2,1,0:T(8,128)S(1)}, u32[]{:S(2)}, u32[]{:S(2)}) async-start(f32[8,64,128]{2,1,0:T(8,128)} %broadcast_in_dim.33), calls=%async_computation.7 | async-start | bytes 524288 | tf_op jit(solution)/shard_map/all_to_all | solution.py:31
  177.2 2.6 %collective-permute-start.1 = (bf16[128,512]{1,0:T(8,128)(2,1)S(1)}, bf16[128,512]{1,0:T(8,128)(2,1)S(1)}, u32[]{:S(2)}, u32[]{:S(2)}) collective-permute-start(bf16[128,512]{1,0:T(8,128)(2,1)S(1)} %broadcast_select_fusion), channel_id=1, source_target_pairs={{0,8},{8,0},{1,9},{9,1},{2,10},{10,2},{3,11},{11,3},{4,12},{12,4},... | collective-permute-start | bytes 393224 | tf_op jit(solution)/shard_map/ppermute | solution.py:332
  179.8 4.2 %collective-permute-done.1 = bf16[128,512]{1,0:T(8,128)(2,1)S(1)} collective-permute-done((bf16[128,512]{1,0:T(8,128)(2,1)S(1)}, bf16[128,512]{1,0:T(8,128)(2,1)S(1)}, u32[]{:S(2)}, u32[]{:S(2)}) %collective-permute-start.1) | collective-permute-done | bytes 131104 | tf_op jit(solution)/shard_map/ppermute | solution.py:332
  185.1 3.5 %all-to-all-done.6 = f32[8,64,128]{2,1,0:T(8,128)S(1)} async-done(((f32[8,64,128]{2,1,0:T(8,128)}), f32[8,64,128]{2,1,0:T(8,128)S(1)}, u32[]{:S(2)}, u32[]{:S(2)}) %all-to-all-start.6) | async-done | bytes 262176 | tf_op jit(solution)/shard_map/all_to_all | solution.py:31
  189.8 6.9 %all-to-all-start.7 = ((f32[64,2,128]{2,1,0:T(2,128)}), f32[64,2,128]{2,1,0:T(2,128)S(1)}, u32[]{:S(2)}, u32[]{:S(2)}) async-start(f32[64,2,128]{2,1,0:T(2,128)} %bitcast.21), calls=%async_computation.8 | async-start | bytes 131072 | tf_op jit(solution)/shard_map/all_to_all | solution.py:31
  196.7 2.9 %cholesky.17 = f32[32,32]{1,0:T(8,128)S(1)} custom-call(f32[32,32]{1,0:T(8,128)S(1)} %fusion.38), custom_call_target="Cholesky" | custom-call | tf_op jit(solution)/shard_map/jit(cholesky)/cholesky | solution.py:348
  200.3 3.5 %all-to-all-done.7 = f32[64,2,128]{2,1,0:T(2,128)S(1)} async-done(((f32[64,2,128]{2,1,0:T(2,128)}), f32[64,2,128]{2,1,0:T(2,128)S(1)}, u32[]{:S(2)}, u32[]{:S(2)}) %all-to-all-start.7) | async-done | bytes 65568 | tf_op jit(solution)/shard_map/all_to_all | solution.py:31
  204.6 7.0 %all-to-all-start.8 = ((f32[64,2,128]{2,1,0:T(2,128)}), f32[64,2,128]{2,1,0:T(2,128)S(1)}, u32[]{:S(2)}, u32[]{:S(2)}) async-start(f32[64,2,128]{2,1,0:T(2,128)} %broadcast_in_dim.60), calls=%async_computation.9 | async-start | bytes 131072 | tf_op jit(solution)/shard_map/all_to_all | solution.py:31
  212.2 2.4 %custom-call.6 = f32[1,32,32]{1,2,0:T(8,128)S(1)} custom-call(f32[1,32,32]{2,1,0:T(8,128)S(1)} %fusion.35), custom_call_target="InvertDiagBlocksLowerTriangular" | custom-call | tf_op jit(solution)/shard_map/triangular_solve | solution.py:349
  214.7 4.3 %all-to-all-done.8 = f32[64,2,128]{2,1,0:T(2,128)S(1)} async-done(((f32[64,2,128]{2,1,0:T(2,128)}), f32[64,2,128]{2,1,0:T(2,128)S(1)}, u32[]{:S(2)}, u32[]{:S(2)}) %all-to-all-start.8) | async-done | bytes 65568 | tf_op jit(solution)/shard_map/all_to_all | solution.py:31
  218.9 5.0 %all-to-all-start.9 = ((bf16[16,16,512]{2,1,0:T(8,128)(2,1)}), bf16[16,16,512]{2,1,0:T(8,128)(2,1)S(1)}, u32[]{:S(2)}, u32[]{:S(2)}) async-start(bf16[16,16,512]{2,1,0:T(8,128)(2,1)} %bitcast.103), calls=%async_computation.11 | async-start | bytes 524288 | tf_op jit(solution)/shard_map/all_to_all | solution.py:31
  226.0 8.5 %all-to-all-done.9 = bf16[16,16,512]{2,1,0:T(8,128)(2,1)S(1)} async-done(((bf16[16,16,512]{2,1,0:T(8,128)(2,1)}), bf16[16,16,512]{2,1,0:T(8,128)(2,1)S(1)}, u32[]{:S(2)}, u32[]{:S(2)}) %all-to-all-start.9) | async-done | bytes 262176 | tf_op jit(solution)/shard_map/all_to_all | solution.py:31
  (80 shorter events, 26.4 us)
Async XLA Ops:
  7.2 119.8 %copy-start = (bf16[1,128,1792]{2,1,0:T(8,128)(2,1)S(1)}, bf16[1,128,1792]{2,1,0:T(8,128)(2,1)}, u32[]{:S(2)}) copy-start(bf16[1,128,1792]{2,1,0:T(8,128)(2,1)} %param.8) | copy-start | bytes 1376260
  7.2 15.7 %copy-start.8 = (s32[1,128]{1,0:T(1,128)S(1)}, s32[1,128]{1,0:T(1,128)}, u32[]{:S(2)}) copy-start(s32[1,128]{1,0:T(1,128)} %param.7) | copy-start | bytes 1540
  7.2 27.9 %copy-start.7 = (bf16[1,128,512]{2,1,0:T(8,128)(2,1)S(1)}, bf16[1,128,512]{2,1,0:T(8,128)(2,1)}, u32[]{:S(2)}) copy-start(bf16[1,128,512]{2,1,0:T(8,128)(2,1)} %param.5) | copy-start | bytes 393220
  8.3 0.9 copy-start.4
  10.3 24.8 %all-to-all-start = ((bf16[16,16,768]{2,1,0:T(8,128)(2,1)}), bf16[16,16,768]{2,1,0:T(8,128)(2,1)S(1)}, u32[]{:S(2)}, u32[]{:S(2)}) async-start(bf16[16,16,768]{2,1,0:T(8,128)(2,1)} %bitcast.2), calls=%async_computation | async-start | bytes 786432 | tf_op jit(solution)/shard_map/all_to_all | solution.py:31
  22.9 66.0 %all-gather.3.cloned.1.call-start = ((), (), s32[]{:S(2)}) async-start(), calls=%async_computation.14 | async-start | bytes 3538944 | tf_op jit(solution)/shard_map/all_gather | solution.py:258
  22.9 4.3 %collective-permute-start = (s32[1,128]{1,0:T(1,128)S(1)}, s32[1,128]{1,0:T(1,128)S(1)}, u32[]{:S(2)}, u32[]{:S(2)}) collective-permute-start(s32[1,128]{1,0:T(1,128)S(1)} %copy-done.8), channel_id=1, source_target_pairs={{0,8},{8,0},{1,9},{9,1},{2,10},{10,2},{3,11},{11,3},{4,12},{12,4},... | collective-permute-start | bytes 1544 | tf_op jit(solution)/shard_map/ppermute | solution.py:256
  35.1 1.6 copy-start.6
  36.7 52.2 %all-to-all-start.1 = ((bf16[16,128,512]{2,1,0:T(8,128)(2,1)}), bf16[16,128,512]{2,1,0:T(8,128)(2,1)S(1)}, u32[]{:S(2)}, u32[]{:S(2)}) async-start(bf16[16,128,512]{2,1,0:T(8,128)(2,1)} %broadcast_in_dim.27), calls=%async_computation.1 | async-start | bytes 4194304 | tf_op jit(solution)/shard_map/all_to_all | solution.py:31
  88.9 1.9 copy-start.1
  92.9 13.3 %all-to-all-start.2 = ((f32[16,8,256]{2,1,0:T(8,128)}), f32[16,8,256]{2,1,0:T(8,128)S(1)}, u32[]{:S(2)}, u32[]{:S(2)}) async-start(f32[16,8,256]{2,1,0:T(8,128)} %broadcast_in_dim.28), calls=%async_computation.2 | async-start | bytes 262144 | tf_op jit(solution)/shard_map/all_to_all | solution.py:31
  98.7 73.0 %reduce-scatter.3.cloned.1.call-start = ((), (), s32[]{:S(2)}) async-start(), calls=%async_computation.12 | async-start | bytes 2359296 | tf_op jit(solution)/shard_map/reduce_scatter | solution.py:304
  106.3 1.9 copy-start.2
  113.5 1.3 copy-start.3
  115.6 11.3 %all-to-all-start.3 = ((f32[16,32,128]{2,1,0:T(8,128)}), f32[16,32,128]{2,1,0:T(8,128)S(1)}, u32[]{:S(2)}, u32[]{:S(2)}) async-start(f32[16,32,128]{2,1,0:T(8,128)} %bitcast.8), calls=%async_computation.3 | async-start | bytes 524288 | tf_op jit(solution)/shard_map/all_to_all | solution.py:31
  119.2 95.5 %reduce-scatter.5.cloned.1.call-start = ((), (), s32[]{:S(2)}) async-start(), calls=%async_computation.13 | async-start | bytes 2359296 | tf_op jit(solution)/shard_map/reduce_scatter | solution.py:306
  172.5 16.1 %all-to-all-start.6 = ((f32[8,64,128]{2,1,0:T(8,128)}), f32[8,64,128]{2,1,0:T(8,128)S(1)}, u32[]{:S(2)}, u32[]{:S(2)}) async-start(f32[8,64,128]{2,1,0:T(8,128)} %broadcast_in_dim.33), calls=%async_computation.7 | async-start | bytes 524288 | tf_op jit(solution)/shard_map/all_to_all | solution.py:31
  177.2 6.8 %collective-permute-start.1 = (bf16[128,512]{1,0:T(8,128)(2,1)S(1)}, bf16[128,512]{1,0:T(8,128)(2,1)S(1)}, u32[]{:S(2)}, u32[]{:S(2)}) collective-permute-start(bf16[128,512]{1,0:T(8,128)(2,1)S(1)} %broadcast_select_fusion), channel_id=1, source_target_pairs={{0,8},{8,0},{1,9},{9,1},{2,10},{10,2},{3,11},{11,3},{4,12},{12,4},... | collective-permute-start | bytes 393224 | tf_op jit(solution)/shard_map/ppermute | solution.py:332
  185.1 50.2 %copy-start.5 = (bf16[128,512]{1,0:T(8,128)(2,1)}, bf16[128,512]{1,0:T(8,128)(2,1)S(1)}, u32[]{:S(2)}) copy-start(bf16[128,512]{1,0:T(8,128)(2,1)S(1)} %add_convert_fusion) | copy-start | bytes 393220
  189.8 14.1 %all-to-all-start.7 = ((f32[64,2,128]{2,1,0:T(2,128)}), f32[64,2,128]{2,1,0:T(2,128)S(1)}, u32[]{:S(2)}, u32[]{:S(2)}) async-start(f32[64,2,128]{2,1,0:T(2,128)} %bitcast.21), calls=%async_computation.8 | async-start | bytes 131072 | tf_op jit(solution)/shard_map/all_to_all | solution.py:31
  204.6 14.4 %all-to-all-start.8 = ((f32[64,2,128]{2,1,0:T(2,128)}), f32[64,2,128]{2,1,0:T(2,128)S(1)}, u32[]{:S(2)}, u32[]{:S(2)}) async-start(f32[64,2,128]{2,1,0:T(2,128)} %broadcast_in_dim.60), calls=%async_computation.9 | async-start | bytes 131072 | tf_op jit(solution)/shard_map/all_to_all | solution.py:31
  218.9 15.6 %all-to-all-start.9 = ((bf16[16,16,512]{2,1,0:T(8,128)(2,1)}), bf16[16,16,512]{2,1,0:T(8,128)(2,1)S(1)}, u32[]{:S(2)}, u32[]{:S(2)}) async-start(bf16[16,16,512]{2,1,0:T(8,128)(2,1)} %bitcast.103), calls=%async_computation.11 | async-start | bytes 524288 | tf_op jit(solution)/shard_map/all_to_all | solution.py:31
Sparse Core Ops, SparseCore 0:
  36.8 43.7 all-gather.2
  115.0 40.8 reduce-scatter.2
  158.7 42.1 reduce-scatter.4

commit v6 on v5

--- a/solution.py
+++ b/solution.py
@@ -17,7 +17,6 @@
 bf16 = jnp.bfloat16
 HIGHEST = lax.Precision.HIGHEST
 VMEM = pl.BlockSpec(memory_space=pltpu.VMEM)
-HBM = pl.BlockSpec(memory_space=pltpu.HBM)
 ALL_ROWS = ("rep", "y", "xh", "xl")
 NT = (((1,), (1,)), ((), ()))
 TN = (((0,), (0,)), ((), ()))
@@ -61,29 +60,25 @@
     return jnp.concatenate([q_ref[half, chunk, :, low:high] for half in range(2)], axis=0)
 
 
-def level_scores(q_ref, raw_p_ref, p_ref, sems, finish):
+def passage_rows(p_ref, chunk, low, high):
+    ys, places = p_ref.shape[:2]
+    return jnp.concatenate(
+        [
+            p_ref[y, place, :, low:high]
+            for y in range(ys)
+            for place in (chunk, places // 2 + chunk)
+        ],
+        axis=0,
+    )
+
+
+def level_scores(q_ref, p_ref, finish):
     _, chunks, half_rows, width = q_ref.shape
     full = chunks * width
-    piece = raw_p_ref.shape[2]
     lane = lax.broadcasted_iota(jnp.int32, (2 * half_rows, LANES), 1)
-    moves = []
-    for y in range(raw_p_ref.shape[0]):
-        for half in range(2):
-            moves.append(
-                pltpu.make_async_copy(
-                    raw_p_ref.at[y, pl.ds(half * chunks, chunks), :, pl.ds(0, p_ref.shape[2])],
-                    p_ref.at[:, pl.ds((2 * y + half) * piece, piece)],
-                    sems.at[2 * y + half],
-                )
-            )
-    for move in moves:
-        move.start()
-    for move in moves:
-        move.wait()
-
     def dot(chunk, low, high):
         return lax.dot_general(
-            query_rows(q_ref, chunk, low, high), p_ref[chunk, :, low:high], NT,
+            query_rows(q_ref, chunk, low, high), passage_rows(p_ref, chunk, low, high), NT,
             preferred_element_type=f32,
         )
 
@@ -96,7 +91,9 @@
             q = jnp.where(lane < upper, q, jnp.zeros_like(q))
             finish(
                 level,
-                lax.dot_general(q, p_ref[0, :, :LANES], NT, preferred_element_type=f32),
+                lax.dot_general(
+                    q, passage_rows(p_ref, 0, 0, LANES), NT, preferred_element_type=f32
+                ),
             )
             continue
         if upper == LANES:
@@ -111,7 +108,7 @@
         finish(level, raw)
 
 
-def scores_kernel(q_ref, raw_p_ref, stats_ref, p_ref, table_ref, sems):
+def scores_kernel(q_ref, p_ref, stats_ref, table_ref):
     full = q_ref.shape[1] * q_ref.shape[3]
     lane = lax.broadcasted_iota(jnp.int32, table_ref.shape, 1)
     table_ref[...] = jnp.zeros(table_ref.shape, f32)
@@ -122,17 +119,17 @@
         total = jnp.sum(jnp.exp(logits - top), axis=1, keepdims=True)
         table_ref[...] = jnp.where(lane == level, top + jnp.log(total), table_ref[...])
 
-    level_scores(q_ref, raw_p_ref, p_ref, sems, finish)
+    level_scores(q_ref, p_ref, finish)
     stats_ref[...] = table_ref[...].T[:8]
 
 
 def grads_kernel(
-    q_ref, raw_p_ref, all_ref, pos_ref, gq_ref, gp_ref, sk_ref, p_ref, grad_ref, sems
+    q_ref, p_ref, all_ref, pos_ref, gq_ref, gp_ref, sk_ref, grad_ref
 ):
     _, chunks, half_rows, width = q_ref.shape
     rows = 2 * half_rows
     full = chunks * width
-    cols = p_ref.shape[1]
+    cols = p_ref.shape[0] * 2 * p_ref.shape[2]
     rank = sk_ref.shape[0]
     piece = gp_ref.shape[2]
     peak = all_ref[0]
@@ -151,15 +148,15 @@
         soft = jnp.exp(scale * raw - table[:, level:level + 1])
         grad_ref[level] = scale * jnp.where(column == table[:, 8:9], soft - 1.0, soft)
 
-    level_scores(q_ref, raw_p_ref, p_ref, sems, finish)
+    level_scores(q_ref, p_ref, finish)
     coef = jnp.zeros((rows, cols), f32)
     lane = lax.broadcasted_iota(jnp.int32, (1, LANES), 1)
     sub_lane = lax.broadcasted_iota(jnp.int32, (cols, LANES), 1) // rank
     sketched = jnp.zeros((rows, LANES), f32)
 
     def products(chunk):
-        hi = p_ref[chunk, :, width:width + LANES].astype(f32)
-        return hi + p_ref[chunk, :, width + LANES:].astype(f32)
+        both = passage_rows(p_ref, chunk, width, width + 2 * LANES).astype(f32)
+        return both[:, :LANES] + both[:, LANES:]
 
     def put(chunk, low, high, gq, gp):
         gq_ref[chunk, :, low:high] = gq.astype(bf16)
@@ -170,7 +167,7 @@
             ]
 
     def both(c, chunk, low, high):
-        gq = jnp.dot(c, p_ref[chunk, :, low:high], preferred_element_type=f32)
+        gq = jnp.dot(c, passage_rows(p_ref, chunk, low, high), preferred_element_type=f32)
         gp = lax.dot_general(
             c, query_rows(q_ref, chunk, low, high), TN, preferred_element_type=f32
         )
@@ -252,8 +249,8 @@
         name="pieces",
     )(p, s_subs)
     p_cut = swap(p_cut.reshape(2 * NZ, piece, wide), ("xh", "z"))
+    pos_other = lax.ppermute(positives, "xl", flip)
     q_blocks = jnp.broadcast_to(q[None], (2 * NZ, rows, width))
-    pos_other = lax.ppermute(positives, "xl", flip)
     p_cut, q_blocks, pos_other = lax.optimization_barrier((p_cut, q_blocks, pos_other))
     p_raw = lax.all_gather(p_cut, "y")
 
@@ -266,12 +263,10 @@
     stats = pl.pallas_call(
         scores_kernel,
         out_shape=jax.ShapeDtypeStruct((8, tile), f32),
-        in_specs=[VMEM, HBM],
+        in_specs=[VMEM, VMEM],
         out_specs=VMEM,
         scratch_shapes=[
-            pltpu.VMEM((NZ, tile, width), bf16),
             pltpu.VMEM((tile, LANES), f32),
-            pltpu.SemaphoreType.DMA((2 * NY,)),
         ],
         compiler_params=pltpu.CompilerParams(vmem_limit_bytes=20 << 20),
         name="scores",
@@ -290,12 +285,10 @@
             jax.ShapeDtypeStruct((NY, 2 * NZ, piece, width), bf16),
             jax.ShapeDtypeStruct((rank, tile), f32),
         ),
-        in_specs=[VMEM, HBM, VMEM, VMEM],
+        in_specs=[VMEM] * 4,
         out_specs=(VMEM, VMEM, VMEM),
         scratch_shapes=[
-            pltpu.VMEM((NZ, tile, wide), bf16),
             pltpu.VMEM((LEVELS, tile, tile), f32),
-            pltpu.SemaphoreType.DMA((2 * NY,)),
         ],
         compiler_params=pltpu.CompilerParams(vmem_limit_bytes=28 << 20),
         name="grads",

time: 246 us -> 245 us (level)
  no operation moved by 1% of the time
where the time goes in v6:
time: 245 us; the launch traced here: 241 us
  waiting for transfers between devices  96.4 us (39%)
  starting transfers between devices  54.4 us (22%)
  blocking collectives  42.8 us (17%)
  between operations  14.1 us (6%)
  local copies, waits for them, and re-layouts  12.4 us (5%)
  other arithmetic  9.86 us (4%)
  Pallas kernels  6.73 us (3%)
  matrix products  4.16 us (2%)
    all_to_all x8, waiting for transfers between devices, swap(): return lax.all_to_all(blocks, axes, 0, 0, tiled=True)  89.4 us
    all_to_all x8, starting transfers between devices, swap(): return lax.all_to_all(blocks, axes, 0, 0, tiled=True)  49.4 us
    all_to_all x2, blocking collectives, swap(): return lax.all_to_all(blocks, axes, 0, 0, tiled=True)  42.8 us
    unnamed x18, local copies, waits for them, and re-layouts  6.03 us
  transfers between devices with their start and end apart: 13, of which 10 were waited for; matrix products, arithmetic and copies ran while one was open for 7% of the time, Pallas kernels for 0%

profile of v6, /device:TPU:57, one launch (start us, length us, event | category | flops | bytes accessed | tf_op | source)
XLA Modules:
  0.0 240.8 jit_solution(18313297225044238470)
XLA Ops:
  10.3 12.6 %all-to-all-start = ((bf16[16,16,768]{2,1,0:T(8,128)(2,1)}), bf16[16,16,768]{2,1,0:T(8,128)(2,1)S(1)}, u32[]{:S(2)}, u32[]{:S(2)}) async-start(bf16[16,16,768]{2,1,0:T(8,128)(2,1)} %bitcast.2), calls=%async_computation | async-start | bytes 786432 | tf_op jit(solution)/shard_map/all_to_all | solution.py:30
  22.9 2.2 collective-permute-start
  27.2 7.9 %all-to-all-done = bf16[16,16,768]{2,1,0:T(8,128)(2,1)S(1)} async-done(((bf16[16,16,768]{2,1,0:T(8,128)(2,1)}), bf16[16,16,768]{2,1,0:T(8,128)(2,1)S(1)}, u32[]{:S(2)}, u32[]{:S(2)}) %all-to-all-start) | async-done | bytes 393248 | tf_op jit(solution)/shard_map/all_to_all | solution.py:30
  36.7 5.0 %all-to-all-start.1 = ((bf16[16,128,512]{2,1,0:T(8,128)(2,1)}), bf16[16,128,512]{2,1,0:T(8,128)(2,1)S(1)}, u32[]{:S(2)}, u32[]{:S(2)}) async-start(bf16[16,128,512]{2,1,0:T(8,128)(2,1)} %broadcast_in_dim.27), calls=%async_computation.1 | async-start | bytes 4194304 | tf_op jit(solution)/shard_map/all_to_all | solution.py:30
  41.7 47.2 %all-to-all-done.1 = bf16[16,128,512]{2,1,0:T(8,128)(2,1)S(1)} async-done(((bf16[16,128,512]{2,1,0:T(8,128)(2,1)}), bf16[16,128,512]{2,1,0:T(8,128)(2,1)S(1)}, u32[]{:S(2)}, u32[]{:S(2)}) %all-to-all-start.1) | async-done | bytes 2097184 | tf_op jit(solution)/shard_map/all_to_all | solution.py:30
  92.6 5.8 %all-to-all-start.2 = ((f32[16,8,256]{2,1,0:T(8,128)}), f32[16,8,256]{2,1,0:T(8,128)S(1)}, u32[]{:S(2)}, u32[]{:S(2)}) async-start(f32[16,8,256]{2,1,0:T(8,128)} %broadcast_in_dim.28), calls=%async_computation.2 | async-start | bytes 262144 | tf_op jit(solution)/shard_map/all_to_all | solution.py:30
  98.5 7.4 %all-to-all-done.2.all_ref = f32[16,8,256]{2,1,0:T(8,128)S(1)} async-done(((f32[16,8,256]{2,1,0:T(8,128)}), f32[16,8,256]{2,1,0:T(8,128)S(1)}, u32[]{:S(2)}, u32[]{:S(2)}) %all-to-all-start.2) | async-done | bytes 131104 | tf_op jit(solution)/shard_map/all_to_all | solution.py:30
  107.8 4.6 %grads.1 = (bf16[8,256,512]{2,1,0:T(8,128)(2,1)S(1)}, bf16[8,16,16,512]{3,2,1,0:T(8,128)(2,1)}, f32[32,256]{1,0:T(8,128)S(1)}) custom-call(bf16[2,8,128,512]{3,2,1,0:T(8,128)(2,1)S(1)} %bitcast.90, bf16[8,16,16,768]{3,2,1,0:T(8,128)(2,1)S(1)} %bitcast.92, f32[16,8,256]{2,1,0:T(8,128)S(1)} %all-to-all-done.2.all_ref, s32[1,256]{1,0:T(1,128)S(1)} %and_select_fusion.3.pos_ref), custom_call_target="tpu_custom_call" | custom-call | tf_op jit(solution)/shard_map/grads/pallas_call | solution.py:281
  114.5 3.5 %all-to-all-start.3 = ((f32[16,32,128]{2,1,0:T(8,128)}), f32[16,32,128]{2,1,0:T(8,128)S(1)}, u32[]{:S(2)}, u32[]{:S(2)}) async-start(f32[16,32,128]{2,1,0:T(8,128)} %bitcast.8), calls=%async_computation.3 | async-start | bytes 524288 | tf_op jit(solution)/shard_map/all_to_all | solution.py:30
  118.8 7.0 %all-to-all-done.3 = f32[16,32,128]{2,1,0:T(8,128)S(1)} async-done(((f32[16,32,128]{2,1,0:T(8,128)}), f32[16,32,128]{2,1,0:T(8,128)S(1)}, u32[]{:S(2)}, u32[]{:S(2)}) %all-to-all-start.3) | async-done | bytes 262176 | tf_op jit(solution)/shard_map/all_to_all | solution.py:30
  126.6 25.1 %all_to_all.50 = f32[64,8,128]{2,1,0:T(8,128)S(1)} all-to-all(f32[64,8,128]{2,1,0:T(8,128)S(1)} %pad_bitcast_fusion), channel_id=1, replica_groups=mesh['rep'=2,'y'=8,'xh'=2,'xl'=2,'z'=8] {'rep','y','xh','xl'}, dimensions={0} | all-to-all | bytes 524288 | tf_op jit(solution)/shard_map/all_to_all | solution.py:30
  151.8 17.7 %all_to_all.51 = f32[64,8,128]{2,1,0:T(8,128)S(1)} all-to-all(f32[64,8,128]{2,1,0:T(8,128)S(1)} %broadcast_in_dim.30), channel_id=1, replica_groups=mesh['rep'=2,'y'=8,'xh'=2,'xl'=2,'z'=8] {'rep','y','xh','xl'}, dimensions={0} | all-to-all | bytes 524288 | tf_op jit(solution)/shard_map/all_to_all | solution.py:30
  171.5 3.7 %all-to-all-start.6 = ((f32[8,64,128]{2,1,0:T(8,128)}), f32[8,64,128]{2,1,0:T(8,128)S(1)}, u32[]{:S(2)}, u32[]{:S(2)}) async-start(f32[8,64,128]{2,1,0:T(8,128)} %broadcast_in_dim.33), calls=%async_computation.7 | async-start | bytes 524288 | tf_op jit(solution)/shard_map/all_to_all | solution.py:30
  176.2 2.6 %collective-permute-start.1 = (bf16[128,512]{1,0:T(8,128)(2,1)S(1)}, bf16[128,512]{1,0:T(8,128)(2,1)S(1)}, u32[]{:S(2)}, u32[]{:S(2)}) collective-permute-start(bf16[128,512]{1,0:T(8,128)(2,1)S(1)} %broadcast_select_fusion), channel_id=1, source_target_pairs={{0,8},{8,0},{1,9},{9,1},{2,10},{10,2},{3,11},{11,3},{4,12},{12,4},... | collective-permute-start | bytes 393224 | tf_op jit(solution)/shard_map/ppermute | solution.py:325
  178.8 4.2 %collective-permute-done.1 = bf16[128,512]{1,0:T(8,128)(2,1)S(1)} collective-permute-done((bf16[128,512]{1,0:T(8,128)(2,1)S(1)}, bf16[128,512]{1,0:T(8,128)(2,1)S(1)}, u32[]{:S(2)}, u32[]{:S(2)}) %collective-permute-start.1) | collective-permute-done | bytes 131104 | tf_op jit(solution)/shard_map/ppermute | solution.py:325
  184.1 3.5 %all-to-all-done.6 = f32[8,64,128]{2,1,0:T(8,128)S(1)} async-done(((f32[8,64,128]{2,1,0:T(8,128)}), f32[8,64,128]{2,1,0:T(8,128)S(1)}, u32[]{:S(2)}, u32[]{:S(2)}) %all-to-all-start.6) | async-done | bytes 262176 | tf_op jit(solution)/shard_map/all_to_all | solution.py:30
  188.8 6.8 %all-to-all-start.7 = ((f32[64,2,128]{2,1,0:T(2,128)}), f32[64,2,128]{2,1,0:T(2,128)S(1)}, u32[]{:S(2)}, u32[]{:S(2)}) async-start(f32[64,2,128]{2,1,0:T(2,128)} %bitcast.21), calls=%async_computation.8 | async-start | bytes 131072 | tf_op jit(solution)/shard_map/all_to_all | solution.py:30
  195.7 2.9 %cholesky.17 = f32[32,32]{1,0:T(8,128)S(1)} custom-call(f32[32,32]{1,0:T(8,128)S(1)} %fusion.38), custom_call_target="Cholesky" | custom-call | tf_op jit(solution)/shard_map/jit(cholesky)/cholesky | solution.py:341
  199.3 3.6 %all-to-all-done.7 = f32[64,2,128]{2,1,0:T(2,128)S(1)} async-done(((f32[64,2,128]{2,1,0:T(2,128)}), f32[64,2,128]{2,1,0:T(2,128)S(1)}, u32[]{:S(2)}, u32[]{:S(2)}) %all-to-all-start.7) | async-done | bytes 65568 | tf_op jit(solution)/shard_map/all_to_all | solution.py:30
  203.7 7.0 %all-to-all-start.8 = ((f32[64,2,128]{2,1,0:T(2,128)}), f32[64,2,128]{2,1,0:T(2,128)S(1)}, u32[]{:S(2)}, u32[]{:S(2)}) async-start(f32[64,2,128]{2,1,0:T(2,128)} %broadcast_in_dim.60), calls=%async_computation.9 | async-start | bytes 131072 | tf_op jit(solution)/shard_map/all_to_all | solution.py:30
  211.3 2.4 %custom-call.6 = f32[1,32,32]{1,2,0:T(8,128)S(1)} custom-call(f32[1,32,32]{2,1,0:T(8,128)S(1)} %fusion.35), custom_call_target="InvertDiagBlocksLowerTriangular" | custom-call | tf_op jit(solution)/shard_map/triangular_solve | solution.py:342
  213.8 4.3 %all-to-all-done.8 = f32[64,2,128]{2,1,0:T(2,128)S(1)} async-done(((f32[64,2,128]{2,1,0:T(2,128)}), f32[64,2,128]{2,1,0:T(2,128)S(1)}, u32[]{:S(2)}, u32[]{:S(2)}) %all-to-all-start.8) | async-done | bytes 65568 | tf_op jit(solution)/shard_map/all_to_all | solution.py:30
  218.0 4.9 %all-to-all-start.9 = ((bf16[16,16,512]{2,1,0:T(8,128)(2,1)}), bf16[16,16,512]{2,1,0:T(8,128)(2,1)S(1)}, u32[]{:S(2)}, u32[]{:S(2)}) async-start(bf16[16,16,512]{2,1,0:T(8,128)(2,1)} %bitcast.103), calls=%async_computation.11 | async-start | bytes 524288 | tf_op jit(solution)/shard_map/all_to_all | solution.py:30
  225.0 8.5 %all-to-all-done.9 = bf16[16,16,512]{2,1,0:T(8,128)(2,1)S(1)} async-done(((bf16[16,16,512]{2,1,0:T(8,128)(2,1)}), bf16[16,16,512]{2,1,0:T(8,128)(2,1)S(1)}, u32[]{:S(2)}, u32[]{:S(2)}) %all-to-all-start.9) | async-done | bytes 262176 | tf_op jit(solution)/shard_map/all_to_all | solution.py:30
  (80 shorter events, 26.1 us)
Async XLA Ops:
  7.2 118.7 %copy-start = (bf16[1,128,1792]{2,1,0:T(8,128)(2,1)S(1)}, bf16[1,128,1792]{2,1,0:T(8,128)(2,1)}, u32[]{:S(2)}) copy-start(bf16[1,128,1792]{2,1,0:T(8,128)(2,1)} %param.8) | copy-start | bytes 1376260
  7.2 15.7 %copy-start.8 = (s32[1,128]{1,0:T(1,128)S(1)}, s32[1,128]{1,0:T(1,128)}, u32[]{:S(2)}) copy-start(s32[1,128]{1,0:T(1,128)} %param.7) | copy-start | bytes 1540
  7.2 27.9 %copy-start.7 = (bf16[1,128,512]{2,1,0:T(8,128)(2,1)S(1)}, bf16[1,128,512]{2,1,0:T(8,128)(2,1)}, u32[]{:S(2)}) copy-start(bf16[1,128,512]{2,1,0:T(8,128)(2,1)} %param.5) | copy-start | bytes 393220
  8.3 0.9 copy-start.4
  10.3 24.8 %all-to-all-start = ((bf16[16,16,768]{2,1,0:T(8,128)(2,1)}), bf16[16,16,768]{2,1,0:T(8,128)(2,1)S(1)}, u32[]{:S(2)}, u32[]{:S(2)}) async-start(bf16[16,16,768]{2,1,0:T(8,128)(2,1)} %bitcast.2), calls=%async_computation | async-start | bytes 786432 | tf_op jit(solution)/shard_map/all_to_all | solution.py:30
  22.9 66.0 %all-gather.3.cloned.1.call-start = ((), (), s32[]{:S(2)}) async-start(), calls=%async_computation.14 | async-start | bytes 3538944 | tf_op jit(solution)/shard_map/all_gather | solution.py:255
  22.9 4.3 %collective-permute-start = (s32[1,128]{1,0:T(1,128)S(1)}, s32[1,128]{1,0:T(1,128)S(1)}, u32[]{:S(2)}, u32[]{:S(2)}) collective-permute-start(s32[1,128]{1,0:T(1,128)S(1)} %copy-done.8), channel_id=1, source_target_pairs={{0,8},{8,0},{1,9},{9,1},{2,10},{10,2},{3,11},{11,3},{4,12},{12,4},... | collective-permute-start | bytes 1544 | tf_op jit(solution)/shard_map/ppermute | solution.py:252
  35.1 1.6 copy-start.6
  36.7 52.2 %all-to-all-start.1 = ((bf16[16,128,512]{2,1,0:T(8,128)(2,1)}), bf16[16,128,512]{2,1,0:T(8,128)(2,1)S(1)}, u32[]{:S(2)}, u32[]{:S(2)}) async-start(bf16[16,128,512]{2,1,0:T(8,128)(2,1)} %broadcast_in_dim.27), calls=%async_computation.1 | async-start | bytes 4194304 | tf_op jit(solution)/shard_map/all_to_all | solution.py:30
  88.9 1.9 copy-start.1
  92.6 13.3 %all-to-all-start.2 = ((f32[16,8,256]{2,1,0:T(8,128)}), f32[16,8,256]{2,1,0:T(8,128)S(1)}, u32[]{:S(2)}, u32[]{:S(2)}) async-start(f32[16,8,256]{2,1,0:T(8,128)} %broadcast_in_dim.28), calls=%async_computation.2 | async-start | bytes 262144 | tf_op jit(solution)/shard_map/all_to_all | solution.py:30
  98.4 72.4 %reduce-scatter.3.cloned.1.call-start = ((), (), s32[]{:S(2)}) async-start(), calls=%async_computation.12 | async-start | bytes 2359296 | tf_op jit(solution)/shard_map/reduce_scatter | solution.py:297
  105.9 1.9 copy-start.2
  112.4 1.3 copy-start.3
  114.5 11.3 %all-to-all-start.3 = ((f32[16,32,128]{2,1,0:T(8,128)}), f32[16,32,128]{2,1,0:T(8,128)S(1)}, u32[]{:S(2)}, u32[]{:S(2)}) async-start(f32[16,32,128]{2,1,0:T(8,128)} %bitcast.8), calls=%async_computation.3 | async-start | bytes 524288 | tf_op jit(solution)/shard_map/all_to_all | solution.py:30
  118.1 95.7 %reduce-scatter.5.cloned.1.call-start = ((), (), s32[]{:S(2)}) async-start(), calls=%async_computation.13 | async-start | bytes 2359296 | tf_op jit(solution)/shard_map/reduce_scatter | solution.py:299
  171.5 16.1 %all-to-all-start.6 = ((f32[8,64,128]{2,1,0:T(8,128)}), f32[8,64,128]{2,1,0:T(8,128)S(1)}, u32[]{:S(2)}, u32[]{:S(2)}) async-start(f32[8,64,128]{2,1,0:T(8,128)} %broadcast_in_dim.33), calls=%async_computation.7 | async-start | bytes 524288 | tf_op jit(solution)/shard_map/all_to_all | solution.py:30
  176.2 6.8 %collective-permute-start.1 = (bf16[128,512]{1,0:T(8,128)(2,1)S(1)}, bf16[128,512]{1,0:T(8,128)(2,1)S(1)}, u32[]{:S(2)}, u32[]{:S(2)}) collective-permute-start(bf16[128,512]{1,0:T(8,128)(2,1)S(1)} %broadcast_select_fusion), channel_id=1, source_target_pairs={{0,8},{8,0},{1,9},{9,1},{2,10},{10,2},{3,11},{11,3},{4,12},{12,4},... | collective-permute-start | bytes 393224 | tf_op jit(solution)/shard_map/ppermute | solution.py:325
  184.0 50.2 %copy-start.5 = (bf16[128,512]{1,0:T(8,128)(2,1)}, bf16[128,512]{1,0:T(8,128)(2,1)S(1)}, u32[]{:S(2)}) copy-start(bf16[128,512]{1,0:T(8,128)(2,1)S(1)} %add_convert_fusion) | copy-start | bytes 393220
  188.8 14.2 %all-to-all-start.7 = ((f32[64,2,128]{2,1,0:T(2,128)}), f32[64,2,128]{2,1,0:T(2,128)S(1)}, u32[]{:S(2)}, u32[]{:S(2)}) async-start(f32[64,2,128]{2,1,0:T(2,128)} %bitcast.21), calls=%async_computation.8 | async-start | bytes 131072 | tf_op jit(solution)/shard_map/all_to_all | solution.py:30
  203.7 14.4 %all-to-all-start.8 = ((f32[64,2,128]{2,1,0:T(2,128)}), f32[64,2,128]{2,1,0:T(2,128)S(1)}, u32[]{:S(2)}, u32[]{:S(2)}) async-start(f32[64,2,128]{2,1,0:T(2,128)} %broadcast_in_dim.60), calls=%async_computation.9 | async-start | bytes 131072 | tf_op jit(solution)/shard_map/all_to_all | solution.py:30
  218.0 15.5 %all-to-all-start.9 = ((bf16[16,16,512]{2,1,0:T(8,128)(2,1)}), bf16[16,16,512]{2,1,0:T(8,128)(2,1)S(1)}, u32[]{:S(2)}, u32[]{:S(2)}) async-start(bf16[16,16,512]{2,1,0:T(8,128)(2,1)} %bitcast.103), calls=%async_computation.11 | async-start | bytes 524288 | tf_op jit(solution)/shard_map/all_to_all | solution.py:30
Sparse Core Ops, SparseCore 0:
  36.8 43.7 all-gather.2
  113.9 40.6 reduce-scatter.2
  157.4 42.7 reduce-scatter.4

commit v7 on v6

--- a/solution.py
+++ b/solution.py
@@ -208,9 +208,10 @@
 
 
 def exact_dot(wide, narrow, dims):
-    hi, mid, lo = [
-        lax.dot_general(t, narrow, dims, preferred_element_type=f32) for t in three_terms(wide)
-    ]
+    rows = wide.shape[0]
+    terms = jnp.concatenate(three_terms(wide), axis=0)
+    out = lax.dot_general(terms, narrow, dims, preferred_element_type=f32)
+    hi, mid, lo = out[:rows], out[rows:2 * rows], out[2 * rows:]
     return (lo + mid) + hi
 
 
@@ -268,7 +269,7 @@
         scratch_shapes=[
             pltpu.VMEM((tile, LANES), f32),
         ],
-        compiler_params=pltpu.CompilerParams(vmem_limit_bytes=20 << 20),
+        compiler_params=pltpu.CompilerParams(vmem_limit_bytes=10 << 20),
         name="scores",
     )(q_tile, p_raw)
     stats_all = share(stats, ("xl", "z"), 2 * NZ)
@@ -290,7 +291,7 @@
         scratch_shapes=[
             pltpu.VMEM((LEVELS, tile, tile), f32),
         ],
-        compiler_params=pltpu.CompilerParams(vmem_limit_bytes=28 << 20),
+        compiler_params=pltpu.CompilerParams(vmem_limit_bytes=14 << 20),
         name="grads",
     )(q_tile, p_raw, stats_all, local)
 

time: 245 us -> 244 us (level)
  transfers between devices with their start and end apart: 13 -> 13, of which waited for: 10 -> 10; matrix products, arithmetic and copies ran while one was open for 7% -> 6% of each run, Pallas kernels for 0% -> 0%
where the time goes in v7:
time: 244 us; the launch traced here: 240 us
  waiting for transfers between devices  97.2 us (40%)
  starting transfers between devices  53.5 us (22%)
  blocking collectives  42.8 us (18%)
  between operations  14.1 us (6%)
  local copies, waits for them, and re-layouts  11.7 us (5%)
  other arithmetic  10.5 us (4%)
  Pallas kernels  6.71 us (3%)
  matrix products  3 us (1%)
    all_to_all x8, waiting for transfers between devices, swap(): return lax.all_to_all(blocks, axes, 0, 0, tiled=True)  90.1 us
    all_to_all x8, starting transfers between devices, swap(): return lax.all_to_all(blocks, axes, 0, 0, tiled=True)  48.6 us
    all_to_all x2, blocking collectives, swap(): return lax.all_to_all(blocks, axes, 0, 0, tiled=True)  42.8 us
    unnamed x18, local copies, waits for them, and re-layouts  6.02 us
  transfers between devices with their start and end apart: 13, of which 10 were waited for; matrix products, arithmetic and copies ran while one was open for 6% of the time, Pallas kernels for 0%

profile of v7, /device:TPU:57, one launch (start us, length us, event | category | flops | bytes accessed | tf_op | source)
XLA Modules:
  0.0 239.6 jit_solution(3485590066294782430)
XLA Ops:
  10.3 12.6 %all-to-all-start = ((bf16[16,16,768]{2,1,0:T(8,128)(2,1)}), bf16[16,16,768]{2,1,0:T(8,128)(2,1)S(1)}, u32[]{:S(2)}, u32[]{:S(2)}) async-start(bf16[16,16,768]{2,1,0:T(8,128)(2,1)} %bitcast.2), calls=%async_computation | async-start | bytes 786432 | tf_op jit(solution)/shard_map/all_to_all | solution.py:30
  22.9 2.2 collective-permute-start
  27.2 7.9 %all-to-all-done = bf16[16,16,768]{2,1,0:T(8,128)(2,1)S(1)} async-done(((bf16[16,16,768]{2,1,0:T(8,128)(2,1)}), bf16[16,16,768]{2,1,0:T(8,128)(2,1)S(1)}, u32[]{:S(2)}, u32[]{:S(2)}) %all-to-all-start) | async-done | bytes 393248 | tf_op jit(solution)/shard_map/all_to_all | solution.py:30
  36.7 5.0 %all-to-all-start.1 = ((bf16[16,128,512]{2,1,0:T(8,128)(2,1)}), bf16[16,128,512]{2,1,0:T(8,128)(2,1)S(1)}, u32[]{:S(2)}, u32[]{:S(2)}) async-start(bf16[16,128,512]{2,1,0:T(8,128)(2,1)} %broadcast_in_dim.27), calls=%async_computation.1 | async-start | bytes 4194304 | tf_op jit(solution)/shard_map/all_to_all | solution.py:30
  41.7 47.2 %all-to-all-done.1 = bf16[16,128,512]{2,1,0:T(8,128)(2,1)S(1)} async-done(((bf16[16,128,512]{2,1,0:T(8,128)(2,1)}), bf16[16,128,512]{2,1,0:T(8,128)(2,1)S(1)}, u32[]{:S(2)}, u32[]{:S(2)}) %all-to-all-start.1) | async-done | bytes 2097184 | tf_op jit(solution)/shard_map/all_to_all | solution.py:30
  92.6 5.8 %all-to-all-start.2 = ((f32[16,8,256]{2,1,0:T(8,128)}), f32[16,8,256]{2,1,0:T(8,128)S(1)}, u32[]{:S(2)}, u32[]{:S(2)}) async-start(f32[16,8,256]{2,1,0:T(8,128)} %broadcast_in_dim.28), calls=%async_computation.2 | async-start | bytes 262144 | tf_op jit(solution)/shard_map/all_to_all | solution.py:30
  98.5 7.4 %all-to-all-done.2.all_ref = f32[16,8,256]{2,1,0:T(8,128)S(1)} async-done(((f32[16,8,256]{2,1,0:T(8,128)}), f32[16,8,256]{2,1,0:T(8,128)S(1)}, u32[]{:S(2)}, u32[]{:S(2)}) %all-to-all-start.2) | async-done | bytes 131104 | tf_op jit(solution)/shard_map/all_to_all | solution.py:30
  107.8 4.6 %grads.1 = (bf16[8,256,512]{2,1,0:T(8,128)(2,1)S(1)}, bf16[8,16,16,512]{3,2,1,0:T(8,128)(2,1)}, f32[32,256]{1,0:T(8,128)S(1)}) custom-call(bf16[2,8,128,512]{3,2,1,0:T(8,128)(2,1)S(1)} %bitcast.78, bf16[8,16,16,768]{3,2,1,0:T(8,128)(2,1)S(1)} %bitcast.80, f32[16,8,256]{2,1,0:T(8,128)S(1)} %all-to-all-done.2.all_ref, s32[1,256]{1,0:T(1,128)S(1)} %and_select_fusion.3.pos_ref), custom_call_target="tpu_custom_call" | custom-call | tf_op jit(solution)/shard_map/grads/pallas_call | solution.py:282
  114.5 3.5 %all-to-all-start.3 = ((f32[16,32,128]{2,1,0:T(8,128)}), f32[16,32,128]{2,1,0:T(8,128)S(1)}, u32[]{:S(2)}, u32[]{:S(2)}) async-start(f32[16,32,128]{2,1,0:T(8,128)} %bitcast.8), calls=%async_computation.3 | async-start | bytes 524288 | tf_op jit(solution)/shard_map/all_to_all | solution.py:30
  118.8 7.0 %all-to-all-done.3 = f32[16,32,128]{2,1,0:T(8,128)S(1)} async-done(((f32[16,32,128]{2,1,0:T(8,128)}), f32[16,32,128]{2,1,0:T(8,128)S(1)}, u32[]{:S(2)}, u32[]{:S(2)}) %all-to-all-start.3) | async-done | bytes 262176 | tf_op jit(solution)/shard_map/all_to_all | solution.py:30
  126.3 25.1 %all_to_all.50 = f32[64,8,128]{2,1,0:T(8,128)S(1)} all-to-all(f32[64,8,128]{2,1,0:T(8,128)S(1)} %pad_bitcast_fusion), channel_id=1, replica_groups=mesh['rep'=2,'y'=8,'xh'=2,'xl'=2,'z'=8] {'rep','y','xh','xl'}, dimensions={0} | all-to-all | bytes 524288 | tf_op jit(solution)/shard_map/all_to_all | solution.py:30
  151.5 17.7 %all_to_all.51 = f32[64,8,128]{2,1,0:T(8,128)S(1)} all-to-all(f32[64,8,128]{2,1,0:T(8,128)S(1)} %broadcast_in_dim.30), channel_id=1, replica_groups=mesh['rep'=2,'y'=8,'xh'=2,'xl'=2,'z'=8] {'rep','y','xh','xl'}, dimensions={0} | all-to-all | bytes 524288 | tf_op jit(solution)/shard_map/all_to_all | solution.py:30
  170.6 3.7 %all-to-all-start.6 = ((f32[8,64,128]{2,1,0:T(8,128)}), f32[8,64,128]{2,1,0:T(8,128)S(1)}, u32[]{:S(2)}, u32[]{:S(2)}) async-start(f32[8,64,128]{2,1,0:T(8,128)} %broadcast_in_dim.33), calls=%async_computation.7 | async-start | bytes 524288 | tf_op jit(solution)/shard_map/all_to_all | solution.py:30
  175.3 2.6 %collective-permute-start.1 = (bf16[128,512]{1,0:T(8,128)(2,1)S(1)}, bf16[128,512]{1,0:T(8,128)(2,1)S(1)}, u32[]{:S(2)}, u32[]{:S(2)}) collective-permute-start(bf16[128,512]{1,0:T(8,128)(2,1)S(1)} %broadcast_select_fusion), channel_id=1, source_target_pairs={{0,8},{8,0},{1,9},{9,1},{2,10},{10,2},{3,11},{11,3},{4,12},{12,4},... | collective-permute-start | bytes 393224 | tf_op jit(solution)/shard_map/ppermute | solution.py:326
  178.0 4.3 %collective-permute-done.1 = bf16[128,512]{1,0:T(8,128)(2,1)S(1)} collective-permute-done((bf16[128,512]{1,0:T(8,128)(2,1)S(1)}, bf16[128,512]{1,0:T(8,128)(2,1)S(1)}, u32[]{:S(2)}, u32[]{:S(2)}) %collective-permute-start.1) | collective-permute-done | bytes 131104 | tf_op jit(solution)/shard_map/ppermute | solution.py:326
  183.3 3.4 %all-to-all-done.6 = f32[8,64,128]{2,1,0:T(8,128)S(1)} async-done(((f32[8,64,128]{2,1,0:T(8,128)}), f32[8,64,128]{2,1,0:T(8,128)S(1)}, u32[]{:S(2)}, u32[]{:S(2)}) %all-to-all-start.6) | async-done | bytes 262176 | tf_op jit(solution)/shard_map/all_to_all | solution.py:30
  187.7 6.8 %all-to-all-start.7 = ((f32[64,2,128]{2,1,0:T(2,128)}), f32[64,2,128]{2,1,0:T(2,128)S(1)}, u32[]{:S(2)}, u32[]{:S(2)}) async-start(f32[64,2,128]{2,1,0:T(2,128)} %bitcast.21), calls=%async_computation.8 | async-start | bytes 131072 | tf_op jit(solution)/shard_map/all_to_all | solution.py:30
  194.6 2.9 %cholesky.17 = f32[32,32]{1,0:T(8,128)S(1)} custom-call(f32[32,32]{1,0:T(8,128)S(1)} %fusion.41), custom_call_target="Cholesky" | custom-call | tf_op jit(solution)/shard_map/jit(cholesky)/cholesky | solution.py:342
  198.2 4.3 %all-to-all-done.7 = f32[64,2,128]{2,1,0:T(2,128)S(1)} async-done(((f32[64,2,128]{2,1,0:T(2,128)}), f32[64,2,128]{2,1,0:T(2,128)S(1)}, u32[]{:S(2)}, u32[]{:S(2)}) %all-to-all-start.7) | async-done | bytes 65568 | tf_op jit(solution)/shard_map/all_to_all | solution.py:30
  203.3 6.4 %all-to-all-start.8 = ((f32[64,2,128]{2,1,0:T(2,128)}), f32[64,2,128]{2,1,0:T(2,128)S(1)}, u32[]{:S(2)}, u32[]{:S(2)}) async-start(f32[64,2,128]{2,1,0:T(2,128)} %broadcast_in_dim.60), calls=%async_computation.9 | async-start | bytes 131072 | tf_op jit(solution)/shard_map/all_to_all | solution.py:30
  210.4 2.4 %custom-call.6 = f32[1,32,32]{1,2,0:T(8,128)S(1)} custom-call(f32[1,32,32]{2,1,0:T(8,128)S(1)} %fusion.38), custom_call_target="InvertDiagBlocksLowerTriangular" | custom-call | tf_op jit(solution)/shard_map/triangular_solve | solution.py:343
  212.8 4.3 %all-to-all-done.8 = f32[64,2,128]{2,1,0:T(2,128)S(1)} async-done(((f32[64,2,128]{2,1,0:T(2,128)}), f32[64,2,128]{2,1,0:T(2,128)S(1)}, u32[]{:S(2)}, u32[]{:S(2)}) %all-to-all-start.8) | async-done | bytes 65568 | tf_op jit(solution)/shard_map/all_to_all | solution.py:30
  217.1 4.6 %all-to-all-start.9 = ((bf16[16,16,512]{2,1,0:T(8,128)(2,1)}), bf16[16,16,512]{2,1,0:T(8,128)(2,1)S(1)}, u32[]{:S(2)}, u32[]{:S(2)}) async-start(bf16[16,16,512]{2,1,0:T(8,128)(2,1)} %bitcast.92), calls=%async_computation.11 | async-start | bytes 524288 | tf_op jit(solution)/shard_map/all_to_all | solution.py:30
  223.7 8.6 %all-to-all-done.9 = bf16[16,16,512]{2,1,0:T(8,128)(2,1)S(1)} async-done(((bf16[16,16,512]{2,1,0:T(8,128)(2,1)}), bf16[16,16,512]{2,1,0:T(8,128)(2,1)S(1)}, u32[]{:S(2)}, u32[]{:S(2)}) %all-to-all-start.9) | async-done | bytes 262176 | tf_op jit(solution)/shard_map/all_to_all | solution.py:30
  (79 shorter events, 24.9 us)
Async XLA Ops:
  7.2 118.7 %copy-start = (bf16[1,128,1792]{2,1,0:T(8,128)(2,1)S(1)}, bf16[1,128,1792]{2,1,0:T(8,128)(2,1)}, u32[]{:S(2)}) copy-start(bf16[1,128,1792]{2,1,0:T(8,128)(2,1)} %param.8) | copy-start | bytes 1376260
  7.2 15.7 %copy-start.8 = (s32[1,128]{1,0:T(1,128)S(1)}, s32[1,128]{1,0:T(1,128)}, u32[]{:S(2)}) copy-start(s32[1,128]{1,0:T(1,128)} %param.7) | copy-start | bytes 1540
  7.2 27.9 %copy-start.7 = (bf16[1,128,512]{2,1,0:T(8,128)(2,1)S(1)}, bf16[1,128,512]{2,1,0:T(8,128)(2,1)}, u32[]{:S(2)}) copy-start(bf16[1,128,512]{2,1,0:T(8,128)(2,1)} %param.5) | copy-start | bytes 393220
  8.3 0.9 copy-start.4
  10.3 24.8 %all-to-all-start = ((bf16[16,16,768]{2,1,0:T(8,128)(2,1)}), bf16[16,16,768]{2,1,0:T(8,128)(2,1)S(1)}, u32[]{:S(2)}, u32[]{:S(2)}) async-start(bf16[16,16,768]{2,1,0:T(8,128)(2,1)} %bitcast.2), calls=%async_computation | async-start | bytes 786432 | tf_op jit(solution)/shard_map/all_to_all | solution.py:30
  22.9 66.0 %all-gather.3.cloned.1.call-start = ((), (), s32[]{:S(2)}) async-start(), calls=%async_computation.14 | async-start | bytes 3538944 | tf_op jit(solution)/shard_map/all_gather | solution.py:256
  22.9 4.3 %collective-permute-start = (s32[1,128]{1,0:T(1,128)S(1)}, s32[1,128]{1,0:T(1,128)S(1)}, u32[]{:S(2)}, u32[]{:S(2)}) collective-permute-start(s32[1,128]{1,0:T(1,128)S(1)} %copy-done.8), channel_id=1, source_target_pairs={{0,8},{8,0},{1,9},{9,1},{2,10},{10,2},{3,11},{11,3},{4,12},{12,4},... | collective-permute-start | bytes 1544 | tf_op jit(solution)/shard_map/ppermute | solution.py:253
  35.1 1.6 copy-start.5
  36.7 52.2 %all-to-all-start.1 = ((bf16[16,128,512]{2,1,0:T(8,128)(2,1)}), bf16[16,128,512]{2,1,0:T(8,128)(2,1)S(1)}, u32[]{:S(2)}, u32[]{:S(2)}) async-start(bf16[16,128,512]{2,1,0:T(8,128)(2,1)} %broadcast_in_dim.27), calls=%async_computation.1 | async-start | bytes 4194304 | tf_op jit(solution)/shard_map/all_to_all | solution.py:30
  88.9 1.9 copy-start.1
  92.6 13.3 %all-to-all-start.2 = ((f32[16,8,256]{2,1,0:T(8,128)}), f32[16,8,256]{2,1,0:T(8,128)S(1)}, u32[]{:S(2)}, u32[]{:S(2)}) async-start(f32[16,8,256]{2,1,0:T(8,128)} %broadcast_in_dim.28), calls=%async_computation.2 | async-start | bytes 262144 | tf_op jit(solution)/shard_map/all_to_all | solution.py:30
  98.4 71.5 %reduce-scatter.3.cloned.1.call-start = ((), (), s32[]{:S(2)}) async-start(), calls=%async_computation.12 | async-start | bytes 2359296 | tf_op jit(solution)/shard_map/reduce_scatter | solution.py:298
  105.9 1.9 copy-start.2
  112.4 1.3 copy-start.3
  114.5 11.3 %all-to-all-start.3 = ((f32[16,32,128]{2,1,0:T(8,128)}), f32[16,32,128]{2,1,0:T(8,128)S(1)}, u32[]{:S(2)}, u32[]{:S(2)}) async-start(f32[16,32,128]{2,1,0:T(8,128)} %bitcast.8), calls=%async_computation.3 | async-start | bytes 524288 | tf_op jit(solution)/shard_map/all_to_all | solution.py:30
  118.0 94.8 %reduce-scatter.5.cloned.1.call-start = ((), (), s32[]{:S(2)}) async-start(), calls=%async_computation.13 | async-start | bytes 2359296 | tf_op jit(solution)/shard_map/reduce_scatter | solution.py:300
  170.6 16.1 %all-to-all-start.6 = ((f32[8,64,128]{2,1,0:T(8,128)}), f32[8,64,128]{2,1,0:T(8,128)S(1)}, u32[]{:S(2)}, u32[]{:S(2)}) async-start(f32[8,64,128]{2,1,0:T(8,128)} %broadcast_in_dim.33), calls=%async_computation.7 | async-start | bytes 524288 | tf_op jit(solution)/shard_map/all_to_all | solution.py:30
  175.3 6.9 %collective-permute-start.1 = (bf16[128,512]{1,0:T(8,128)(2,1)S(1)}, bf16[128,512]{1,0:T(8,128)(2,1)S(1)}, u32[]{:S(2)}, u32[]{:S(2)}) collective-permute-start(bf16[128,512]{1,0:T(8,128)(2,1)S(1)} %broadcast_select_fusion), channel_id=1, source_target_pairs={{0,8},{8,0},{1,9},{9,1},{2,10},{10,2},{3,11},{11,3},{4,12},{12,4},... | collective-permute-start | bytes 393224 | tf_op jit(solution)/shard_map/ppermute | solution.py:326
  183.3 49.8 %copy-start.6 = (bf16[128,512]{1,0:T(8,128)(2,1)}, bf16[128,512]{1,0:T(8,128)(2,1)S(1)}, u32[]{:S(2)}) copy-start(bf16[128,512]{1,0:T(8,128)(2,1)S(1)} %add_convert_fusion) | copy-start | bytes 393220
  187.7 14.9 %all-to-all-start.7 = ((f32[64,2,128]{2,1,0:T(2,128)}), f32[64,2,128]{2,1,0:T(2,128)S(1)}, u32[]{:S(2)}, u32[]{:S(2)}) async-start(f32[64,2,128]{2,1,0:T(2,128)} %bitcast.21), calls=%async_computation.8 | async-start | bytes 131072 | tf_op jit(solution)/shard_map/all_to_all | solution.py:30
  203.3 13.8 %all-to-all-start.8 = ((f32[64,2,128]{2,1,0:T(2,128)}), f32[64,2,128]{2,1,0:T(2,128)S(1)}, u32[]{:S(2)}, u32[]{:S(2)}) async-start(f32[64,2,128]{2,1,0:T(2,128)} %broadcast_in_dim.60), calls=%async_computation.9 | async-start | bytes 131072 | tf_op jit(solution)/shard_map/all_to_all | solution.py:30
  217.1 15.3 %all-to-all-start.9 = ((bf16[16,16,512]{2,1,0:T(8,128)(2,1)}), bf16[16,16,512]{2,1,0:T(8,128)(2,1)S(1)}, u32[]{:S(2)}, u32[]{:S(2)}) async-start(bf16[16,16,512]{2,1,0:T(8,128)(2,1)} %bitcast.92), calls=%async_computation.11 | async-start | bytes 524288 | tf_op jit(solution)/shard_map/all_to_all | solution.py:30
Sparse Core Ops, SparseCore 0:
  36.8 43.7 all-gather.2
  113.9 40.9 reduce-scatter.2
  157.7 42.0 reduce-scatter.4

commit v8 on v7

--- a/solution.py
+++ b/solution.py
@@ -310,9 +310,12 @@
     tiles = units // LANES
     padded = -(-tiles // 2) * 2 + (2 if tiles % 4 else 0)
     p_local = exact_dot(sketched, hidden, (((1,), (0,)), ((), ())))
-    flat = p_local.reshape(rank, tiles, LANES).transpose(1, 0, 2).reshape(tiles * rank, LANES)
     pad = padded * rank - tiles * rank
-    flat = jnp.concatenate([flat, jnp.zeros((pad, LANES), f32)], axis=0)
+    flat = jnp.concatenate(
+        [p_local[:, t * LANES:(t + 1) * LANES] for t in range(tiles)]
+        + [jnp.zeros((pad, LANES), f32)],
+        axis=0,
+    )
     p_flat = gathered(sum_scattered(flat))[:tiles * rank]
     p_sum = p_flat.reshape(tiles, rank, LANES).transpose(1, 0, 2).reshape(rank, units)
     gram_part = lax.dot_general(p_sum, p_sum, NT, precision=HIGHEST)
@@ -330,7 +333,9 @@
     gram = joined[rank:, :rank]
 
     q_local = exact_dot(proj, grad_queries, (((1,), (0,)), ((), ())))
-    q_flat = q_local.reshape(rank, width // LANES, LANES).transpose(1, 0, 2).reshape(-1, LANES)
+    q_flat = jnp.concatenate(
+        [q_local[:, t * LANES:(t + 1) * LANES] for t in range(width // LANES)], axis=0
+    )
     q_flat, gram = lax.optimization_barrier((q_flat, gram))
     q_part = sum_scattered(q_flat)
     q_sum = gathered(q_part)

time: 244 us -> 253 us (1.037)
  blocking collectives: 42.8 us -> 17.7 us
  starting transfers between devices: 53.5 us -> 68 us
  waiting for transfers between devices: 97.2 us -> 108 us
  local copies, waits for them, and re-layouts: 11.7 us -> 20.6 us
    all_to_all x2 -> x1, blocking collectives: 42.8 us -> 17.7 us  [swap(): return lax.all_to_all(blocks, axes, 0, 0, tiled=True)]
    all_to_all x8 -> x9, starting transfers between devices: 48.6 us -> 63.1 us  [swap(): return lax.all_to_all(blocks, axes, 0, 0, tiled=True)]
    all_to_all x8 -> x9, waiting for transfers between devices: 90.1 us -> 100 us  [swap(): return lax.all_to_all(blocks, axes, 0, 0, tiled=True)]
    unnamed x18 -> x32, local copies, waits for them, and re-layouts: 6.02 us -> 14.4 us
  transfers between devices with their start and end apart: 13 -> 14, of which waited for: 10 -> 11; matrix products, arithmetic and copies ran while one was open for 6% -> 9% of each run, Pallas kernels for 0% -> 0%
where the time goes in v8:
time: 253 us; the launch traced here: 249 us
  waiting for transfers between devices  108 us (43%)
  starting transfers between devices  68 us (27%)
  local copies, waits for them, and re-layouts  20.6 us (8%)
  blocking collectives  17.7 us (7%)
  between operations  14.1 us (6%)
  other arithmetic  10.5 us (4%)
  Pallas kernels  6.7 us (3%)
  matrix products  3 us (1%)
    all_to_all x9, waiting for transfers between devices, swap(): return lax.all_to_all(blocks, axes, 0, 0, tiled=True)  100 us
    all_to_all x9, starting transfers between devices, swap(): return lax.all_to_all(blocks, axes, 0, 0, tiled=True)  63.1 us
    all_to_all x1, blocking collectives, swap(): return lax.all_to_all(blocks, axes, 0, 0, tiled=True)  17.7 us
    unnamed x32, local copies, waits for them, and re-layouts  14.4 us
  transfers between devices with their start and end apart: 14, of which 11 were waited for; matrix products, arithmetic and copies ran while one was open for 9% of the time, Pallas kernels for 0%

profile of v8, /device:TPU:57, one launch (start us, length us, event | category | flops | bytes accessed | tf_op | source)
XLA Modules:
  0.0 248.6 jit_solution(14384941350034304252)
XLA Ops:
  10.3 12.6 %all-to-all-start = ((bf16[16,16,768]{2,1,0:T(8,128)(2,1)}), bf16[16,16,768]{2,1,0:T(8,128)(2,1)S(1)}, u32[]{:S(2)}, u32[]{:S(2)}) async-start(bf16[16,16,768]{2,1,0:T(8,128)(2,1)} %bitcast.2), calls=%async_computation | async-start | bytes 786432 | tf_op jit(solution)/shard_map/all_to_all | solution.py:30
  27.2 7.9 %all-to-all-done = bf16[16,16,768]{2,1,0:T(8,128)(2,1)S(1)} async-done(((bf16[16,16,768]{2,1,0:T(8,128)(2,1)}), bf16[16,16,768]{2,1,0:T(8,128)(2,1)S(1)}, u32[]{:S(2)}, u32[]{:S(2)}) %all-to-all-start) | async-done | bytes 393248 | tf_op jit(solution)/shard_map/all_to_all | solution.py:30
  36.7 5.0 %all-to-all-start.1 = ((bf16[16,128,512]{2,1,0:T(8,128)(2,1)}), bf16[16,128,512]{2,1,0:T(8,128)(2,1)S(1)}, u32[]{:S(2)}, u32[]{:S(2)}) async-start(bf16[16,128,512]{2,1,0:T(8,128)(2,1)} %broadcast_in_dim.29), calls=%async_computation.1 | async-start | bytes 4194304 | tf_op jit(solution)/shard_map/all_to_all | solution.py:30
  41.7 47.2 %all-to-all-done.1 = bf16[16,128,512]{2,1,0:T(8,128)(2,1)S(1)} async-done(((bf16[16,128,512]{2,1,0:T(8,128)(2,1)}), bf16[16,128,512]{2,1,0:T(8,128)(2,1)S(1)}, u32[]{:S(2)}, u32[]{:S(2)}) %all-to-all-start.1) | async-done | bytes 2097184 | tf_op jit(solution)/shard_map/all_to_all | solution.py:30
  92.6 5.8 %all-to-all-start.2 = ((f32[16,8,256]{2,1,0:T(8,128)}), f32[16,8,256]{2,1,0:T(8,128)S(1)}, u32[]{:S(2)}, u32[]{:S(2)}) async-start(f32[16,8,256]{2,1,0:T(8,128)} %broadcast_in_dim.30), calls=%async_computation.2 | async-start | bytes 262144 | tf_op jit(solution)/shard_map/all_to_all | solution.py:30
  98.4 7.5 %all-to-all-done.2.all_ref = f32[16,8,256]{2,1,0:T(8,128)S(1)} async-done(((f32[16,8,256]{2,1,0:T(8,128)}), f32[16,8,256]{2,1,0:T(8,128)S(1)}, u32[]{:S(2)}, u32[]{:S(2)}) %all-to-all-start.2) | async-done | bytes 131104 | tf_op jit(solution)/shard_map/all_to_all | solution.py:30
  107.8 4.6 %grads.1 = (bf16[8,256,512]{2,1,0:T(8,128)(2,1)S(1)}, bf16[8,16,16,512]{3,2,1,0:T(8,128)(2,1)}, f32[32,256]{1,0:T(8,128)S(1)}) custom-call(bf16[2,8,128,512]{3,2,1,0:T(8,128)(2,1)S(1)} %bitcast.67, bf16[8,16,16,768]{3,2,1,0:T(8,128)(2,1)S(1)} %bitcast.69, f32[16,8,256]{2,1,0:T(8,128)S(1)} %all-to-all-done.2.all_ref, s32[1,256]{1,0:T(1,128)S(1)} %and_select_fusion.3.pos_ref), custom_call_target="tpu_custom_call" | custom-call | tf_op jit(solution)/shard_map/grads/pallas_call | solution.py:282
  114.5 3.5 %all-to-all-start.3 = ((f32[16,32,128]{2,1,0:T(8,128)}), f32[16,32,128]{2,1,0:T(8,128)S(1)}, u32[]{:S(2)}, u32[]{:S(2)}) async-start(f32[16,32,128]{2,1,0:T(8,128)} %bitcast.8), calls=%async_computation.3 | async-start | bytes 524288 | tf_op jit(solution)/shard_map/all_to_all | solution.py:30
  118.8 7.0 %all-to-all-done.3 = f32[16,32,128]{2,1,0:T(8,128)S(1)} async-done(((f32[16,32,128]{2,1,0:T(8,128)}), f32[16,32,128]{2,1,0:T(8,128)S(1)}, u32[]{:S(2)}, u32[]{:S(2)}) %all-to-all-start.3) | async-done | bytes 262176 | tf_op jit(solution)/shard_map/all_to_all | solution.py:30
  135.1 14.4 %all-to-all-start.4 = ((f32[64,8,128]{2,1,0:T(8,128)}), f32[64,8,128]{2,1,0:T(8,128)S(1)}, u32[]{:S(2)}, u32[]{:S(2)}) async-start(f32[64,8,128]{2,1,0:T(8,128)} %bitcast.10), calls=%async_computation.4 | async-start | bytes 524288 | tf_op jit(solution)/shard_map/all_to_all | solution.py:30
  150.3 10.2 %all-to-all-done.4 = f32[64,8,128]{2,1,0:T(8,128)S(1)} async-done(((f32[64,8,128]{2,1,0:T(8,128)}), f32[64,8,128]{2,1,0:T(8,128)S(1)}, u32[]{:S(2)}, u32[]{:S(2)}) %all-to-all-start.4) | async-done | bytes 262176 | tf_op jit(solution)/shard_map/all_to_all | solution.py:30
  160.5 17.7 %all_to_all.50 = f32[64,8,128]{2,1,0:T(8,128)S(1)} all-to-all(f32[64,8,128]{2,1,0:T(8,128)S(1)} %broadcast_in_dim.60), channel_id=1, replica_groups=mesh['rep'=2,'y'=8,'xh'=2,'xl'=2,'z'=8] {'rep','y','xh','xl'}, dimensions={0} | all-to-all | bytes 524288 | tf_op jit(solution)/shard_map/all_to_all | solution.py:30
  179.7 3.7 %all-to-all-start.6 = ((f32[8,64,128]{2,1,0:T(8,128)}), f32[8,64,128]{2,1,0:T(8,128)S(1)}, u32[]{:S(2)}, u32[]{:S(2)}) async-start(f32[8,64,128]{2,1,0:T(8,128)} %broadcast_in_dim.62), calls=%async_computation.7 | async-start | bytes 524288 | tf_op jit(solution)/shard_map/all_to_all | solution.py:30
  184.4 2.6 %collective-permute-start.1 = (bf16[128,512]{1,0:T(8,128)(2,1)S(1)}, bf16[128,512]{1,0:T(8,128)(2,1)S(1)}, u32[]{:S(2)}, u32[]{:S(2)}) collective-permute-start(bf16[128,512]{1,0:T(8,128)(2,1)S(1)} %broadcast_select_fusion), channel_id=1, source_target_pairs={{0,8},{8,0},{1,9},{9,1},{2,10},{10,2},{3,11},{11,3},{4,12},{12,4},... | collective-permute-start | bytes 393224 | tf_op jit(solution)/shard_map/ppermute | solution.py:329
  187.0 4.2 %collective-permute-done.1 = bf16[128,512]{1,0:T(8,128)(2,1)S(1)} collective-permute-done((bf16[128,512]{1,0:T(8,128)(2,1)S(1)}, bf16[128,512]{1,0:T(8,128)(2,1)S(1)}, u32[]{:S(2)}, u32[]{:S(2)}) %collective-permute-start.1) | collective-permute-done | bytes 131104 | tf_op jit(solution)/shard_map/ppermute | solution.py:329
  192.2 3.5 %all-to-all-done.6 = f32[8,64,128]{2,1,0:T(8,128)S(1)} async-done(((f32[8,64,128]{2,1,0:T(8,128)}), f32[8,64,128]{2,1,0:T(8,128)S(1)}, u32[]{:S(2)}, u32[]{:S(2)}) %all-to-all-start.6) | async-done | bytes 262176 | tf_op jit(solution)/shard_map/all_to_all | solution.py:30
  196.7 6.9 %all-to-all-start.7 = ((f32[64,2,128]{2,1,0:T(2,128)}), f32[64,2,128]{2,1,0:T(2,128)S(1)}, u32[]{:S(2)}, u32[]{:S(2)}) async-start(f32[64,2,128]{2,1,0:T(2,128)} %bitcast.17), calls=%async_computation.8 | async-start | bytes 131072 | tf_op jit(solution)/shard_map/all_to_all | solution.py:30
  203.6 2.9 %cholesky.17 = f32[32,32]{1,0:T(8,128)S(1)} custom-call(f32[32,32]{1,0:T(8,128)S(1)} %fusion.40), custom_call_target="Cholesky" | custom-call | tf_op jit(solution)/shard_map/jit(cholesky)/cholesky | solution.py:347
  207.2 4.2 %all-to-all-done.7 = f32[64,2,128]{2,1,0:T(2,128)S(1)} async-done(((f32[64,2,128]{2,1,0:T(2,128)}), f32[64,2,128]{2,1,0:T(2,128)S(1)}, u32[]{:S(2)}, u32[]{:S(2)}) %all-to-all-start.7) | async-done | bytes 65568 | tf_op jit(solution)/shard_map/all_to_all | solution.py:30
  212.2 6.5 %all-to-all-start.8 = ((f32[64,2,128]{2,1,0:T(2,128)}), f32[64,2,128]{2,1,0:T(2,128)S(1)}, u32[]{:S(2)}, u32[]{:S(2)}) async-start(f32[64,2,128]{2,1,0:T(2,128)} %broadcast_in_dim.63), calls=%async_computation.9 | async-start | bytes 131072 | tf_op jit(solution)/shard_map/all_to_all | solution.py:30
  219.3 2.4 custom-call.6
  221.8 4.3 %all-to-all-done.8 = f32[64,2,128]{2,1,0:T(2,128)S(1)} async-done(((f32[64,2,128]{2,1,0:T(2,128)}), f32[64,2,128]{2,1,0:T(2,128)S(1)}, u32[]{:S(2)}, u32[]{:S(2)}) %all-to-all-start.8) | async-done | bytes 65568 | tf_op jit(solution)/shard_map/all_to_all | solution.py:30
  226.0 4.7 %all-to-all-start.9 = ((bf16[16,16,512]{2,1,0:T(8,128)(2,1)}), bf16[16,16,512]{2,1,0:T(8,128)(2,1)S(1)}, u32[]{:S(2)}, u32[]{:S(2)}) async-start(bf16[16,16,512]{2,1,0:T(8,128)(2,1)} %bitcast.79), calls=%async_computation.11 | async-start | bytes 524288 | tf_op jit(solution)/shard_map/all_to_all | solution.py:30
  232.8 8.6 %all-to-all-done.9 = bf16[16,16,512]{2,1,0:T(8,128)(2,1)S(1)} async-done(((bf16[16,16,512]{2,1,0:T(8,128)(2,1)}), bf16[16,16,512]{2,1,0:T(8,128)(2,1)S(1)}, u32[]{:S(2)}, u32[]{:S(2)}) %all-to-all-start.9) | async-done | bytes 262176 | tf_op jit(solution)/shard_map/all_to_all | solution.py:30
  (94 shorter events, 36.7 us)
Async XLA Ops:
  7.2 118.6 %copy-start = (bf16[1,128,1792]{2,1,0:T(8,128)(2,1)S(1)}, bf16[1,128,1792]{2,1,0:T(8,128)(2,1)}, u32[]{:S(2)}) copy-start(bf16[1,128,1792]{2,1,0:T(8,128)(2,1)} %param.8) | copy-start | bytes 1376260
  7.2 15.7 %copy-start.8 = (s32[1,128]{1,0:T(1,128)S(1)}, s32[1,128]{1,0:T(1,128)}, u32[]{:S(2)}) copy-start(s32[1,128]{1,0:T(1,128)} %param.7) | copy-start | bytes 1540
  7.2 27.9 %copy-start.7 = (bf16[1,128,512]{2,1,0:T(8,128)(2,1)S(1)}, bf16[1,128,512]{2,1,0:T(8,128)(2,1)}, u32[]{:S(2)}) copy-start(bf16[1,128,512]{2,1,0:T(8,128)(2,1)} %param.5) | copy-start | bytes 393220
  8.3 0.9 copy-start.4
  10.3 24.8 %all-to-all-start = ((bf16[16,16,768]{2,1,0:T(8,128)(2,1)}), bf16[16,16,768]{2,1,0:T(8,128)(2,1)S(1)}, u32[]{:S(2)}, u32[]{:S(2)}) async-start(bf16[16,16,768]{2,1,0:T(8,128)(2,1)} %bitcast.2), calls=%async_computation | async-start | bytes 786432 | tf_op jit(solution)/shard_map/all_to_all | solution.py:30
  22.9 66.0 %all-gather.3.cloned.1.call-start = ((), (), s32[]{:S(2)}) async-start(), calls=%async_computation.14 | async-start | bytes 3538944 | tf_op jit(solution)/shard_map/all_gather | solution.py:256
  22.9 4.3 %collective-permute-start = (s32[1,128]{1,0:T(1,128)S(1)}, s32[1,128]{1,0:T(1,128)S(1)}, u32[]{:S(2)}, u32[]{:S(2)}) collective-permute-start(s32[1,128]{1,0:T(1,128)S(1)} %copy-done.8), channel_id=1, source_target_pairs={{0,8},{8,0},{1,9},{9,1},{2,10},{10,2},{3,11},{11,3},{4,12},{12,4},... | collective-permute-start | bytes 1544 | tf_op jit(solution)/shard_map/ppermute | solution.py:253
  35.1 1.6 copy-start.5
  36.7 52.2 %all-to-all-start.1 = ((bf16[16,128,512]{2,1,0:T(8,128)(2,1)}), bf16[16,128,512]{2,1,0:T(8,128)(2,1)S(1)}, u32[]{:S(2)}, u32[]{:S(2)}) async-start(bf16[16,128,512]{2,1,0:T(8,128)(2,1)} %broadcast_in_dim.29), calls=%async_computation.1 | async-start | bytes 4194304 | tf_op jit(solution)/shard_map/all_to_all | solution.py:30
  88.9 1.9 copy-start.1
  92.6 13.3 %all-to-all-start.2 = ((f32[16,8,256]{2,1,0:T(8,128)}), f32[16,8,256]{2,1,0:T(8,128)S(1)}, u32[]{:S(2)}, u32[]{:S(2)}) async-start(f32[16,8,256]{2,1,0:T(8,128)} %broadcast_in_dim.30), calls=%async_computation.2 | async-start | bytes 262144 | tf_op jit(solution)/shard_map/all_to_all | solution.py:30
  105.9 1.9 copy-start.2
  112.4 1.3 copy-start.3
  114.5 11.3 %all-to-all-start.3 = ((f32[16,32,128]{2,1,0:T(8,128)}), f32[16,32,128]{2,1,0:T(8,128)S(1)}, u32[]{:S(2)}, u32[]{:S(2)}) async-start(f32[16,32,128]{2,1,0:T(8,128)} %bitcast.8), calls=%async_computation.3 | async-start | bytes 524288 | tf_op jit(solution)/shard_map/all_to_all | solution.py:30
  118.0 60.9 %reduce-scatter.3.cloned.1.call-start = ((), (), s32[]{:S(2)}) async-start(), calls=%async_computation.12 | async-start | bytes 2359296 | tf_op jit(solution)/shard_map/reduce_scatter | solution.py:298
  135.1 25.3 %all-to-all-start.4 = ((f32[64,8,128]{2,1,0:T(8,128)}), f32[64,8,128]{2,1,0:T(8,128)S(1)}, u32[]{:S(2)}, u32[]{:S(2)}) async-start(f32[64,8,128]{2,1,0:T(8,128)} %bitcast.10), calls=%async_computation.4 | async-start | bytes 524288 | tf_op jit(solution)/shard_map/all_to_all | solution.py:30
  149.5 72.2 %reduce-scatter.5.cloned.1.call-start = ((), (), s32[]{:S(2)}) async-start(), calls=%async_computation.13 | async-start | bytes 2359296 | tf_op jit(solution)/shard_map/reduce_scatter | solution.py:300
  179.7 16.1 %all-to-all-start.6 = ((f32[8,64,128]{2,1,0:T(8,128)}), f32[8,64,128]{2,1,0:T(8,128)S(1)}, u32[]{:S(2)}, u32[]{:S(2)}) async-start(f32[8,64,128]{2,1,0:T(8,128)} %broadcast_in_dim.62), calls=%async_computation.7 | async-start | bytes 524288 | tf_op jit(solution)/shard_map/all_to_all | solution.py:30
  184.4 6.8 %collective-permute-start.1 = (bf16[128,512]{1,0:T(8,128)(2,1)S(1)}, bf16[128,512]{1,0:T(8,128)(2,1)S(1)}, u32[]{:S(2)}, u32[]{:S(2)}) collective-permute-start(bf16[128,512]{1,0:T(8,128)(2,1)S(1)} %broadcast_select_fusion), channel_id=1, source_target_pairs={{0,8},{8,0},{1,9},{9,1},{2,10},{10,2},{3,11},{11,3},{4,12},{12,4},... | collective-permute-start | bytes 393224 | tf_op jit(solution)/shard_map/ppermute | solution.py:329
  192.2 49.9 %copy-start.6 = (bf16[128,512]{1,0:T(8,128)(2,1)}, bf16[128,512]{1,0:T(8,128)(2,1)S(1)}, u32[]{:S(2)}) copy-start(bf16[128,512]{1,0:T(8,128)(2,1)S(1)} %add_convert_fusion) | copy-start | bytes 393220
  196.7 14.8 %all-to-all-start.7 = ((f32[64,2,128]{2,1,0:T(2,128)}), f32[64,2,128]{2,1,0:T(2,128)S(1)}, u32[]{:S(2)}, u32[]{:S(2)}) async-start(f32[64,2,128]{2,1,0:T(2,128)} %bitcast.17), calls=%async_computation.8 | async-start | bytes 131072 | tf_op jit(solution)/shard_map/all_to_all | solution.py:30
  212.2 13.8 %all-to-all-start.8 = ((f32[64,2,128]{2,1,0:T(2,128)}), f32[64,2,128]{2,1,0:T(2,128)S(1)}, u32[]{:S(2)}, u32[]{:S(2)}) async-start(f32[64,2,128]{2,1,0:T(2,128)} %broadcast_in_dim.63), calls=%async_computation.9 | async-start | bytes 131072 | tf_op jit(solution)/shard_map/all_to_all | solution.py:30
  226.0 15.3 %all-to-all-start.9 = ((bf16[16,16,512]{2,1,0:T(8,128)(2,1)}), bf16[16,16,512]{2,1,0:T(8,128)(2,1)S(1)}, u32[]{:S(2)}, u32[]{:S(2)}) async-start(bf16[16,16,512]{2,1,0:T(8,128)(2,1)} %bitcast.79), calls=%async_computation.11 | async-start | bytes 524288 | tf_op jit(solution)/shard_map/all_to_all | solution.py:30
Sparse Core Ops, SparseCore 0:
  36.8 43.7 all-gather.2
  121.7 44.7 reduce-scatter.2
  169.3 41.3 reduce-scatter.4
